TPU v7x, 32 devices: a whole 2x2x4 slice. The times are simulated.
32 devices in a mesh: replica: 2 (over y), group: 16 (over z, x, core).
Axes of the slice: x: 2, y: 2, z: 4, core: 2. Of those that a mesh axis runs over, the one named last changes fastest.
Arguments:
- hidden_in: bfloat16 [4, 1024, 1536], P('replica', 'group'), may hold values from -6 to 6
- lengths: int32 [4], P('replica'), may hold values from 256 to 1024, as said below
- gain_attn: bfloat16 [1536], P('group'), may hold values from 0.5 to 1.5
- w_query: bfloat16 [1536, 1536], P('group'), may hold values from -0.15625 to 0.15625
- b_query: bfloat16 [1536], P('group'), may hold values from -3 to 3
- w_key: bfloat16 [1536, 256], P('group'), may hold values from -0.3125 to 0.3125
- b_key: bfloat16 [256], P('group'), may hold values from -3 to 3
- w_value: bfloat16 [1536, 256], P('group'), may hold values from -0.15625 to 0.15625
- b_value: bfloat16 [256], P('group'), may hold values from -3 to 3
- w_out: bfloat16 [1536, 1536], P('group'), may hold values from -1.75 to 1.75
- gain_mlp: bfloat16 [1536], P('group'), may hold values from 0.25 to 2.5
- w_gate: bfloat16 [1536, 8960], P('group'), may hold values from -0.15625 to 0.15625
- w_up: bfloat16 [1536, 8960], P('group'), may hold values from -0.15625 to 0.15625
- w_down: bfloat16 [1536, 8960], P('group'), may hold values from -0.125 to 0.125
- cotangent: bfloat16 [4, 1024, 1536], P('replica', 'group'), may hold values from -6 to 6
Outputs:
- layer_out: bfloat16 [4, 1024, 1536], P('replica', 'group')
- grad_input: float32 [4, 1024, 1536], P('replica', 'group')
- grad_gain_attn: float32 [1536], P('group')
- grad_w_query: float32 [1536, 1536], P('group')
- grad_b_query: float32 [1536], P('group')
- grad_w_key: float32 [1536, 256], P('group')
- grad_b_key: float32 [256], P('group')
- grad_w_value: float32 [1536, 256], P('group')
- grad_b_value: float32 [256], P('group')
- grad_w_out: float32 [1536, 1536], P('group')
- grad_gain_mlp: float32 [1536], P('group')
- grad_w_gate: float32 [1536, 8960], P('group')
- grad_w_up: float32 [1536, 8960], P('group')
- grad_w_down: float32 [1536, 8960], P('group')
Inputs may be any that keep to these rules, and one draw needn't show every extreme that they name: Slot s holds valid tokens at its first lengths[s] positions; in every draw one slot has 1024 and another 1024 // 4.
All inputs are finite; a program needn't handle non-finite values.
Results may differ from a plain program's by a relative error of at most 0.034.
Values may be sent and summed in bfloat16 or wider, within the bound.
A program may use at most 512 MiB of HBM per device.

v0:
```python
import jax
import jax.numpy as jnp
from jax import lax
from jax.sharding import PartitionSpec as P

HEADS = 12
KV_HEADS = 2
HEAD_DIM = 128


EPSILON = 1e-06
THETA = 1000000.0


def rope_tables(positions, head_dim):
    freqs = THETA ** (-jnp.arange(0, head_dim, 2).astype(jnp.float32) / head_dim)
    angles = positions.astype(jnp.float32)[:, None] * freqs[None, :]
    angles = jnp.concatenate((angles, angles), axis=-1)
    return (jnp.cos(angles), jnp.sin(angles))


def rotate(tensor, cos_table, sin_table):
    halfway = tensor.shape[-1] // 2
    turned = jnp.concatenate((-tensor[..., halfway:], tensor[..., :halfway]), axis=-1)
    return tensor * cos_table + turned * sin_table


def rotate_back(gradient, cos_table, sin_table):
    halfway = gradient.shape[-1] // 2
    scaled = gradient * sin_table
    turned = jnp.concatenate((scaled[..., halfway:], -scaled[..., :halfway]), axis=-1)
    return gradient * cos_table + turned


def normalize(row_values, gain_vec):
    factor = lax.rsqrt(jnp.mean(row_values * row_values, axis=-1, keepdims=True) + EPSILON)
    return (row_values * factor * gain_vec, factor)


def norm_back(row_values, factor, gain_vec, upstream):
    weighted = upstream * gain_vec
    inner_mean = jnp.mean(weighted * row_values, axis=-1, keepdims=True)
    grad_rows = factor * weighted - row_values * (factor * factor * factor) * inner_mean
    grad_gain = jnp.sum(upstream * row_values * factor, axis=0)
    return (grad_rows, grad_gain)


def matmul(first_mat, second_mat):
    return jnp.dot(first_mat, second_mat, preferred_element_type=jnp.float32)


def matmul_nt(first_mat, second_mat):
    return lax.dot_general(
        first_mat, second_mat, (((1,), (1,)), ((), ())), preferred_element_type=jnp.float32
    )


def matmul_tn(first_mat, second_mat):
    return lax.dot_general(
        first_mat, second_mat, (((0,), (0,)), ((), ())), preferred_element_type=jnp.float32
    )


def arrange(per_token, kv_heads):
    block_len, head_count, head_dim = per_token.shape
    repeat = head_count // kv_heads
    grouped = per_token.reshape(block_len, kv_heads, repeat, head_dim)
    return jnp.transpose(grouped, (1, 2, 0, 3)).reshape(kv_heads, repeat * block_len, head_dim)


def restore(per_group, block_len):
    kv_heads, row_count, head_dim = per_group.shape
    repeat = row_count // block_len
    grouped = per_group.reshape(kv_heads, repeat, block_len, head_dim)
    return jnp.transpose(grouped, (2, 0, 1, 3)).reshape(block_len, kv_heads * repeat * head_dim)


def masked_exp(query_rows, key_block, row_pos, first_key, length, score_scale):
    key_step = key_block.shape[0]
    raw_scores = jnp.einsum(
        "grd,kgd->grk", query_rows, key_block, preferred_element_type=jnp.float32
    )
    key_pos = first_key + jnp.arange(key_step, dtype=jnp.int32)
    allowed = (key_pos[None, :] <= row_pos[:, None]) & (key_pos[None, :] < length)
    return jnp.where(allowed[None], jnp.exp(raw_scores * score_scale), 0.0)


def block_total(length, rank_end, key_step):
    key_limit = jnp.minimum(length, rank_end)
    return (key_limit + key_step - 1) // key_step


def attend_forward(
    query_rows, key_all, value_all, row_pos, length, rank_end, key_step, score_scale
):
    kv_heads, row_count, head_dim = query_rows.shape

    def visit(block_index, state_tuple):
        totals, numerator = state_tuple
        first_key = block_index * key_step
        key_block = lax.dynamic_slice_in_dim(key_all, first_key, key_step, 0)
        value_block = lax.dynamic_slice_in_dim(value_all, first_key, key_step, 0)
        weights = masked_exp(query_rows, key_block, row_pos, first_key, length, score_scale)
        totals = totals + jnp.sum(weights, axis=-1)
        numerator = numerator + jnp.einsum(
            "grk,kgd->grd",
            weights.astype(jnp.bfloat16),
            value_block,
            preferred_element_type=jnp.float32,
        )
        return (totals, numerator)

    initial = (
        jnp.zeros((kv_heads, row_count), jnp.float32),
        jnp.zeros((kv_heads, row_count, head_dim), jnp.float32),
    )
    return lax.fori_loop(0, block_total(length, rank_end, key_step), visit, initial)


def attend_backward(
    query_rows,
    key_all,
    value_all,
    row_pos,
    length,
    rank_end,
    key_step,
    score_scale,
    grad_numer,
    grad_total,
):
    kv_heads, row_count, head_dim = query_rows.shape

    def visit(block_index, state_tuple):
        grad_query, grad_key, grad_value = state_tuple
        first_key = block_index * key_step
        key_block = lax.dynamic_slice_in_dim(key_all, first_key, key_step, 0)
        value_block = lax.dynamic_slice_in_dim(value_all, first_key, key_step, 0)
        weights = masked_exp(query_rows, key_block, row_pos, first_key, length, score_scale)
        grad_prob = jnp.einsum(
            "grd,kgd->grk", grad_numer, value_block, preferred_element_type=jnp.float32
        )
        grad_score = (weights * (grad_prob + grad_total[..., None])).astype(jnp.bfloat16)
        grad_query = grad_query + jnp.einsum(
            "grk,kgd->grd", grad_score, key_block, preferred_element_type=jnp.float32
        )
        key_part = jnp.einsum(
            "grk,grd->kgd", grad_score, query_rows, preferred_element_type=jnp.float32
        )
        value_part = jnp.einsum(
            "grk,grd->kgd",
            weights.astype(jnp.bfloat16),
            grad_numer,
            preferred_element_type=jnp.float32,
        )
        key_old = lax.dynamic_slice_in_dim(grad_key, first_key, key_step, 0)
        value_old = lax.dynamic_slice_in_dim(grad_value, first_key, key_step, 0)
        grad_key = lax.dynamic_update_slice_in_dim(grad_key, key_old + key_part, first_key, 0)
        grad_value = lax.dynamic_update_slice_in_dim(
            grad_value, value_old + value_part, first_key, 0
        )
        return (grad_query, grad_key, grad_value)

    initial = (
        jnp.zeros((kv_heads, row_count, head_dim), jnp.float32),
        jnp.zeros(key_all.shape, jnp.float32),
        jnp.zeros(value_all.shape, jnp.float32),
    )
    return lax.fori_loop(0, block_total(length, rank_end, key_step), visit, initial)


def shards(
    hidden_in,
    lengths,
    gain_attn,
    w_query,
    b_query,
    w_key,
    b_key,
    w_value,
    b_value,
    w_out,
    gain_mlp,
    w_gate,
    w_up,
    w_down,
    cotangent,
):
    group_count = lax.axis_size("group")
    group_rank = lax.axis_index("group")
    slot_count, block_len, model_width = hidden_in.shape
    kv_heads = KV_HEADS
    head_dim = HEAD_DIM
    repeat = HEADS // kv_heads
    slot_span = block_len * group_count
    key_step = min(512, slot_span)
    score_scale = head_dim ** (-0.5)
    tokens = slot_count * block_len
    hidden_units = w_gate.shape[1]
    positions = group_rank * block_len + jnp.arange(block_len, dtype=jnp.int32)
    valid_rows = (positions[None, :] < lengths[:, None]).astype(jnp.float32).reshape(tokens, 1)
    cos_table, sin_table = rope_tables(positions, head_dim)
    cos_heads = cos_table[:, None, :]
    sin_heads = sin_table[:, None, :]
    rank_end = (group_rank + 1) * block_len
    row_pos = jnp.tile(positions, repeat)
    attn_set = (
        lax.all_gather(gain_attn, "group", axis=0, tiled=True),
        lax.all_gather(w_query, "group", axis=0, tiled=True),
        lax.all_gather(b_query, "group", axis=0, tiled=True),
        lax.all_gather(w_key, "group", axis=0, tiled=True),
        lax.all_gather(b_key, "group", axis=0, tiled=True),
        lax.all_gather(w_value, "group", axis=0, tiled=True),
        lax.all_gather(b_value, "group", axis=0, tiled=True),
        lax.all_gather(w_out, "group", axis=0, tiled=True),
    )
    gain_one, query_w, query_b, key_w, key_b, value_w, value_b, out_w = attn_set
    inputs = hidden_in.reshape(tokens, model_width).astype(jnp.float32)
    normed_full, factor_one = normalize(inputs, gain_one.astype(jnp.float32))
    normed = normed_full.astype(jnp.bfloat16)
    query_pre = matmul(normed, query_w) + query_b.astype(jnp.float32)
    key_pre = matmul(normed, key_w) + key_b.astype(jnp.float32)
    value_pre = matmul(normed, value_w) + value_b.astype(jnp.float32)
    query_rot = rotate(
        query_pre.reshape(slot_count, block_len, HEADS, head_dim), cos_heads, sin_heads
    ).astype(jnp.bfloat16)
    key_rot = rotate(
        key_pre.reshape(slot_count, block_len, kv_heads, head_dim), cos_heads, sin_heads
    ).astype(jnp.bfloat16)
    value_low = value_pre.astype(jnp.bfloat16).reshape(slot_count, block_len, kv_heads, head_dim)
    pair_fwd = (
        lax.all_gather(key_rot, "group", axis=1, tiled=True),
        lax.all_gather(value_low, "group", axis=1, tiled=True),
    )
    key_all, value_all = pair_fwd
    query_groups = []
    slot_totals = []
    slot_attended = []
    attended_rows = []
    for slot_index in range(slot_count):
        query_rows = arrange(query_rot[slot_index], kv_heads)
        totals, numerator = attend_forward(
            query_rows,
            key_all[slot_index],
            value_all[slot_index],
            row_pos,
            lengths[slot_index],
            rank_end,
            key_step,
            score_scale,
        )
        attended = numerator / totals[..., None]
        query_groups.append(query_rows)
        slot_totals.append(totals)
        slot_attended.append(attended)
        attended_rows.append(restore(attended, block_len))
    attended_low = jnp.concatenate(attended_rows, axis=0).astype(jnp.bfloat16)
    mlp_set = (
        lax.all_gather(gain_mlp, "group", axis=0, tiled=True),
        lax.all_gather(w_gate, "group", axis=0, tiled=True),
        lax.all_gather(w_up, "group", axis=0, tiled=True),
        lax.all_gather(w_down, "group", axis=0, tiled=True),
    )
    gain_two, gate_w, up_w, down_w = mlp_set
    residual_mid = inputs + matmul(attended_low, out_w)
    normed_two_full, factor_two = normalize(residual_mid, gain_two.astype(jnp.float32))
    normed_two = normed_two_full.astype(jnp.bfloat16)
    gate_pre = matmul(normed_two, gate_w)
    up_pre = matmul(normed_two, up_w)
    sigmoid_gate = jax.nn.sigmoid(gate_pre)
    silu_gate = gate_pre * sigmoid_gate
    hidden = (silu_gate * up_pre).astype(jnp.bfloat16)
    final_rows = residual_mid + matmul_nt(hidden, down_w)
    layer_out = (
        (final_rows * valid_rows).reshape(slot_count, block_len, model_width).astype(jnp.bfloat16)
    )
    mlp_back = (
        lax.all_gather(gain_mlp, "group", axis=0, tiled=True),
        lax.all_gather(w_gate, "group", axis=0, tiled=True),
        lax.all_gather(w_up, "group", axis=0, tiled=True),
        lax.all_gather(w_down, "group", axis=0, tiled=True),
    )
    attn_back = (
        lax.all_gather(gain_attn, "group", axis=0, tiled=True),
        lax.all_gather(w_query, "group", axis=0, tiled=True),
        lax.all_gather(b_query, "group", axis=0, tiled=True),
        lax.all_gather(w_key, "group", axis=0, tiled=True),
        lax.all_gather(b_key, "group", axis=0, tiled=True),
        lax.all_gather(w_value, "group", axis=0, tiled=True),
        lax.all_gather(b_value, "group", axis=0, tiled=True),
        lax.all_gather(w_out, "group", axis=0, tiled=True),
    )
    pair_back = (
        lax.all_gather(key_rot, "group", axis=1, tiled=True),
        lax.all_gather(value_low, "group", axis=1, tiled=True),
    )
    gain_two_back, gate_back, up_back, down_back = mlp_back
    (
        gain_one_back,
        query_back,
        query_bias_back,
        key_back,
        key_bias_back,
        value_back,
        value_bias_back,
        out_back,
    ) = attn_back
    key_all_back, value_all_back = pair_back
    grad_final = cotangent.reshape(tokens, model_width).astype(jnp.float32) * valid_rows
    grad_down_in = grad_final.astype(jnp.bfloat16)
    grad_hidden = matmul(grad_down_in, down_back)
    grad_gate = (
        grad_hidden * up_pre * (sigmoid_gate * (1.0 + gate_pre * (1.0 - sigmoid_gate)))
    ).astype(jnp.bfloat16)
    grad_up = (grad_hidden * silu_gate).astype(jnp.bfloat16)
    grad_normed_two = matmul_nt(grad_gate, gate_back) + matmul_nt(grad_up, up_back)
    gate_up_grad = jnp.concatenate((grad_gate, grad_up), axis=1)
    down_share = lax.psum_scatter(
        matmul_tn(grad_down_in, hidden), "group", scatter_dimension=0, tiled=True
    )
    gate_up_share = lax.psum_scatter(
        matmul_tn(normed_two, gate_up_grad), "group", scatter_dimension=0, tiled=True
    )
    down_sum, gate_up_sum = (
        lax.psum(down_share.astype(jnp.bfloat16), "replica").astype(jnp.float32),
        lax.psum(gate_up_share.astype(jnp.bfloat16), "replica").astype(jnp.float32),
    )
    grad_mid_norm, grad_gain_two = norm_back(
        residual_mid, factor_two, gain_two_back.astype(jnp.float32), grad_normed_two
    )
    grad_mid = grad_final + grad_mid_norm
    grad_branch = grad_mid.astype(jnp.bfloat16)
    out_term = matmul_tn(attended_low, grad_branch)
    grad_attended = matmul_nt(grad_branch, out_back)
    grad_query_rows = []
    grad_key_slots = []
    grad_value_slots = []
    for slot_index in range(slot_count):
        slot_grad = grad_attended[slot_index * block_len : (slot_index + 1) * block_len].reshape(
            block_len, HEADS, head_dim
        )
        grad_out = arrange(slot_grad, kv_heads)
        totals = slot_totals[slot_index]
        grad_total = -jnp.sum(grad_out * slot_attended[slot_index], axis=-1) / totals
        grad_numer = (grad_out / totals[..., None]).astype(jnp.bfloat16)
        grad_query, grad_key, grad_value = attend_backward(
            query_groups[slot_index],
            key_all_back[slot_index],
            value_all_back[slot_index],
            row_pos,
            lengths[slot_index],
            rank_end,
            key_step,
            score_scale,
            grad_numer,
            grad_total,
        )
        query_back_rows = restore(grad_query * score_scale, block_len).reshape(
            block_len, HEADS, head_dim
        )
        grad_query_rows.append(
            rotate_back(query_back_rows, cos_heads, sin_heads).reshape(block_len, HEADS * head_dim)
        )
        grad_key_slots.append(grad_key)
        grad_value_slots.append(grad_value)
    key_sum, value_sum = (
        lax.psum_scatter(jnp.stack(grad_key_slots), "group", scatter_dimension=1, tiled=True),
        lax.psum_scatter(jnp.stack(grad_value_slots), "group", scatter_dimension=1, tiled=True),
    )
    grad_query_pre = jnp.concatenate(grad_query_rows, axis=0).astype(jnp.bfloat16)
    grad_key_pre = (
        rotate_back(key_sum * score_scale, cos_heads, sin_heads)
        .astype(jnp.bfloat16)
        .reshape(tokens, kv_heads * head_dim)
    )
    grad_value_pre = value_sum.astype(jnp.bfloat16).reshape(tokens, kv_heads * head_dim)
    grad_normed = (
        matmul_nt(grad_query_pre, query_back)
        + matmul_nt(grad_key_pre, key_back)
        + matmul_nt(grad_value_pre, value_back)
    )
    grad_in_norm, grad_gain_one = norm_back(
        inputs, factor_one, gain_one_back.astype(jnp.float32), grad_normed
    )
    grad_input = (grad_mid + grad_in_norm).reshape(slot_count, block_len, model_width)
    query_term = matmul_tn(normed, grad_query_pre)
    query_bias = jnp.sum(grad_query_pre.astype(jnp.float32), axis=0)
    key_term = matmul_tn(normed, grad_key_pre)
    key_bias = jnp.sum(grad_key_pre.astype(jnp.float32), axis=0)
    value_term = matmul_tn(normed, grad_value_pre)
    value_bias = jnp.sum(grad_value_pre.astype(jnp.float32), axis=0)
    shares = (
        lax.psum_scatter(grad_gain_one, "group", scatter_dimension=0, tiled=True),
        lax.psum_scatter(grad_gain_two, "group", scatter_dimension=0, tiled=True),
        lax.psum_scatter(query_term, "group", scatter_dimension=0, tiled=True),
        lax.psum_scatter(query_bias, "group", scatter_dimension=0, tiled=True),
        lax.psum_scatter(key_term, "group", scatter_dimension=0, tiled=True),
        lax.psum_scatter(key_bias, "group", scatter_dimension=0, tiled=True),
        lax.psum_scatter(value_term, "group", scatter_dimension=0, tiled=True),
        lax.psum_scatter(value_bias, "group", scatter_dimension=0, tiled=True),
        lax.psum_scatter(out_term, "group", scatter_dimension=0, tiled=True),
    )
    (
        gain_one_share,
        gain_two_share,
        query_share,
        query_bias_share,
        key_share,
        key_bias_share,
        value_share,
        value_bias_share,
        out_share,
    ) = shares
    summed = (
        lax.psum(gain_one_share.astype(jnp.bfloat16), "replica").astype(jnp.float32),
        lax.psum(gain_two_share.astype(jnp.bfloat16), "replica").astype(jnp.float32),
        lax.psum(query_share.astype(jnp.bfloat16), "replica").astype(jnp.float32),
        lax.psum(query_bias_share.astype(jnp.bfloat16), "replica").astype(jnp.float32),
        lax.psum(key_share.astype(jnp.bfloat16), "replica").astype(jnp.float32),
        lax.psum(key_bias_share.astype(jnp.bfloat16), "replica").astype(jnp.float32),
        lax.psum(value_share.astype(jnp.bfloat16), "replica").astype(jnp.float32),
        lax.psum(value_bias_share.astype(jnp.bfloat16), "replica").astype(jnp.float32),
        lax.psum(out_share.astype(jnp.bfloat16), "replica").astype(jnp.float32),
    )
    (
        gain_one_sum,
        gain_two_sum,
        query_sum,
        query_bias_sum,
        key_sum_w,
        key_bias_sum,
        value_sum_w,
        value_bias_sum,
        out_sum,
    ) = summed
    gate_sum = gate_up_sum[:, :hidden_units]
    up_sum = gate_up_sum[:, hidden_units:]
    return (
        layer_out,
        grad_input,
        gain_one_sum,
        query_sum,
        query_bias_sum,
        key_sum_w,
        key_bias_sum,
        value_sum_w,
        value_bias_sum,
        out_sum,
        gain_two_sum,
        gate_sum,
        up_sum,
        down_sum,
    )


def solution(mesh):
    placed = (
        P("replica", "group", None),
        P("replica"),
        P("group"),
        P("group", None),
        P("group"),
        P("group", None),
        P("group"),
        P("group", None),
        P("group"),
        P("group", None),
        P("group"),
        P("group", None),
        P("group", None),
        P("group", None),
        P("replica", "group", None),
    )
    return jax.shard_map(
        shards,
        mesh=mesh,
        in_specs=placed,
        out_specs=(
            P("replica", "group", None),
            P("replica", "group", None),
            P("group"),
            P("group", None),
            P("group"),
            P("group", None),
            P("group"),
            P("group", None),
            P("group"),
            P("group", None),
            P("group"),
            P("group", None),
            P("group", None),
            P("group", None),
        ),
        check_vma=False,
    )
```

profile of v0, /device:TPU:0, one launch (start us, length us, event | category | flops | bytes accessed | tf_op | source)
XLA Modules:
  0.0 2968.2 jit_solution(4528222993031043682)
XLA Ops:
  15.4 62.9 %all-reduce.11 = (bf16[1536]{0:T(1024)(128)(2,1)S(1)}, bf16[256]{0:T(256)(128)(2,1)S(1)}, bf16[1536]{0:T(1024)(128)(2,1)S(1)}, bf16[256]{0:T(256)(128)(2,1)S(1)}, bf16[1536]{0:T(1024)(128)(2,1)S(1)}) all-reduce(bf16[1536]{0:T(1024)(128)(2,1)S(1)} %dynamic-update-slice, ...), channel_id=1, replica_groups=mesh['replica'=2,'group'=16] {'group'}, use_global_device_ids=true, to_apply=%add | all-reduce | flops 5120 | bytes 20480
  79.2 20.1 all_gather.54
  102.1 21.0 all_gather.59
  140.9 38.4 %all-gather.12.cloned.1.call-done = bf16[2,1024,2,128]{3,1,2,0:T(8,128)(2,1)} async-done(((bf16[2,64,2,128]{3,1,2,0:T(8,128)(2,1)}), bf16[2,1024,2,128]{3,1,2,0:T(8,128)(2,1)}) %all-gather.12.cloned.1.call-update) | async-done | bytes 1048592 | tf_op jit(solution)/shard_map/all_gather | solution.py:233
  180.6 53.2 %all-gather.10.cloned.1.call-done = bf16[1536,1536]{1,0:T(8,128)(2,1)} async-done(((bf16[96,1536]{1,0:T(8,128)(2,1)}), bf16[1536,1536]{1,0:T(8,128)(2,1)}) %all-gather.10.cloned.1.call-update) | async-done | bytes 4718608 | tf_op jit(solution)/shard_map/all_gather | solution.py:209
  249.1 38.8 %all-gather.14.cloned.1.call-done = bf16[1536,1536]{1,0:T(8,128)(2,1)} async-done(((bf16[96,1536]{1,0:T(8,128)(2,1)}), bf16[1536,1536]{1,0:T(8,128)(2,1)}) %all-gather.14.cloned.1.call-update) | async-done | bytes 4718608 | tf_op jit(solution)/shard_map/all_gather | solution.py:215
  291.8 135.8 %all-gather.18.cloned.1.call-done = bf16[1536,8960]{1,0:T(8,128)(2,1)} async-done(((bf16[96,8960]{1,0:T(8,128)(2,1)}), bf16[1536,8960]{1,0:T(8,128)(2,1)}) %all-gather.18.cloned.1.call-update) | async-done | bytes 27525136 | tf_op jit(solution)/shard_map/all_gather | solution.py:261
  427.6 15.5 fusion.112
  443.1 125.7 %all-gather.16.cloned.1.call-done = bf16[1536,8960]{1,0:T(8,128)(2,1)} async-done(((bf16[96,8960]{1,0:T(8,128)(2,1)}), bf16[1536,8960]{1,0:T(8,128)(2,1)}) %all-gather.16.cloned.1.call-update) | async-done | bytes 27525136 | tf_op jit(solution)/shard_map/all_gather | solution.py:260
  568.8 15.3 fusion.111
  584.1 126.1 %all-gather.20.cloned.1.call-done = bf16[1536,8960]{1,0:T(8,128)(2,1)} async-done(((bf16[96,8960]{1,0:T(8,128)(2,1)}), bf16[1536,8960]{1,0:T(8,128)(2,1)}) %all-gather.20.cloned.1.call-update) | async-done | bytes 27525136 | tf_op jit(solution)/shard_map/all_gather | solution.py:262
  710.1 17.4 multiply_convert_fusion
  742.0 15.4 multiply_reduce_fusion
  785.7 70.3 %reduce-scatter.11.cloned.1.call-done = f32[2,64,2,128]{3,1,2,0:T(8,128)} async-done(((f32[2,1024,2,128]{3,1,2,0:T(8,128)}), f32[2,64,2,128]{3,1,2,0:T(8,128)}) %reduce-scatter.11.cloned.1.call-update) | async-done | bytes 131088 | tf_op jit(solution)/shard_map/reduce_scatter | solution.py:368
  858.6 62.3 %reduce-scatter.9.cloned.1.call-done = f32[2,64,2,128]{3,1,2,0:T(8,128)} async-done(((f32[2,1024,2,128]{3,1,2,0:T(8,128)}), f32[2,64,2,128]{3,1,2,0:T(8,128)}) %reduce-scatter.9.cloned.1.call-update) | async-done | bytes 131088 | tf_op jit(solution)/shard_map/reduce_scatter | solution.py:367
  940.0 21.5 fusion.114
  963.2 39.6 %fusion.42 = f32[1536,17920]{1,0:T(8,128)} fusion(bf16[128,1536]{1,0:T(8,128)(2,1)S(1)} %copy-done.30, bf16[128,8960]{1,0:T(8,128)(2,1)} %get-tuple-element.469, bf16[128,8960]{1,0:T(8,128)(2,1)S(1)} %copy-done.14), kind=kOutput, calls=%fused_computation.64 | convolution fusion | flops 7055605760 | bytes 115081216 | tf_op jit(solution)/shard_map/dot_general | solution.py:59
  1010.7 57.8 %all-reduce.10 = (bf16[1536]{0:T(1024)(128)(2,1)S(1)}, bf16[1536]{0:T(1024)(128)(2,1)S(1)}, bf16[256]{0:T(256)(128)(2,1)S(1)}, bf16[256]{0:T(256)(128)(2,1)S(1)}, bf16[1536]{0:T(1024)(128)(2,1)S(1)}) all-reduce(f32[1536]{0:T(1024)S(1)} %get-tuple-element.354, ...), channel_id=4, replica_groups=mesh['replica'=2,'group'=16] {'group'}, use_global_device_ids=true, to_apply=%region_19.20.clone | all-reduce | flops 5120 | bytes 30720
  1074.6 85.5 %reduce-scatter.19.cloned.1.call-done = f32[96,1536]{1,0:T(8,128)} async-done(((f32[1536,1536]{1,0:T(8,128)}), f32[96,1536]{1,0:T(8,128)}) %reduce-scatter.19.cloned.1.call-update) | async-done | bytes 589840 | tf_op jit(solution)/shard_map/reduce_scatter | solution.py:401
  1161.9 114.0 %reduce-scatter.13.cloned.1.call-done = f32[96,1536]{1,0:T(8,128)} async-done(((f32[1536,1536]{1,0:T(8,128)}), f32[96,1536]{1,0:T(8,128)}) %reduce-scatter.13.cloned.1.call-update) | async-done | bytes 589840 | tf_op jit(solution)/shard_map/reduce_scatter | solution.py:395
  1277.7 508.7 %reduce-scatter.23.cloned.1.call-done = f32[96,8960]{1,0:T(8,128)} async-done(((f32[1536,8960]{1,0:T(8,128)}), f32[96,8960]{1,0:T(8,128)}) %reduce-scatter.23.cloned.1.call-update) | async-done | bytes 3440656 | tf_op jit(solution)/shard_map/reduce_scatter | solution.py:318
  1789.7 989.4 %reduce-scatter.21.cloned.1.call-done = f32[96,17920]{1,0:T(8,128)} async-done(((f32[1536,17920]{1,0:T(8,128)}), f32[96,17920]{1,0:T(8,128)}) %reduce-scatter.21.cloned.1.call-update) | async-done | bytes 6881296 | tf_op jit(solution)/shard_map/reduce_scatter | solution.py:321
  2786.1 14.9 fusion.48
  2812.7 137.9 %all-reduce.19.cloned.1.call-done = (bf16[96,1536]{1,0:T(8,128)(2,1)}, bf16[96,1536]{1,0:T(8,128)(2,1)}, bf16[96,17920]{1,0:T(8,128)(2,1)}, bf16[96,8960]{1,0:T(8,128)(2,1)}) async-done(((bf16[96,1536]{1,0:T(8,128)(2,1)}, bf16[96,1536]{1,0:T(8,128)(2,1)}, bf16[96,17920]{1,0:T(8,128)(2,1)}, bf16[96,8960]{1,0:T(8,128)(2,1)}), (bf16[96,1536]{1,0:T(8,128)(2,1)}, bf16[96,1536]{1,0:T(8,128)(2,1)}, ...) | async-done | bytes 5750800 | tf_op jit(solution)/shard_map/psum | solution.py:417
  (328 shorter events, 176.0 us)
Async XLA Ops:
  7.2 132.4 %all-gather.8.cloned.1.call-start = ((), (), s32[]{:S(2)}) async-start(), calls=%async_computation.8 | async-start | bytes 1114112 | tf_op jit(solution)/shard_map/all_gather | solution.py:232
  79.2 160.8 %copy-start.39 = (f32[64,128]{1,0:T(8,128)}, f32[64,128]{1,0:T(8,128)S(1)}, u32[]{:S(2)}) copy-start(f32[64,128]{1,0:T(8,128)S(1)} %get-tuple-element.501) | copy-start | bytes 98308
  79.2 160.8 %copy-start.41 = (f32[64,128]{1,0:T(8,128)}, f32[64,128]{1,0:T(8,128)S(1)}, u32[]{:S(2)}) copy-start(f32[64,128]{1,0:T(8,128)S(1)} %get-tuple-element.500) | copy-start | bytes 98308
  102.0 77.3 %all-gather.12.cloned.1.call-start = ((), (), s32[]{:S(2)}) async-start(), calls=%async_computation.10 | async-start | bytes 1114112 | tf_op jit(solution)/shard_map/all_gather | solution.py:233
  125.0 108.8 %all-gather.10.cloned.1.call-start = ((), (), s32[]{:S(2)}) async-start(), calls=%async_computation.9 | async-start | bytes 5013504 | tf_op jit(solution)/shard_map/all_gather | solution.py:209
  125.7 162.2 %all-gather.14.cloned.1.call-start = ((), (), s32[]{:S(2)}) async-start(), calls=%async_computation.11 | async-start | bytes 5013504 | tf_op jit(solution)/shard_map/all_gather | solution.py:215
  126.3 301.3 %all-gather.18.cloned.1.call-start = ((), (), s32[]{:S(2)}) async-start(), calls=%async_computation.13 | async-start | bytes 29245440 | tf_op jit(solution)/shard_map/all_gather | solution.py:261
  126.9 441.9 %all-gather.16.cloned.1.call-start = ((), (), s32[]{:S(2)}) async-start(), calls=%async_computation.12 | async-start | bytes 29245440 | tf_op jit(solution)/shard_map/all_gather | solution.py:260
  127.4 582.7 %all-gather.20.cloned.1.call-start = ((), (), s32[]{:S(2)}) async-start(), calls=%async_computation.14 | async-start | bytes 29245440 | tf_op jit(solution)/shard_map/all_gather | solution.py:262
  128.2 727.8 %reduce-scatter.11.cloned.1.call-start = ((), (), s32[]{:S(2)}) async-start(), calls=%async_computation.16 | async-start | bytes 2228224 | tf_op jit(solution)/shard_map/reduce_scatter | solution.py:368
  291.1 467.0 %copy-start.3 = (f32[128,1536]{1,0:T(8,128)}, f32[128,1536]{1,0:T(8,128)S(1)}, u32[]{:S(2)}) copy-start(f32[128,1536]{1,0:T(8,128)S(1)} %get-tuple-element.511) | copy-start | bytes 2359300
  291.8 277.0 %copy-start.29 = (bf16[128,1536]{1,0:T(8,128)(2,1)}, bf16[128,1536]{1,0:T(8,128)(2,1)S(1)}, u32[]{:S(2)}) copy-start(bf16[128,1536]{1,0:T(8,128)(2,1)S(1)} %multiply_convert_fusion.3) | copy-start | bytes 1179652
  443.1 267.0 %copy-start.33 = (bf16[128,1536]{1,0:T(8,128)(2,1)S(1)}, bf16[128,1536]{1,0:T(8,128)(2,1)}, u32[]{:S(2)}) copy-start(bf16[128,1536]{1,0:T(8,128)(2,1)} %fusion.53) | copy-start | bytes 1179652
  783.9 137.0 %reduce-scatter.9.cloned.1.call-start = ((), (), s32[]{:S(2)}) async-start(), calls=%async_computation.15 | async-start | bytes 2228224 | tf_op jit(solution)/shard_map/reduce_scatter | solution.py:367
  785.4 135.5 %copy-start.46 = (f32[64,128]{1,0:T(8,128)S(1)}, f32[64,128]{1,0:T(8,128)}, u32[]{:S(2)}) copy-start(f32[64,128]{1,0:T(8,128)} %get-tuple-element.499) | copy-start | bytes 98308
  785.4 136.5 %copy-start.47 = (f32[64,128]{1,0:T(8,128)S(1)}, f32[64,128]{1,0:T(8,128)}, u32[]{:S(2)}) copy-start(f32[64,128]{1,0:T(8,128)} %get-tuple-element.498) | copy-start | bytes 98308
  785.5 286.0 %reduce-scatter.17.cloned.1.call-start = ((), (), s32[]{:S(2)}) async-start(), calls=%async_computation.19 | async-start | bytes 1671168 | tf_op jit(solution)/shard_map/reduce_scatter | solution.py:399
  858.6 214.4 %reduce-scatter.15.cloned.1.call-start = ((), (), s32[]{:S(2)}) async-start(), calls=%async_computation.18 | async-start | bytes 1671168 | tf_op jit(solution)/shard_map/reduce_scatter | solution.py:397
  925.2 234.8 %reduce-scatter.19.cloned.1.call-start = ((), (), s32[]{:S(2)}) async-start(), calls=%async_computation.20 | async-start | bytes 10027008 | tf_op jit(solution)/shard_map/reduce_scatter | solution.py:401
  930.3 345.5 %reduce-scatter.13.cloned.1.call-start = ((), (), s32[]{:S(2)}) async-start(), calls=%async_computation.17 | async-start | bytes 10027008 | tf_op jit(solution)/shard_map/reduce_scatter | solution.py:395
  938.3 848.1 %reduce-scatter.23.cloned.1.call-start = ((), (), s32[]{:S(2)}) async-start(), calls=%async_computation.22 | async-start | bytes 58490880 | tf_op jit(solution)/shard_map/reduce_scatter | solution.py:318
  961.5 1817.7 %reduce-scatter.21.cloned.1.call-start = ((), (), s32[]{:S(2)}) async-start(), calls=%async_computation.21 | async-start | bytes 116981760 | tf_op jit(solution)/shard_map/reduce_scatter | solution.py:321
  1002.8 1801.3 %all-reduce.17.cloned.1.call-start = ((), (), s32[]{:S(2)}) async-start(), calls=%async_computation.23 | async-start | bytes 201728 | tf_op jit(solution)/shard_map/psum | solution.py:415
  1074.5 1876.1 %all-reduce.19.cloned.1.call-start = ((), (), s32[]{:S(2)}) async-start(), calls=%async_computation.24 | async-start | bytes 11501568 | tf_op jit(solution)/shard_map/psum | solution.py:417
  (52 other events, 904.7 us)
Sparse Core Ops, SparseCore 0:
  102.2 37.4 all-gather.7
  142.4 36.8 all-gather.11
  181.6 52.1 all-gather.9
  235.9 51.9 all-gather.13
  289.3 138.2 all-gather.17
  429.1 139.6 all-gather.15
  570.4 139.6 all-gather.19
  784.0 71.9 reduce-scatter.10
  860.2 60.6 reduce-scatter.8
  924.4 58.4 reduce-scatter.16
  987.0 58.6 reduce-scatter.14
  1049.7 110.3 reduce-scatter.18
  1164.7 111.1 reduce-scatter.12
  1280.0 506.3 reduce-scatter.22
  1791.0 988.0 reduce-scatter.20
  2782.8 21.2 all-reduce.16
  2807.8 142.7 all-reduce.18
where the time goes:
time: 2980 us; the launch traced here: 2970 us
  waiting for transfers between devices  2500 us (84%)
  matrix products  195 us (7%)
  blocking collectives  162 us (5%)
  other arithmetic  58.3 us (2%)
  local copies, waits for them, and re-layouts  34.3 us (1%)
    reduce_scatter x1, waiting for transfers between devices, shards(): lax.psum_scatter(matmul_tn(normed_two, gate_up_grad), 'group', scatter_di...  989 us
    reduce_scatter x1, waiting for transfers between devices, shards(): lax.psum_scatter(matmul_tn(grad_down_in, hidden), 'group', scatter_dimens...  509 us
    psum x1, waiting for transfers between devices, shards(): lax.psum(query_share.astype(jnp.bfloat16), 'replica').astype(jnp.float32)  138 us
    all_gather x1, waiting for transfers between devices, shards(): lax.all_gather(w_up, 'group', axis=0, tiled=True)  136 us
    all_gather x1, waiting for transfers between devices, shards(): lax.all_gather(w_down, 'group', axis=0, tiled=True)  126 us
    all_gather x1, waiting for transfers between devices, shards(): lax.all_gather(w_gate, 'group', axis=0, tiled=True)  126 us
    unnamed x2, blocking collectives  121 us
    reduce_scatter x1, waiting for transfers between devices, shards(): lax.psum_scatter(query_term, 'group', scatter_dimension=0, tiled=True)  114 us
  transfers between devices with their start and end apart: 17, of which 15 were waited for; matrix products, arithmetic and copies ran while one was open for 6% of the time, Pallas kernels for 0%

commit v1 on v0

v1 whole, which is shorter than its diff:
```python
import jax
import jax.numpy as jnp
from jax import lax
from jax.sharding import PartitionSpec as P

HEADS = 12
KV_HEADS = 2
HEAD_DIM = 128
EPSILON = 1e-06
THETA = 1000000.0
BF = jnp.bfloat16
F32 = jnp.float32


def rope_tables(positions, head_dim):
    freqs = THETA ** (-jnp.arange(0, head_dim, 2).astype(F32) / head_dim)
    angles = positions.astype(F32)[:, None] * freqs[None, :]
    angles = jnp.concatenate((angles, angles), axis=-1)
    return (jnp.cos(angles), jnp.sin(angles))


def rotate(tensor, cos_table, sin_table):
    halfway = tensor.shape[-1] // 2
    turned = jnp.concatenate((-tensor[..., halfway:], tensor[..., :halfway]), axis=-1)
    return tensor * cos_table + turned * sin_table


def rotate_back(gradient, cos_table, sin_table):
    halfway = gradient.shape[-1] // 2
    scaled = gradient * sin_table
    turned = jnp.concatenate((scaled[..., halfway:], -scaled[..., :halfway]), axis=-1)
    return gradient * cos_table + turned


def normalize(row_values, gain_vec):
    factor = lax.rsqrt(jnp.mean(row_values * row_values, axis=-1, keepdims=True) + EPSILON)
    return (row_values * factor * gain_vec, factor)


def norm_back(row_values, factor, gain_vec, upstream):
    weighted = upstream * gain_vec
    inner_mean = jnp.mean(weighted * row_values, axis=-1, keepdims=True)
    grad_rows = factor * weighted - row_values * (factor * factor * factor) * inner_mean
    grad_gain = jnp.sum(upstream * row_values * factor, axis=0)
    return (grad_rows, grad_gain)


def matmul(a, b):
    return jnp.dot(a, b, preferred_element_type=F32)


def matmul_nt(a, b):
    return lax.dot_general(a, b, (((1,), (1,)), ((), ())), preferred_element_type=F32)


def matmul_tn(a, b):
    return lax.dot_general(a, b, (((0,), (0,)), ((), ())), preferred_element_type=F32)


def arrange(per_token, kv_heads):
    block_len, head_count, head_dim = per_token.shape
    repeat = head_count // kv_heads
    grouped = per_token.reshape(block_len, kv_heads, repeat, head_dim)
    return jnp.transpose(grouped, (1, 2, 0, 3)).reshape(kv_heads, repeat * block_len, head_dim)


def restore(per_group, block_len):
    kv_heads, row_count, head_dim = per_group.shape
    repeat = row_count // block_len
    grouped = per_group.reshape(kv_heads, repeat, block_len, head_dim)
    return jnp.transpose(grouped, (2, 0, 1, 3)).reshape(block_len, kv_heads * repeat * head_dim)


def masked_exp(query_rows, key_block, row_pos, first_key, length, score_scale):
    key_step = key_block.shape[0]
    raw_scores = jnp.einsum("grd,kgd->grk", query_rows, key_block, preferred_element_type=F32)
    key_pos = first_key + jnp.arange(key_step, dtype=jnp.int32)
    allowed = (key_pos[None, :] <= row_pos[:, None]) & (key_pos[None, :] < length)
    return jnp.where(allowed[None], jnp.exp(raw_scores * score_scale), 0.0)


def block_total(length, rank_end, key_step):
    key_limit = jnp.minimum(length, rank_end)
    return (key_limit + key_step - 1) // key_step


def attend_forward(query_rows, key_all, value_all, row_pos, length, rank_end, key_step, scale):
    kv_heads, row_count, head_dim = query_rows.shape

    def visit(block_index, state_tuple):
        totals, numerator = state_tuple
        first_key = block_index * key_step
        key_block = lax.dynamic_slice_in_dim(key_all, first_key, key_step, 0)
        value_block = lax.dynamic_slice_in_dim(value_all, first_key, key_step, 0)
        weights = masked_exp(query_rows, key_block, row_pos, first_key, length, scale)
        totals = totals + jnp.sum(weights, axis=-1)
        numerator = numerator + jnp.einsum(
            "grk,kgd->grd", weights.astype(BF), value_block, preferred_element_type=F32
        )
        return (totals, numerator)

    initial = (
        jnp.zeros((kv_heads, row_count), F32),
        jnp.zeros((kv_heads, row_count, head_dim), F32),
    )
    return lax.fori_loop(0, block_total(length, rank_end, key_step), visit, initial)


def attend_backward(
    query_rows, key_all, value_all, row_pos, length, rank_end, key_step, scale, grad_numer, grad_total
):
    kv_heads, row_count, head_dim = query_rows.shape

    def visit(block_index, state_tuple):
        grad_query, grad_key, grad_value = state_tuple
        first_key = block_index * key_step
        key_block = lax.dynamic_slice_in_dim(key_all, first_key, key_step, 0)
        value_block = lax.dynamic_slice_in_dim(value_all, first_key, key_step, 0)
        weights = masked_exp(query_rows, key_block, row_pos, first_key, length, scale)
        grad_prob = jnp.einsum("grd,kgd->grk", grad_numer, value_block, preferred_element_type=F32)
        grad_score = (weights * (grad_prob + grad_total[..., None])).astype(BF)
        grad_query = grad_query + jnp.einsum(
            "grk,kgd->grd", grad_score, key_block, preferred_element_type=F32
        )
        key_part = jnp.einsum("grk,grd->kgd", grad_score, query_rows, preferred_element_type=F32)
        value_part = jnp.einsum(
            "grk,grd->kgd", weights.astype(BF), grad_numer, preferred_element_type=F32
        )
        key_old = lax.dynamic_slice_in_dim(grad_key, first_key, key_step, 0)
        value_old = lax.dynamic_slice_in_dim(grad_value, first_key, key_step, 0)
        grad_key = lax.dynamic_update_slice_in_dim(grad_key, key_old + key_part, first_key, 0)
        grad_value = lax.dynamic_update_slice_in_dim(
            grad_value, value_old + value_part, first_key, 0
        )
        return (grad_query, grad_key, grad_value)

    initial = (
        jnp.zeros((kv_heads, row_count, head_dim), F32),
        jnp.zeros(key_all.shape, F32),
        jnp.zeros(value_all.shape, F32),
    )
    return lax.fori_loop(0, block_total(length, rank_end, key_step), visit, initial)


def gather(x):
    return lax.all_gather(x, "group", axis=0, tiled=True)


def scatter_sum(x):
    return lax.psum_scatter(x, "group", scatter_dimension=0, tiled=True)


def shards(
    hidden_in,
    lengths,
    gain_attn,
    w_query,
    b_query,
    w_key,
    b_key,
    w_value,
    b_value,
    w_out,
    gain_mlp,
    w_gate,
    w_up,
    w_down,
    cotangent,
):
    group_count = lax.axis_size("group")
    group_rank = lax.axis_index("group")
    slot_count, block_len, model_width = hidden_in.shape
    kv_heads = KV_HEADS
    head_dim = HEAD_DIM
    kv_width = kv_heads * head_dim
    repeat = HEADS // kv_heads
    slot_span = block_len * group_count
    key_step = min(512, slot_span)
    score_scale = head_dim ** (-0.5)
    tokens = slot_count * block_len
    hidden_units = w_gate.shape[1]
    own_rows = w_gate.shape[0]
    share = hidden_units // group_count
    positions = group_rank * block_len + jnp.arange(block_len, dtype=jnp.int32)
    valid_rows = (positions[None, :] < lengths[:, None]).astype(F32).reshape(tokens, 1)
    cos_table, sin_table = rope_tables(positions, head_dim)
    cos_heads = cos_table[:, None, :]
    sin_heads = sin_table[:, None, :]
    rank_end = (group_rank + 1) * block_len
    row_pos = jnp.tile(positions, repeat)

    pieces = (gain_attn, b_query, b_key, b_value, gain_mlp)
    sizes = [p.shape[0] for p in pieces]
    small = gather(jnp.concatenate(pieces)[None])
    offsets = [sum(sizes[:i]) for i in range(len(sizes) + 1)]
    gain_one, query_b, key_b, value_b, gain_two = [
        small[:, offsets[i] : offsets[i + 1]].reshape(-1).astype(F32) for i in range(len(sizes))
    ]
    qkv_w = gather(jnp.concatenate((w_query, w_key, w_value), axis=1))
    out_w = gather(w_out)
    qkv_b = jnp.concatenate((query_b, key_b, value_b))

    stacked = jnp.stack((w_gate, w_up, w_down)).reshape(3, own_rows, group_count, share)
    stacked = jnp.transpose(stacked, (2, 1, 0, 3)).reshape(group_count, own_rows, 3 * share)
    columns = lax.all_to_all(stacked, "group", 0, 0, tiled=True).reshape(model_width, 3 * share)
    gate_up_w = columns[:, : 2 * share]
    down_w = columns[:, 2 * share :]

    grad_final = cotangent.reshape(tokens, model_width).astype(F32) * valid_rows
    grad_all = gather(grad_final.astype(BF))

    inputs = hidden_in.reshape(tokens, model_width).astype(F32)
    normed_full, factor_one = normalize(inputs, gain_one)
    normed = normed_full.astype(BF)
    qkv = matmul(normed, qkv_w) + qkv_b
    query_rot = rotate(
        qkv[:, :model_width].reshape(slot_count, block_len, HEADS, head_dim), cos_heads, sin_heads
    ).astype(BF)
    key_rot = rotate(
        qkv[:, model_width : model_width + kv_width].reshape(
            slot_count, block_len, kv_heads, head_dim
        ),
        cos_heads,
        sin_heads,
    ).astype(BF)
    value_low = qkv[:, model_width + kv_width :].astype(BF)
    pair = jnp.concatenate(
        (key_rot.reshape(tokens, kv_width), value_low), axis=1
    ).reshape(1, slot_count, block_len, 2 * kv_width)
    pair_all = jnp.transpose(gather(pair), (1, 0, 2, 3)).reshape(
        slot_count, slot_span, 2, kv_heads, head_dim
    )
    key_all = pair_all[:, :, 0]
    value_all = pair_all[:, :, 1]
    query_groups = []
    slot_totals = []
    slot_attended = []
    attended_rows = []
    for s in range(slot_count):
        query_rows = arrange(query_rot[s], kv_heads)
        totals, numerator = attend_forward(
            query_rows, key_all[s], value_all[s], row_pos, lengths[s], rank_end, key_step, score_scale
        )
        attended = numerator / totals[..., None]
        query_groups.append(query_rows)
        slot_totals.append(totals)
        slot_attended.append(attended)
        attended_rows.append(restore(attended, block_len))
    attended_low = jnp.concatenate(attended_rows, axis=0).astype(BF)
    residual_mid = inputs + matmul(attended_low, out_w)
    normed_two_full, factor_two = normalize(residual_mid, gain_two)
    normed_all = gather(normed_two_full.astype(BF))

    pre = matmul(normed_all, gate_up_w)
    gate_pre = pre[:, :share]
    up_pre = pre[:, share:]
    sigmoid_gate = jax.nn.sigmoid(gate_pre)
    silu_gate = gate_pre * sigmoid_gate
    hidden = (silu_gate * up_pre).astype(BF)
    grad_hidden = matmul(grad_all, down_w)
    grad_gate = (
        grad_hidden * up_pre * (sigmoid_gate * (1.0 + gate_pre * (1.0 - sigmoid_gate)))
    ).astype(BF)
    grad_up = (grad_hidden * silu_gate).astype(BF)
    gate_up_grad = jnp.concatenate((grad_gate, grad_up), axis=1)
    grad_normed_two = scatter_sum(matmul_nt(gate_up_grad, gate_up_w).astype(BF)).astype(F32)
    mlp_out = scatter_sum(matmul_nt(hidden, down_w).astype(BF)).astype(F32)
    down_term = matmul_tn(grad_all, hidden)
    gate_up_term = matmul_tn(normed_all, gate_up_grad)
    terms = jnp.concatenate((gate_up_term, down_term), axis=1).astype(BF)
    back = lax.all_to_all(
        terms.reshape(group_count, own_rows, 3 * share), "group", 0, 0, tiled=True
    )
    summed = back.astype(F32) + lax.ppermute(back, "replica", [(0, 1), (1, 0)]).astype(F32)
    summed = jnp.transpose(summed.reshape(group_count, own_rows, 3, share), (2, 1, 0, 3))
    gate_sum, up_sum, down_sum = summed.reshape(3, own_rows, hidden_units)

    final_rows = residual_mid + mlp_out
    layer_out = (final_rows * valid_rows).reshape(slot_count, block_len, model_width).astype(BF)
    grad_mid_norm, grad_gain_two = norm_back(residual_mid, factor_two, gain_two, grad_normed_two)
    grad_mid = grad_final + grad_mid_norm
    grad_branch = grad_mid.astype(BF)
    out_term = matmul_tn(attended_low, grad_branch)
    grad_attended = matmul_nt(grad_branch, out_w)
    grad_query_rows = []
    grad_pairs = []
    for s in range(slot_count):
        slot_grad = grad_attended[s * block_len : (s + 1) * block_len].reshape(
            block_len, HEADS, head_dim
        )
        grad_out = arrange(slot_grad, kv_heads)
        totals = slot_totals[s]
        grad_total = -jnp.sum(grad_out * slot_attended[s], axis=-1) / totals
        grad_numer = (grad_out / totals[..., None]).astype(BF)
        grad_query, grad_key, grad_value = attend_backward(
            query_groups[s],
            key_all[s],
            value_all[s],
            row_pos,
            lengths[s],
            rank_end,
            key_step,
            score_scale,
            grad_numer,
            grad_total,
        )
        query_back_rows = restore(grad_query * score_scale, block_len).reshape(
            block_len, HEADS, head_dim
        )
        grad_query_rows.append(
            rotate_back(query_back_rows, cos_heads, sin_heads).reshape(block_len, HEADS * head_dim)
        )
        grad_pairs.append(
            jnp.concatenate(
                (grad_key.reshape(slot_span, kv_width), grad_value.reshape(slot_span, kv_width)),
                axis=1,
            )
        )
    pair_grads = jnp.stack(grad_pairs).reshape(slot_count, group_count, block_len, 2 * kv_width)
    pair_grads = jnp.transpose(pair_grads, (1, 0, 2, 3)).astype(BF)
    pair_sum = scatter_sum(pair_grads).reshape(slot_count, block_len, 2 * kv_width).astype(F32)
    grad_query_pre = jnp.concatenate(grad_query_rows, axis=0).astype(BF)
    key_sum = pair_sum[..., :kv_width].reshape(slot_count, block_len, kv_heads, head_dim)
    grad_key_pre = (
        rotate_back(key_sum * score_scale, cos_heads, sin_heads).astype(BF).reshape(tokens, kv_width)
    )
    grad_value_pre = pair_sum[..., kv_width:].astype(BF).reshape(tokens, kv_width)
    grad_qkv = jnp.concatenate((grad_query_pre, grad_key_pre, grad_value_pre), axis=1)
    grad_normed = matmul_nt(grad_qkv, qkv_w)
    grad_in_norm, grad_gain_one = norm_back(inputs, factor_one, gain_one, grad_normed)
    grad_input = (grad_mid + grad_in_norm).reshape(slot_count, block_len, model_width)
    qkv_term = matmul_tn(normed, grad_qkv)
    qkv_bias = jnp.sum(grad_qkv.astype(F32), axis=0)

    weight_share = scatter_sum(
        jnp.concatenate((qkv_term, out_term), axis=1).astype(BF)
    )
    weight_sum = weight_share.astype(F32) + lax.ppermute(
        weight_share, "replica", [(0, 1), (1, 0)]
    ).astype(F32)
    vectors = jnp.concatenate(
        [
            grad_gain_one.reshape(group_count, -1),
            qkv_bias[:model_width].reshape(group_count, -1),
            qkv_bias[model_width : model_width + kv_width].reshape(group_count, -1),
            qkv_bias[model_width + kv_width :].reshape(group_count, -1),
            grad_gain_two.reshape(group_count, -1),
        ],
        axis=1,
    )
    vector_sum = lax.psum(scatter_sum(vectors), "replica").reshape(-1)
    gain_one_sum, query_bias_sum, key_bias_sum, value_bias_sum, gain_two_sum = [
        vector_sum[offsets[i] : offsets[i + 1]] for i in range(len(sizes))
    ]
    ends = (0, model_width, model_width + kv_width, model_width + 2 * kv_width)
    query_sum, key_sum_w, value_sum_w = [weight_sum[:, ends[i] : ends[i + 1]] for i in range(3)]
    out_sum = weight_sum[:, ends[3] :]
    return (
        layer_out,
        grad_input,
        gain_one_sum,
        query_sum,
        query_bias_sum,
        key_sum_w,
        key_bias_sum,
        value_sum_w,
        value_bias_sum,
        out_sum,
        gain_two_sum,
        gate_sum,
        up_sum,
        down_sum,
    )


def solution(mesh):
    act = P("replica", "group", None)
    vec = P("group")
    mat = P("group", None)
    return jax.shard_map(
        shards,
        mesh=mesh,
        in_specs=(act, P("replica"), vec, mat, vec, mat, vec, mat, vec, mat, vec, mat, mat, mat, act),
        out_specs=(act, act, vec, mat, vec, mat, vec, mat, vec, mat, vec, mat, mat, mat),
        check_vma=False,
    )
```

time: 2980 us -> 1160 us (0.39)
  waiting for transfers between devices: 2500 us -> 507 us
  blocking collectives: 162 us -> 370 us
  matrix products: 195 us -> 100 us
  local copies, waits for them, and re-layouts: 34.3 us -> 103 us
    reduce_scatter x8 -> x3, waiting for transfers between devices: 1830 us -> 164 us  [scatter_sum(): return lax.psum_scatter(x, 'group', scatter_dimension=0, tiled=True)]
    all_gather x7 -> x5, waiting for transfers between devices: 526 us -> 109 us  [gather(): return lax.all_gather(x, 'group', axis=0, tiled=True)]
    all_to_all x0 -> x1, blocking collectives: none -> 192 us  [shards(): lax.all_to_all(terms.reshape(group_count, own_rows, 3 * share), 'group',...]
    psum x2 -> x0, waiting for transfers between devices: 138 us -> none  [the longest x1 138 us: shards(): lax.psum(query_share.astype(jnp.bfloat16), 'replica').astype(jnp.float32)]
    all_to_all x0 -> x1, waiting for transfers between devices: none -> 134 us  [shards(): lax.all_to_all(stacked, 'group', 0, 0, tiled=True)]
    unnamed x17 -> x10, waiting for transfers between devices: 3.15 us -> 100 us
    dot_general x24 -> x16, matrix products: 186 us -> 91.7 us  [the longest x4 33 us: matmul(): return jnp.dot(a, b, preferred_element_type=F32)]
    psum x0 -> x1, blocking collectives: none -> 53.9 us  [shards(): vector_sum = lax.psum(scatter_sum(vectors), 'replica').reshape(-1)]
  transfers between devices with their start and end apart: 17 -> 12, of which waited for: 15 -> 7; matrix products, arithmetic and copies ran while one was open for 6% -> 15% of each run, Pallas kernels for 0% -> 0%
where the time goes in v1:
time: 1160 us
  waiting for transfers between devices  507 us (44%)
  blocking collectives  370 us (32%)
  local copies, waits for them, and re-layouts  103 us (9%)
  matrix products  100 us (9%)
  other arithmetic  48.8 us (4%)
  between operations  17.1 us (1%)
    all_to_all x1, blocking collectives, shards(): lax.all_to_all(terms.reshape(group_count, own_rows, 3 * share), 'group',...  192 us
    reduce_scatter x3, waiting for transfers between devices, scatter_sum(): return lax.psum_scatter(x, 'group', scatter_dimension=0, tiled=True)  164 us
    all_to_all x1, waiting for transfers between devices, shards(): lax.all_to_all(stacked, 'group', 0, 0, tiled=True)  134 us
    unnamed x2, blocking collectives  124 us
    all_gather x5, waiting for transfers between devices, gather(): return lax.all_gather(x, 'group', axis=0, tiled=True)  109 us
    unnamed x10, waiting for transfers between devices  100 us
    psum x1, blocking collectives, shards(): vector_sum = lax.psum(scatter_sum(vectors), 'replica').reshape(-1)  53.9 us
    dot_general x4, matrix products, matmul(): return jnp.dot(a, b, preferred_element_type=F32)  33 us
  transfers between devices with their start and end apart: 12, of which 7 were waited for; matrix products, arithmetic and copies ran while one was open for 15% of the time, Pallas kernels for 0%

profile of v1, /device:TPU:0, one launch (start us, length us, event | category | flops | bytes accessed | tf_op | source)
XLA Modules:
  0.0 1155.6 jit_solution(5577868907293726895)
XLA Ops:
  14.8 64.2 %all-reduce = bf16[5120]{0:T(1024)(128)(2,1)S(1)} all-reduce(bf16[5120]{0:T(1024)(128)(2,1)S(1)} %dynamic-update-slice), channel_id=2, replica_groups=mesh['replica'=2,'group'=16] {'group'}, use_global_device_ids=true, to_apply=%add | all-reduce | flops 5120 | bytes 20480
  92.2 34.8 %all-gather.9.cloned.1.call-done = bf16[16,2,64,512]{3,2,0,1:T(8,128)(2,1)} async-done(((bf16[1,2,64,512]{3,2,0,1:T(8,128)(2,1)}), bf16[16,2,64,512]{3,2,0,1:T(8,128)(2,1)}) %all-gather.9.cloned.1.call-update) | async-done | bytes 2097168 | tf_op jit(solution)/shard_map/all_gather | solution.py:146
  138.4 42.9 %all-gather.11.cloned.1.call-done = bf16[1536,1536]{1,0:T(8,128)(2,1)} async-done(((bf16[96,1536]{1,0:T(8,128)(2,1)}), bf16[1536,1536]{1,0:T(8,128)(2,1)}) %all-gather.11.cloned.1.call-update) | async-done | bytes 4718608 | tf_op jit(solution)/shard_map/all_gather | solution.py:146
  197.4 6.2 pad_maximum_fusion.1
  203.6 8.6 copy.128
  218.3 134.1 %all-to-all-done = bf16[16,96,1680]{2,1,0:T(8,128)(2,1)} async-done(((bf16[16,96,1680]{2,1,0:T(8,128)(2,1)}), bf16[16,96,1680]{2,1,0:T(8,128)(2,1)}, u32[]{:S(2)}, u32[]{:S(2)}) %all-to-all-start) | async-done | bytes 5160992 | tf_op jit(solution)/shard_map/all_to_all | solution.py:205
  352.3 13.4 %fusion.44 = f32[2048,1120]{0,1:T(8,128)} fusion(bf16[2048,1536]{1,0:T(8,128)(2,1)} %all-gather.13.cloned.1.call-done, bf16[1536,1680]{1,0:T(8,128)(2,1)} %bitcast.28), kind=kOutput, calls=%fused_computation.80 | convolution fusion | flops 7046430720 | bytes 19005440 | tf_op jit(solution)/shard_map/dot_general | solution.py:49
  365.8 31.5 %all-gather.15.cloned.1.call-done = bf16[2048,1536]{1,0:T(8,128)(2,1)} async-done(((bf16[128,1536]{1,0:T(8,128)(2,1)}), bf16[2048,1536]{1,0:T(8,128)(2,1)}) %all-gather.15.cloned.1.call-update) | async-done | bytes 6291472 | tf_op jit(solution)/shard_map/all_gather | solution.py:146
  397.3 12.5 %multiply_convert_fusion.1 = (bf16[2048,560]{0,1:T(8,128)(2,1)S(1)}, bf16[2048,560]{0,1:T(8,128)(2,1)S(1)}, bf16[2048,560]{0,1:T(8,128)(2,1)}) fusion(f32[2048,1120]{0,1:T(8,128)} %fusion.44, bf16[2048,1536]{1,0:T(8,128)(2,1)} %all-gather.15.cloned.1.call-done, bf16[1536,1680]{1,0:T(8,128)(2,1)} %bitcast.28), kind=kOutput, calls=%fused_computation.75 | convolution fusion | flops 3540418560 | bytes 24313856 | tf_op jit(solution)/shard_map/dot_general | solution.py:49
  411.9 12.3 %convolution_convert_fusion = bf16[2048,1536]{1,0:T(8,128)(2,1)} fusion(bf16[1536,1680]{1,0:T(8,128)(2,1)} %bitcast.28, bf16[2048,560]{0,1:T(8,128)(2,1)S(1)} %get-tuple-element.602, bf16[2048,560]{0,1:T(8,128)(2,1)S(1)} %get-tuple-element.601), kind=kOutput, calls=%fused_computation.66 | convolution fusion | flops 7058751488 | bytes 14417920 | tf_op jit(solution)/shard_map/dot_general | solution.py:53
  424.5 9.7 convolution_convert_fusion.3
  434.3 12.1 %convolution_convert_fusion.1 = bf16[1536,1120]{0,1:T(8,128)(2,1)} fusion(bf16[2048,1536]{1,0:T(8,128)(2,1)} %all-gather.13.cloned.1.call-done, bf16[2048,560]{0,1:T(8,128)(2,1)} %copy-done.40, bf16[2048,560]{0,1:T(8,128)(2,1)} %copy-done.39), kind=kOutput, calls=%fused_computation.67 | convolution fusion | flops 7057326080 | bytes 14319616 | tf_op jit(solution)/shard_map/dot_general | solution.py:57
  446.3 76.4 %reduce-scatter.9.cloned.1.call-done = bf16[128,1536]{1,0:T(8,128)(2,1)} async-done(((bf16[2048,1536]{1,0:T(8,128)(2,1)}), bf16[128,1536]{1,0:T(8,128)(2,1)}) %reduce-scatter.9.cloned.1.call-update) | async-done | bytes 393232 | tf_op jit(solution)/shard_map/reduce_scatter | solution.py:150
  524.0 87.6 %reduce-scatter.7.cloned.1.call-done = bf16[128,1536]{1,0:T(8,128)(2,1)} async-done(((bf16[2048,1536]{1,0:T(8,128)(2,1)}), bf16[128,1536]{1,0:T(8,128)(2,1)}) %reduce-scatter.7.cloned.1.call-update) | async-done | bytes 393232 | tf_op jit(solution)/shard_map/reduce_scatter | solution.py:150
  621.1 5.6 while.59
  649.0 99.3 %all-reduce.5.cloned.1.call-done = bf16[16,2,64,512]{3,2,0,1:T(8,128)(2,1)} async-done(((bf16[16,2,64,512]{3,2,0,1:T(8,128)(2,1)}), bf16[16,2,64,512]{3,2,0,1:T(8,128)(2,1)}) %all-reduce.5.cloned.1.call-update) | async-done | bytes 2097168
  759.4 8.4 convolution_convert_fusion.5
  770.6 6.0 copy.144
  780.7 191.7 %all_to_all.10 = bf16[16,96,1680]{2,1,0:T(8,128)(2,1)} all-to-all(bf16[16,96,1680]{2,1,0:T(8,128)(2,1)S(1)} %pad_maximum_fusion.2), channel_id=1, replica_groups=mesh['replica'=2,'group'=16] {'group'}, dimensions={0} | all-to-all | bytes 10321920 | tf_op jit(solution)/shard_map/all_to_all | solution.py:271
  979.6 60.0 %all-reduce.2 = f32[16,320]{1,0:T(8,128)S(1)} all-reduce(f32[16,320]{1,0:T(8,128)S(1)} %concatenate.137), channel_id=6, replica_groups=mesh['replica'=2,'group'=16] {'group'}, use_global_device_ids=true, to_apply=%region_22.23.clone | all-reduce | flops 5120 | bytes 40960
  1040.2 53.9 %psum.7 = f32[1,320]{1,0:T(1,128)S(1)} all-reduce(f32[1,320]{1,0:T(1,128)S(1)} %constant_dynamic-slice_fusion), channel_id=1, replica_groups=mesh['replica'=2,'group'=16] {'replica'}, use_global_device_ids=true, to_apply=%region_23.24 | all-reduce | flops 320 | bytes 2560 | tf_op jit(solution)/shard_map/psum | solution.py:351
  1096.5 9.6 convert_add_fusion
  1106.1 12.4 %copy.146 = f32[16,96,1680]{1,2,0:T(8,128)} copy(f32[16,96,1680]{2,1,0:T(8,128)} %convert_add_fusion) | data formatting | bytes 20643840 | tf_op jit(solution)/shard_map/add | solution.py:274
  1120.0 10.2 fusion.91
  (295 shorter events, 149.7 us)
Async XLA Ops:
  7.2 75.8 %all-gather.7.cloned.1.call-start = ((), (), s32[]{:S(2)}) async-start(), calls=%async_computation.5 | async-start | bytes 6684672 | tf_op jit(solution)/shard_map/all_gather | solution.py:146
  9.1 117.9 %all-gather.9.cloned.1.call-start = ((), (), s32[]{:S(2)}) async-start(), calls=%async_computation.6 | async-start | bytes 2228224 | tf_op jit(solution)/shard_map/all_gather | solution.py:146
  81.7 9.8 copy-start.32
  88.2 93.1 %all-gather.11.cloned.1.call-start = ((), (), s32[]{:S(2)}) async-start(), calls=%async_computation.7 | async-start | bytes 5013504 | tf_op jit(solution)/shard_map/all_gather | solution.py:146
  88.9 263.4 %all-gather.13.cloned.1.call-start = ((), (), s32[]{:S(2)}) async-start(), calls=%async_computation.8 | async-start | bytes 6684672 | tf_op jit(solution)/shard_map/all_gather | solution.py:146
  135.5 45.8 %copy-start.15 = (bf16[2,64,1536]{2,1,0:T(8,128)(2,1)S(1)}, bf16[2,64,1536]{2,1,0:T(8,128)(2,1)}, u32[]{:S(2)}) copy-start(bf16[2,64,1536]{2,1,0:T(8,128)(2,1)} %param.23) | copy-start | bytes 1179652
  137.7 48.5 %copy-start.6 = (bf16[1024,2,128]{2,0,1:T(8,128)(2,1)}, bf16[1024,2,128]{2,0,1:T(8,128)(2,1)S(1)}, u32[]{:S(2)}) copy-start(bf16[1024,2,128]{2,0,1:T(8,128)(2,1)S(1)} %get-tuple-element.1130) | copy-start | bytes 1572868
  137.7 48.5 %copy-start.8 = (bf16[1024,2,128]{2,0,1:T(8,128)(2,1)}, bf16[1024,2,128]{2,0,1:T(8,128)(2,1)S(1)}, u32[]{:S(2)}) copy-start(bf16[1024,2,128]{2,0,1:T(8,128)(2,1)S(1)} %get-tuple-element.1131) | copy-start | bytes 1572868
  138.4 47.9 %copy-start.17 = (bf16[128,1536]{1,0:T(8,128)(2,1)}, bf16[128,1536]{1,0:T(8,128)(2,1)S(1)}, u32[]{:S(2)}) copy-start(bf16[128,1536]{1,0:T(8,128)(2,1)S(1)} %constant_dynamic-update-slice_fusion) | copy-start | bytes 1179652
  212.2 140.2 %all-to-all-start = ((bf16[16,96,1680]{2,1,0:T(8,128)(2,1)}), bf16[16,96,1680]{2,1,0:T(8,128)(2,1)}, u32[]{:S(2)}, u32[]{:S(2)}) async-start(bf16[16,96,1680]{2,1,0:T(8,128)(2,1)} %copy.128), calls=%async_computation | async-start | bytes 11010048 | tf_op jit(solution)/shard_map/all_to_all | solution.py:205
  217.1 180.1 %all-gather.15.cloned.1.call-start = ((), (), s32[]{:S(2)}) async-start(), calls=%async_computation.10 | async-start | bytes 6684672 | tf_op jit(solution)/shard_map/all_gather | solution.py:146
  218.2 304.5 %reduce-scatter.9.cloned.1.call-start = ((), (), s32[]{:S(2)}) async-start(), calls=%async_computation.11 | async-start | bytes 6684672 | tf_op jit(solution)/shard_map/reduce_scatter | solution.py:150
  424.3 187.3 %reduce-scatter.7.cloned.1.call-start = ((), (), s32[]{:S(2)}) async-start(), calls=%async_computation.9 | async-start | bytes 6684672 | tf_op jit(solution)/shard_map/reduce_scatter | solution.py:150
  434.2 314.1 %all-reduce.5.cloned.1.call-start = ((), (), s32[]{:S(2)}) async-start(), calls=%async_computation.13 | async-start | bytes 4194304
  434.3 88.5 %copy-start.12 = (f32[128,1536]{1,0:T(8,128)S(1)}, f32[128,1536]{1,0:T(8,128)}, u32[]{:S(2)}) copy-start(f32[128,1536]{1,0:T(8,128)} %copy-done.11) | copy-start | bytes 2359300
  641.8 476.7 %reduce-scatter.11.cloned.1.call-start = ((), (), s32[]{:S(2)}) async-start(), calls=%async_computation.12 | async-start | bytes 11698176 | tf_op jit(solution)/shard_map/reduce_scatter | solution.py:150
  648.4 103.7 %copy-start.14 = (bf16[128,1536]{1,0:T(8,128)(2,1)S(1)}, bf16[128,1536]{1,0:T(8,128)(2,1)}, u32[]{:S(2)}) copy-start(bf16[128,1536]{1,0:T(8,128)(2,1)} %copy-done.13) | copy-start | bytes 1179652
  780.6 193.3 %copy-start.38 = (f32[128]{0:T(128)S(1)}, f32[128]{0:T(128)}, u32[]{:S(2)}) copy-start(f32[128]{0:T(128)} %copy-done.37) | copy-start | bytes 1540
  780.6 193.3 %copy-start.16 = (bf16[2,64,1536]{2,1,0:T(8,128)(2,1)S(1)}, bf16[2,64,1536]{2,1,0:T(8,128)(2,1)}, u32[]{:S(2)}) copy-start(bf16[2,64,1536]{2,1,0:T(8,128)(2,1)} %param.23) | copy-start | bytes 1179652
  780.6 193.3 %copy-start.27 = (bf16[2,64,256]{2,1,0:T(8,128)(2,1)S(1)}, bf16[2,64,256]{2,1,0:T(8,128)(2,1)}, u32[]{:S(2)}) copy-start(bf16[2,64,256]{2,1,0:T(8,128)(2,1)} %copy-done.26) | copy-start | bytes 196612
  780.6 193.3 %copy-start.29 = (bf16[128,256]{1,0:T(8,128)(2,1)S(1)}, bf16[128,256]{1,0:T(8,128)(2,1)}, u32[]{:S(2)}) copy-start(bf16[128,256]{1,0:T(8,128)(2,1)} %copy-done.28) | copy-start | bytes 196612
  780.7 193.3 %copy-start.35 = (f32[1536]{0:T(1024)S(1)}, f32[1536]{0:T(1024)}, u32[]{:S(2)}) copy-start(f32[1536]{0:T(1024)} %copy-done.34) | copy-start | bytes 18436
  972.4 124.1 %collective-permute-start.1 = (bf16[16,96,1680]{2,1,0:T(8,128)(2,1)}, bf16[16,96,1680]{2,1,0:T(8,128)(2,1)}, u32[]{:S(2)}, u32[]{:S(2)}) collective-permute-start(bf16[16,96,1680]{2,1,0:T(8,128)(2,1)} %all_to_all.10), channel_id=1, source_target_pairs={{0,16},{16,0},{1,17},{17,1},{2,18},{18,2},{3,19},{19,3},{4,20},{20... | collective-permute-start | bytes 15482888 | tf_op jit(solution)/shard_map/ppermute | solution.py:274
  1118.5 28.4 %collective-permute-start = (bf16[96,3584]{1,0:T(8,128)(2,1)}, bf16[96,3584]{1,0:T(8,128)(2,1)S(1)}, u32[]{:S(2)}, u32[]{:S(2)}) collective-permute-start(bf16[96,3584]{1,0:T(8,128)(2,1)} %reduce-scatter.11.cloned.1.call-done), channel_id=1, source_target_pairs={{0,16},{16,0},{1,17},{17,1},{2,18},{18,2},{3,19},{19,3},{4,20},{20... | collective-permute-start | bytes 2064392 | tf_op jit(solution)/shard_map/ppermute | solution.py:338
  (31 other events, 101.7 us)
Sparse Core Ops, SparseCore 0:
  10.9 65.1 all-gather.6
  88.3 38.5 all-gather.8
  129.2 52.0 all-gather.10
  186.4 98.6 all-gather.12
  287.8 109.4 all-gather.14
  424.4 98.3 reduce-scatter.8
  527.2 84.3 reduce-scatter.6
  641.9 106.3 all-reduce.4
  759.5 200.4 reduce-scatter.10

commit v2 on v1

--- a/solution.py
+++ b/solution.py
@@ -1,8 +1,15 @@
+import functools
+
 import jax
 import jax.numpy as jnp
 from jax import lax
+from jax.experimental import pallas as pl
+from jax.experimental.pallas import tpu as pltpu
 from jax.sharding import PartitionSpec as P
 
+MESH = pl.DeviceIdType.MESH
+NZ = 4
+MAIN = 512
 HEADS = 12
 KV_HEADS = 2
 HEAD_DIM = 128
@@ -142,12 +149,272 @@
     return lax.fori_loop(0, block_total(length, rank_end, key_step), visit, initial)
 
 
-def gather(x):
-    return lax.all_gather(x, "group", axis=0, tiled=True)
-
-
-def scatter_sum(x):
-    return lax.psum_scatter(x, "group", scatter_dimension=0, tiled=True)
+def place():
+    g = lax.axis_index("group")
+    r = lax.axis_index("replica")
+    return r, g // 4, lax.rem(g // 2, 2), lax.rem(g, 2)
+
+def idx(z, x, c):
+    return (z * 2 + x) * 2 + c
+
+def greet(r, z, x, c, with_y=False):
+    bar = pltpu.get_barrier_semaphore()
+    def hail(dev):
+        pl.semaphore_signal(bar, inc=1, device_id=dev, device_id_type=MESH)
+    hail((r, idx(z, 1 - x, c)))
+    hail((r, idx(z, x, 1 - c)))
+    if with_y:
+        hail((1 - r, idx(z, x, c)))
+    @pl.when(z > 0)
+    def _():
+        hail((r, idx(z - 1, x, c)))
+    @pl.when(z < NZ - 1)
+    def _():
+        hail((r, idx(z + 1, x, c)))
+    ends = jnp.where((z > 0) & (z < NZ - 1), 1, 0)
+    pl.semaphore_wait(bar, (4 if with_y else 3) + ends)
+
+def when(cond, fn):
+    pl.when(cond)(fn)
+
+class Gather:
+    def __init__(self, at, src, out, send, recv, local):
+        self.r, self.z, self.x, self.c = at
+        self.src, self.out, self.send, self.recv, self.local = src, out, send, recv, local
+    def put(self, src, b, k, dev):
+        pltpu.make_async_remote_copy(src, self.out.at[b], self.send.at[k], self.recv.at[b], device_id=dev, device_id_type=MESH).start()
+    def sent(self, k):
+        b = 0
+        pltpu.make_async_remote_copy(self.out.at[b], self.out.at[b], self.send.at[k], self.recv.at[b], device_id=(self.r, 0), device_id_type=MESH).wait_send()
+    def got(self, b):
+        pltpu.make_async_remote_copy(self.out.at[b], self.out.at[b], self.send.at[0], self.recv.at[b], device_id=(self.r, 0), device_id_type=MESH).wait_recv()
+    def zdev(self, s): return (self.r, idx(self.z + s, self.x, self.c))
+    def xdev(self): return (self.r, idx(self.z, 1 - self.x, self.c))
+    def cdev(self): return (self.r, idx(self.z, self.x, 1 - self.c))
+    def begin(self):
+        z, x, c = self.z, self.x, self.c
+        me = idx(z, x, c)
+        for s in (1, -1):
+            when(self.inside(z + s), lambda s=s: self.put(self.src, me, 0 if s == 1 else 3, self.zdev(s)))
+        self.put(self.src, me, 6 + z, self.xdev())
+        self.put(self.src, me, 10 + 2 * z + x, self.cdev())
+        pltpu.make_async_copy(self.src, self.out.at[me], self.local).start()
+    def inside(self, z): return (z >= 0) & (z < NZ)
+    def step_z(self, d):
+        z, x, c = self.z, self.x, self.c
+        for s in (-1, 1):
+            zz = z + s * d
+            def arrive(s=s, zz=zz):
+                b = idx(zz, x, c)
+                self.got(b)
+                if d < NZ - 1:
+                    when(self.inside(z - s), lambda: self.put(self.out.at[b], b, (0 if s == -1 else 3) + d, self.zdev(-s)))
+                self.put(self.out.at[b], b, 6 + zz, self.xdev())
+                self.put(self.out.at[b], b, 10 + 2 * zz + x, self.cdev())
+            when(self.inside(zz), arrive)
+    def step_x(self, d):
+        z, x, c = self.z, self.x, self.c
+        for s in ((-1, 1) if d else (1,)):
+            zz = z + s * d
+            def arrive(zz=zz):
+                b = idx(zz, 1 - x, c)
+                self.got(b)
+                self.put(self.out.at[b], b, 10 + 2 * zz + 1 - x, self.cdev())
+            when(self.inside(zz), arrive)
+    def step_c(self, d):
+        z, x, c = self.z, self.x, self.c
+        for s in ((-1, 1) if d else (1,)):
+            zz = z + s * d
+            def arrive(zz=zz):
+                self.got(idx(zz, x, 1 - c))
+                self.got(idx(zz, 1 - x, 1 - c))
+            when(self.inside(zz), arrive)
+    def end(self):
+        z = self.z
+        for d in range(NZ - 1):
+            when((z - d >= 0) & (z < NZ - 1), lambda d=d: self.sent(d))
+            when((z + d < NZ) & (z > 0), lambda d=d: self.sent(3 + d))
+        for k in range(6, 18):
+            self.sent(k)
+        pltpu.make_async_copy(self.src, self.out.at[0], self.local).wait()
+
+def gather_kernel(n, with_side, *refs):
+    srcs, outs = refs[:n], refs[n:2*n]
+    send, recv, local = refs[2*n:]
+    at = place()
+    greet(*at)
+    eng = [Gather(at, srcs[i], outs[i], send.at[i], recv.at[i], local.at[i]) for i in range(n)]
+    for e in eng: e.begin()
+    for d in range(1, NZ):
+        for e in eng: e.step_z(d)
+        for e in eng: e.step_x(d - 1)
+    for e in eng: e.step_x(NZ - 1)
+    for d in range(NZ):
+        for e in eng: e.step_c(d)
+    for e in eng: e.end()
+
+def gather(arrays, cid, chunks=None):
+    n = len(arrays)
+    return pl.pallas_call(
+        functools.partial(gather_kernel, n, False),
+        out_shape=[jax.ShapeDtypeStruct((16,) + a.shape, a.dtype) for a in arrays],
+        in_specs=[pl.BlockSpec(memory_space=pl.ANY)] * n,
+        out_specs=[pl.BlockSpec(memory_space=pl.ANY)] * n,
+        scratch_shapes=[pltpu.SemaphoreType.DMA((n, 18)), pltpu.SemaphoreType.DMA((n, 16)), pltpu.SemaphoreType.DMA((n,))],
+        compiler_params=pltpu.CompilerParams(collective_id=cid, has_side_effects=True),
+    )(*arrays)
+
+class Scatter:
+    def __init__(self, at, part, rc, rx, rz, send, rcs, rxs, rzs):
+        self.r, self.z, self.x, self.c = at
+        self.part, self.rc, self.rx, self.rz = part, rc, rx, rz
+        self.send, self.rcs, self.rxs, self.rzs = send, rcs, rxs, rzs
+    def inside(self, z): return (z >= 0) & (z < NZ)
+    def copy(self, src, dst, k, rs, dev):
+        return pltpu.make_async_remote_copy(src, dst, self.send.at[k], rs, device_id=dev, device_id_type=MESH)
+    def over(self, d):
+        return [(s, self.z + s * d) for s in ((-1, 1) if d else (1,))]
+    def begin(self, far_first=True):
+        z, x, c = self.z, self.x, self.c
+        dev = (self.r, idx(z, x, 1 - c))
+        for xx in (1 - x, x):
+            for d in range(NZ - 1, -1, -1):
+                for s, zz in self.over(d):
+                    k = 2 * zz + xx
+                    when(self.inside(zz), lambda zz=zz, k=k, xx=xx: self.copy(self.part.at[idx(zz, xx, 1 - c)], self.rc.at[k], k, self.rcs.at[k], dev).start())
+    def step_x(self, d):
+        z, x, c = self.z, self.x, self.c
+        dev = (self.r, idx(z, 1 - x, c))
+        for s, zz in self.over(d):
+            def go(zz=zz):
+                k = 2 * zz + 1 - x
+                b = idx(zz, 1 - x, c)
+                self.copy(self.rc.at[k], self.rc.at[k], 0, self.rcs.at[k], dev).wait_recv()
+                self.part[b] = (self.part[b].astype(F32) + self.rc[k].astype(F32)).astype(BF)
+                self.copy(self.part.at[b], self.rx.at[zz], 8 + zz, self.rxs.at[zz], dev).start()
+            when(self.inside(zz), go)
+    def step_z(self, d):
+        z, x, c = self.z, self.x, self.c
+        for s, zz in self.over(d):
+            def go(zz=zz, s=s):
+                k = 2 * zz + x
+                b = idx(zz, x, c)
+                self.copy(self.rc.at[k], self.rc.at[k], 0, self.rcs.at[k], (self.r, 0)).wait_recv()
+                self.copy(self.rx.at[zz], self.rx.at[zz], 0, self.rxs.at[zz], (self.r, 0)).wait_recv()
+                both = self.part[b].astype(F32) + self.rc[k].astype(F32) + self.rx[zz].astype(F32)
+                dev = (self.r, idx(z + s, x, c))
+                slot = jnp.where(zz == z + s, NZ, zz) if s == -1 else zz
+                self.part[b] = both.astype(BF)
+                def more():
+                    self.copy(self.rz.at[zz], self.rz.at[zz], 0, self.rzs.at[zz], dev).wait_recv()
+                    self.part[b] = (self.part[b].astype(F32) + self.rz[zz].astype(F32)).astype(BF)
+                when(self.inside(z - s), more)
+                self.copy(self.part.at[b], self.rz.at[slot], 12 + zz, self.rzs.at[slot], dev).start()
+            when(self.inside(zz), go)
+    def finish(self, out):
+        z, x, c = self.z, self.x, self.c
+        k = 2 * z + x
+        b = idx(z, x, c)
+        self.copy(self.rc.at[k], self.rc.at[k], 0, self.rcs.at[k], (self.r, 0)).wait_recv()
+        self.copy(self.rx.at[z], self.rx.at[z], 0, self.rxs.at[z], (self.r, 0)).wait_recv()
+        out[...] = self.part[b].astype(F32) + self.rc[k].astype(F32) + self.rx[z].astype(F32)
+        def lo():
+            self.copy(self.rz.at[z], self.rz.at[z], 0, self.rzs.at[z], (self.r, 0)).wait_recv()
+            out[...] += self.rz[z].astype(F32)
+        when(z > 0, lo)
+        def hi():
+            self.copy(self.rz.at[NZ], self.rz.at[NZ], 0, self.rzs.at[NZ], (self.r, 0)).wait_recv()
+            out[...] += self.rz[NZ].astype(F32)
+        when(z < NZ - 1, hi)
+        for k in range(8):
+            self.copy(self.part.at[0], self.part.at[0], k, self.rcs.at[0], (self.r, 0)).wait_send()
+        for k in range(8, 12):
+            self.copy(self.part.at[0], self.part.at[0], k, self.rcs.at[0], (self.r, 0)).wait_send()
+        for zz in range(NZ):
+            when(z != zz, lambda zz=zz: self.copy(self.part.at[0], self.part.at[0], 12 + zz, self.rcs.at[0], (self.r, 0)).wait_send())
+
+def scatter_steps(engines):
+    for e in engines: e.begin()
+    order = [("x", 3), ("x", 2), ("z", 3), ("x", 1), ("z", 2), ("x", 0), ("z", 1)]
+    for kind, d in order:
+        for e in engines:
+            (e.step_x if kind == "x" else e.step_z)(d)
+
+def scatter_kernel(n, pair, *refs):
+    ps, os = refs[:n], refs[n:2*n]
+    s = refs[2*n:]
+    vm = [s[4*i:4*i+4] for i in range(n)]
+    ysb = s[4*n:4*n+2*n] if pair else None
+    send, rcs, rxs, rzs, lsem, ysem = s[4*n+(2*n if pair else 0):]
+    at = place()
+    for i in range(n):
+        pltpu.make_async_copy(ps[i], vm[i][0], lsem.at[i]).start()
+    greet(*at, with_y=pair)
+    for i in range(n):
+        pltpu.make_async_copy(ps[i], vm[i][0], lsem.at[i]).wait()
+    engines = [Scatter(at, *vm[i], send.at[i], rcs.at[i], rxs.at[i], rzs.at[i]) for i in range(n)]
+    scatter_steps(engines)
+    r, z, x, c = at
+    for i, e in enumerate(engines):
+        e.finish(os[i])
+        if pair:
+            ysb[2*i][...] = os[i][...].astype(BF)
+            pltpu.make_async_remote_copy(ysb[2*i], ysb[2*i+1], ysem.at[2*i], ysem.at[2*i+1], device_id=(1 - r, idx(z, x, c)), device_id_type=MESH).start()
+    if pair:
+        for i, e in enumerate(engines):
+            pltpu.make_async_remote_copy(ysb[2*i], ysb[2*i+1], ysem.at[2*i], ysem.at[2*i+1], device_id=(1 - r, idx(z, x, c)), device_id_type=MESH).wait()
+            os[i][...] = ysb[2*i][...].astype(F32) + ysb[2*i+1][...].astype(F32)
+
+def scatter(parts, cid, pair=False):
+    n = len(parts)
+    scratch = []
+    for p in parts:
+        blk = p.shape[1:]
+        scratch += [pltpu.VMEM((k,) + blk, BF) for k in (16, 8, 4, 5)]
+    if pair:
+        for p in parts:
+            scratch += [pltpu.VMEM(p.shape[1:], BF)] * 2
+    dma = pltpu.SemaphoreType.DMA
+    return pl.pallas_call(
+        functools.partial(scatter_kernel, n, pair),
+        out_shape=[jax.ShapeDtypeStruct(p.shape[1:], F32) for p in parts],
+        in_specs=[pl.BlockSpec(memory_space=pl.ANY)] * n,
+        out_specs=[pl.BlockSpec(memory_space=pltpu.VMEM)] * n,
+        scratch_shapes=scratch + [dma((n, 16)), dma((n, 8)), dma((n, 4)), dma((n, 5)), dma((n,)), dma((2 * n,))],
+        compiler_params=pltpu.CompilerParams(collective_id=cid, has_side_effects=True, vmem_limit_bytes=60 * 2**20),
+    )(*parts)
+
+
+def gather_all(arrays, cid, fast):
+    if fast:
+        return gather(arrays, cid)
+    return [lax.all_gather(a, "group", axis=0) for a in arrays]
+
+
+def swap(x):
+    return lax.ppermute(x, "replica", [(0, 1), (1, 0)])
+
+
+def scatter_all(parts, cid, fast, pair=False):
+    if fast:
+        return scatter(parts, cid, pair)
+    sums = [
+        lax.psum_scatter(p, "group", scatter_dimension=0, tiled=True)[0].astype(F32) for p in parts
+    ]
+    if pair:
+        low = [p.astype(BF) for p in sums]
+        sums = [p.astype(F32) + swap(p).astype(F32) for p in low]
+    return sums
+
+
+def other_half(x, dim, rank):
+    half = x.shape[dim] // 2
+    return lax.dynamic_slice_in_dim(x, (1 - rank) * half, half, dim)
+
+
+def own_half(x, dim, rank):
+    half = x.shape[dim] // 2
+    return lax.dynamic_slice_in_dim(x, rank * half, half, dim)
 
 
 def shards(
@@ -189,25 +456,55 @@
     rank_end = (group_rank + 1) * block_len
     row_pos = jnp.tile(positions, repeat)
 
+    fast = group_count == 16
+    replica_rank = lax.axis_index("replica")
     pieces = (gain_attn, b_query, b_key, b_value, gain_mlp)
     sizes = [p.shape[0] for p in pieces]
-    small = gather(jnp.concatenate(pieces)[None])
     offsets = [sum(sizes[:i]) for i in range(len(sizes) + 1)]
+    small = jnp.zeros((16 * 128,), BF).at[: offsets[-1]].set(jnp.concatenate(pieces))
+    qkv_w, small = gather_all(
+        [jnp.concatenate((w_query, w_key, w_value), axis=1), small.reshape(16, 128)], 1, fast
+    )
+    qkv_w = qkv_w.reshape(model_width, model_width + 2 * kv_width)
+    small = small.reshape(group_count, 16 * 128)
     gain_one, query_b, key_b, value_b, gain_two = [
         small[:, offsets[i] : offsets[i + 1]].reshape(-1).astype(F32) for i in range(len(sizes))
     ]
-    qkv_w = gather(jnp.concatenate((w_query, w_key, w_value), axis=1))
-    out_w = gather(w_out)
     qkv_b = jnp.concatenate((query_b, key_b, value_b))
 
-    stacked = jnp.stack((w_gate, w_up, w_down)).reshape(3, own_rows, group_count, share)
-    stacked = jnp.transpose(stacked, (2, 1, 0, 3)).reshape(group_count, own_rows, 3 * share)
-    columns = lax.all_to_all(stacked, "group", 0, 0, tiled=True).reshape(model_width, 3 * share)
-    gate_up_w = columns[:, : 2 * share]
-    down_w = columns[:, 2 * share :]
+    main = (hidden_units // 128 // group_count) * 128
+    spare = hidden_units // group_count - main
+    mains = [
+        w[:, : main * group_count].reshape(own_rows, group_count, main) for w in (w_gate, w_up, w_down)
+    ]
+    spares = [
+        w[:, main * group_count :].reshape(own_rows, group_count, spare)
+        for w in (w_gate, w_up, w_down)
+    ]
+    gap = jnp.zeros((own_rows, group_count, 128 - 2 * spare), BF)
+    gap_down = jnp.zeros((own_rows, group_count, 128 - spare), BF)
+    blocks = jnp.concatenate(mains + [spares[0], spares[1], gap, spares[2], gap_down], axis=2)
+    blocks = jnp.transpose(own_half(blocks, 0, replica_rank), (1, 0, 2))
+    own_part = lax.all_to_all(blocks, "group", 0, 0, tiled=True)
+    other_part = swap(own_part)
+    first = jnp.where(replica_rank == 0, own_part, other_part)
+    second = jnp.where(replica_rank == 0, other_part, own_part)
+    columns = jnp.concatenate((first, second), axis=1).reshape(model_width, 3 * main + 256)
+    rest = 3 * main
+    gate_up_w = jnp.concatenate(
+        (
+            columns[:, :main],
+            columns[:, rest : rest + spare],
+            columns[:, main : 2 * main],
+            columns[:, rest + spare : rest + 2 * spare],
+        ),
+        axis=1,
+    )
+    down_w = jnp.concatenate(
+        (columns[:, 2 * main : rest], columns[:, rest + 128 : rest + 128 + spare]), axis=1
+    )
 
     grad_final = cotangent.reshape(tokens, model_width).astype(F32) * valid_rows
-    grad_all = gather(grad_final.astype(BF))
 
     inputs = hidden_in.reshape(tokens, model_width).astype(F32)
     normed_full, factor_one = normalize(inputs, gain_one)
@@ -226,10 +523,13 @@
     value_low = qkv[:, model_width + kv_width :].astype(BF)
     pair = jnp.concatenate(
         (key_rot.reshape(tokens, kv_width), value_low), axis=1
-    ).reshape(1, slot_count, block_len, 2 * kv_width)
-    pair_all = jnp.transpose(gather(pair), (1, 0, 2, 3)).reshape(
-        slot_count, slot_span, 2, kv_heads, head_dim
-    )
+    )
+    pair_all, grad_all, out_w = gather_all([pair, grad_final.astype(BF), w_out], 2, fast)
+    out_w = out_w.reshape(model_width, model_width)
+    grad_all = grad_all.reshape(group_count * tokens, model_width)
+    pair_all = jnp.transpose(
+        pair_all.reshape(group_count, slot_count, block_len, 2 * kv_width), (1, 0, 2, 3)
+    ).reshape(slot_count, slot_span, 2, kv_heads, head_dim)
     key_all = pair_all[:, :, 0]
     value_all = pair_all[:, :, 1]
     query_groups = []
@@ -249,7 +549,8 @@
     attended_low = jnp.concatenate(attended_rows, axis=0).astype(BF)
     residual_mid = inputs + matmul(attended_low, out_w)
     normed_two_full, factor_two = normalize(residual_mid, gain_two)
-    normed_all = gather(normed_two_full.astype(BF))
+    (normed_all,) = gather_all([normed_two_full.astype(BF)], 3, fast)
+    normed_all = normed_all.reshape(group_count * tokens, model_width)
 
     pre = matmul(normed_all, gate_up_w)
     gate_pre = pre[:, :share]
@@ -263,17 +564,45 @@
     ).astype(BF)
     grad_up = (grad_hidden * silu_gate).astype(BF)
     gate_up_grad = jnp.concatenate((grad_gate, grad_up), axis=1)
-    grad_normed_two = scatter_sum(matmul_nt(gate_up_grad, gate_up_w).astype(BF)).astype(F32)
-    mlp_out = scatter_sum(matmul_nt(hidden, down_w).astype(BF)).astype(F32)
-    down_term = matmul_tn(grad_all, hidden)
-    gate_up_term = matmul_tn(normed_all, gate_up_grad)
-    terms = jnp.concatenate((gate_up_term, down_term), axis=1).astype(BF)
-    back = lax.all_to_all(
-        terms.reshape(group_count, own_rows, 3 * share), "group", 0, 0, tiled=True
-    )
-    summed = back.astype(F32) + lax.ppermute(back, "replica", [(0, 1), (1, 0)]).astype(F32)
-    summed = jnp.transpose(summed.reshape(group_count, own_rows, 3, share), (2, 1, 0, 3))
-    gate_sum, up_sum, down_sum = summed.reshape(3, own_rows, hidden_units)
+    sums = [
+        p.astype(BF).reshape(group_count, tokens, model_width)
+        for p in (matmul_nt(gate_up_grad, gate_up_w), matmul_nt(hidden, down_w))
+    ]
+    grad_normed_two, mlp_out = scatter_all(sums, 4, fast)
+    down_term = matmul_tn(grad_all, hidden).astype(BF)
+    gate_up_term = matmul_tn(normed_all, gate_up_grad).astype(BF)
+    zeros = jnp.zeros((model_width, 128), BF)
+    terms = jnp.concatenate(
+        (
+            gate_up_term[:, :main],
+            gate_up_term[:, share : share + main],
+            down_term[:, :main],
+            gate_up_term[:, main:share],
+            gate_up_term[:, share + main :],
+            zeros[:, : 128 - 2 * spare],
+            down_term[:, main:],
+            zeros[:, : 128 - spare],
+        ),
+        axis=1,
+    ).reshape(group_count, own_rows, 3 * main + 256)
+    half_sum = own_half(terms, 1, replica_rank).astype(F32) + swap(
+        other_half(terms, 1, replica_rank)
+    ).astype(F32)
+    half_back = lax.all_to_all(half_sum.astype(BF), "group", 0, 0, tiled=True)
+    half_other = swap(half_back)
+    first = jnp.where(replica_rank == 0, half_back, half_other)
+    second = jnp.where(replica_rank == 0, half_other, half_back)
+    back = jnp.transpose(jnp.concatenate((first, second), axis=1), (1, 0, 2))
+    gate_sum, up_sum, down_sum = [
+        jnp.concatenate(
+            (
+                back[:, :, i * main : (i + 1) * main].reshape(own_rows, group_count * main),
+                back[:, :, at : at + spare].reshape(own_rows, group_count * spare),
+            ),
+            axis=1,
+        ).astype(F32)
+        for i, at in ((0, rest), (1, rest + spare), (2, rest + 128))
+    ]
 
     final_rows = residual_mid + mlp_out
     layer_out = (final_rows * valid_rows).reshape(slot_count, block_len, model_width).astype(BF)
@@ -318,7 +647,10 @@
         )
     pair_grads = jnp.stack(grad_pairs).reshape(slot_count, group_count, block_len, 2 * kv_width)
     pair_grads = jnp.transpose(pair_grads, (1, 0, 2, 3)).astype(BF)
-    pair_sum = scatter_sum(pair_grads).reshape(slot_count, block_len, 2 * kv_width).astype(F32)
+    (pair_sum,) = scatter_all(
+        [pair_grads.reshape(group_count, tokens, 2 * kv_width)], 5, fast
+    )
+    pair_sum = pair_sum.reshape(slot_count, block_len, 2 * kv_width)
     grad_query_pre = jnp.concatenate(grad_query_rows, axis=0).astype(BF)
     key_sum = pair_sum[..., :kv_width].reshape(slot_count, block_len, kv_heads, head_dim)
     grad_key_pre = (
@@ -332,12 +664,6 @@
     qkv_term = matmul_tn(normed, grad_qkv)
     qkv_bias = jnp.sum(grad_qkv.astype(F32), axis=0)
 
-    weight_share = scatter_sum(
-        jnp.concatenate((qkv_term, out_term), axis=1).astype(BF)
-    )
-    weight_sum = weight_share.astype(F32) + lax.ppermute(
-        weight_share, "replica", [(0, 1), (1, 0)]
-    ).astype(F32)
     vectors = jnp.concatenate(
         [
             grad_gain_one.reshape(group_count, -1),
@@ -348,13 +674,25 @@
         ],
         axis=1,
     )
-    vector_sum = lax.psum(scatter_sum(vectors), "replica").reshape(-1)
+    vectors = jnp.concatenate(
+        (vectors, jnp.zeros((group_count, 16 * 128 - offsets[-1]), F32)), axis=1
+    ).reshape(group_count, 16, 128)
+    weight_sum, out_sum, vector_sum = scatter_all(
+        [
+            p.astype(BF).reshape(group_count, p.shape[0] // group_count, -1)
+            for p in (qkv_term, out_term)
+        ]
+        + [vectors.astype(BF)],
+        6,
+        fast,
+        pair=True,
+    )
+    vector_sum = vector_sum.reshape(-1)
     gain_one_sum, query_bias_sum, key_bias_sum, value_bias_sum, gain_two_sum = [
         vector_sum[offsets[i] : offsets[i + 1]] for i in range(len(sizes))
     ]
     ends = (0, model_width, model_width + kv_width, model_width + 2 * kv_width)
     query_sum, key_sum_w, value_sum_w = [weight_sum[:, ends[i] : ends[i + 1]] for i in range(3)]
-    out_sum = weight_sum[:, ends[3] :]
     return (
         layer_out,
         grad_input,

time: 1160 us -> 712 us (0.61)
  waiting for transfers between devices: 507 us -> 1.99 us
  Pallas kernels: 0 us -> 431 us
  blocking collectives: 370 us -> 0 us
  starting transfers between devices: 8.65 us -> 22.8 us
  between operations: 17.1 us -> 3.5 us
    pallas_call x0 -> x6, Pallas kernels: none -> 431 us  [the longest x3 222 us: gather(): pl.pallas_call(functools.partial(gather_kernel, n, False), out_shape=[jax...]
    all_to_all x1 -> x0, blocking collectives: 192 us -> none  [shards(): lax.all_to_all(terms.reshape(group_count, own_rows, 3 * share), 'group',...]
    reduce_scatter x3 -> x0, waiting for transfers between devices: 164 us -> none  [scatter_sum(): return lax.psum_scatter(x, 'group', scatter_dimension=0, tiled=True)]
    all_to_all x1 -> x2, waiting for transfers between devices: 134 us -> 0.01 us  [the longest x1 0.01 us: shards(): own_part = lax.all_to_all(blocks, 'group', 0, 0, tiled=True)]
    unnamed x2 -> x0, blocking collectives: 124 us -> none
    all_gather x5 -> x0, waiting for transfers between devices: 109 us -> none  [gather(): return lax.all_gather(x, 'group', axis=0, tiled=True)]
    unnamed x10 -> x0, waiting for transfers between devices: 100 us -> none
    psum x1 -> x0, blocking collectives: 53.9 us -> none  [shards(): vector_sum = lax.psum(scatter_sum(vectors), 'replica').reshape(-1)]
  transfers between devices with their start and end apart: 12 -> 5, of which waited for: 7 -> 1; matrix products, arithmetic and copies ran while one was open for 15% -> 14% of each run, Pallas kernels for 0% -> 61%
where the time goes in v2:
time: 712 us; the launch traced here: 703 us
  Pallas kernels  431 us (61%)
  local copies, waits for them, and re-layouts  108 us (15%)
  matrix products  94.8 us (13%)
  other arithmetic  40.2 us (6%)
  starting transfers between devices  22.8 us (3%)
    pallas_call x3, Pallas kernels, gather(): pl.pallas_call(functools.partial(gather_kernel, n, False), out_shape=[jax...  222 us
    pallas_call x3, Pallas kernels, scatter(): pl.pallas_call(functools.partial(scatter_kernel, n, pair), out_shape=[jax...  209 us
    dot_general x4, matrix products, matmul(): return jnp.dot(a, b, preferred_element_type=F32)  30.7 us
    dot_general x4, matrix products, matmul_nt(): lax.dot_general(a, b, (((1,), (1,)), ((), ())), preferred_element_type=F32)  28.8 us
    unnamed x120, local copies, waits for them, and re-layouts  23.8 us
    dot_general x4, matrix products, matmul_tn(): lax.dot_general(a, b, (((0,), (0,)), ((), ())), preferred_element_type=F32)  23.3 us
  transfers between devices with their start and end apart: 5, of which 1 were waited for; matrix products, arithmetic and copies ran while one was open for 14% of the time, Pallas kernels for 61%

profile of v2, /device:TPU:0, one launch (start us, length us, event | category | flops | bytes accessed | tf_op | source)
XLA Modules:
  0.0 703.2 jit_solution(17765354976627997782)
XLA Ops:
  16.8 9.0 %concatenate.131 = bf16[96,16,1792]{2,1,0:T(8,128)(2,1)} concatenate(bf16[96,16,512]{2,1,0:T(8,128)(2,1)} %bitcast.328, bf16[96,16,512]{2,1,0:T(8,128)(2,1)} %bitcast.329, bf16[96,16,512]{2,1,0:T(8,128)(2,1)S(1)} %bitcast.327, bf16[96,16,48]{2,1,0:T(8,128)(2,1)S(1)} %copy.146, bf16[96,16,48]{2,1,0:T(8,128)(2,1)S(1)} %copy.147, bf16[96,16,32]{2,1,0:T(8,128)(2,1)S(1)} %broadcast_in_dim.52, ...), dimensions={2} | concatenate | bytes 11010048 | tf_op jit(solution)/shard_map/concatenate | solution.py:486
  30.2 7.5 %all-to-all-start = ((bf16[16,48,1792]{2,1,0:T(8,128)(2,1)}), bf16[16,48,1792]{2,1,0:T(8,128)(2,1)}, u32[]{:S(2)}, u32[]{:S(2)}) async-start(bf16[16,48,1792]{2,1,0:T(8,128)(2,1)} %copy.149), calls=%async_computation | async-start | bytes 5505024 | tf_op jit(solution)/shard_map/all_to_all | solution.py:488
  39.3 101.0 %shard_map.254 = (bf16[16,96,2048]{2,1,0:T(8,128)(2,1)}, bf16[16,16,128]{2,1,0:T(8,128)(2,1)}) custom-call(bf16[96,2048]{1,0:T(8,128)(2,1)} %pad_maximum_fusion.8.refs_0_, bf16[16,128]{1,0:T(8,128)(2,1)} %pad_bitcast_fusion.refs_1_), custom_call_target="tpu_custom_call" | custom-call | tf_op jit(solution)/shard_map/pallas_call | solution.py:258
  142.2 3.9 convolution_add_fusion.5
  151.3 76.1 %shard_map.255 = (bf16[16,128,512]{2,1,0:T(8,128)(2,1)}, bf16[16,128,1536]{2,1,0:T(8,128)(2,1)}, bf16[16,96,1536]{2,1,0:T(8,128)(2,1)}) custom-call(bf16[128,512]{1,0:T(8,128)(2,1)} %pad_maximum_fusion.9.refs_0_, bf16[128,1536]{1,0:T(8,128)(2,1)} %fusion.47.refs_1_, bf16[96,1536]{1,0:T(8,128)(2,1)} %refs_2_.1), custom_call_target="tpu_custom_call" | custom-call | tf_op jit(solution)/shard_map/pallas_call | solution.py:258
  256.3 44.6 %shard_map.256 = bf16[16,128,1536]{2,1,0:T(8,128)(2,1)} custom-call(bf16[128,1536]{1,0:T(8,128)(2,1)} %multiply_convert_fusion.4.refs_0_), custom_call_target="tpu_custom_call" | custom-call | tf_op jit(solution)/shard_map/pallas_call | solution.py:258
  309.7 7.5 %concatenate.134 = bf16[1536,1120]{1,0:T(8,128)(2,1)} concatenate(bf16[1536,512]{1,0:T(8,128)(2,1)} %get-tuple-element.615, bf16[1536,48]{1,0:T(8,128)(2,1)S(1)} %get-tuple-element.618, bf16[1536,512]{1,0:T(8,128)(2,1)} %get-tuple-element.614, bf16[1536,48]{1,0:T(8,128)(2,1)S(1)} %get-tuple-element.617), dimensions={1} | concatenate | bytes 6881280 | tf_op jit(solution)/shard_map/concatenate | solution.py:494
  317.2 12.9 %fusion.99 = f32[2048,1120]{0,1:T(8,128)} fusion(bf16[2048,1536]{1,0:T(8,128)(2,1)} %bitcast.321, bf16[1536,1120]{1,0:T(8,128)(2,1)} %concatenate.134), kind=kOutput, calls=%fused_computation.232 | convolution fusion | flops 7046430720 | bytes 18907136 | tf_op jit(solution)/shard_map/dot_general | solution.py:56
  330.1 10.5 %multiply_convert_fusion.2 = (bf16[2048,560]{0,1:T(8,128)(2,1)}, bf16[2048,560]{0,1:T(8,128)(2,1)}, bf16[2048,560]{0,1:T(8,128)(2,1)S(1)}) fusion(f32[2048,1120]{0,1:T(8,128)} %fusion.99, bf16[2048,1536]{1,0:T(8,128)(2,1)} %bitcast.375, bf16[1536,48]{1,0:T(8,128)(2,1)S(1)} %get-tuple-element.616, bf16[1536,512]{1,0:T(8,128)(2,1)S(1)} %copy-done.20), kind=kOutput, calls=%fused_computation.75 | convolution fusion | flops 3543859200 | bytes 24068096 | tf_op jit(solution)/shard_map/dot_general | solution.py:56
  340.6 6.5 convolution_convert_fusion.5
  347.1 7.2 %convolution_convert_fusion.3 = bf16[2048,1536]{1,0:T(8,128)(2,1)} fusion(bf16[2048,560]{0,1:T(8,128)(2,1)S(1)} %get-tuple-element.604, bf16[1536,48]{1,0:T(8,128)(2,1)S(1)} %get-tuple-element.616, bf16[1536,512]{1,0:T(8,128)(2,1)S(1)} %copy-done.20), kind=kOutput, calls=%fused_computation.67 | convolution fusion | flops 3529801728 | bytes 10305536 | tf_op jit(solution)/shard_map/dot_general | solution.py:60
  354.4 8.8 %convolution_convert_fusion.1 = bf16[1536,1120]{0,1:T(8,128)(2,1)S(1)} fusion(bf16[2048,1536]{1,0:T(8,128)(2,1)S(1)} %bitcast.324, bf16[2048,560]{0,1:T(8,128)(2,1)S(1)} %copy-done.46, bf16[2048,560]{0,1:T(8,128)(2,1)S(1)} %copy-done.44), kind=kOutput, calls=%fused_computation.65 | convolution fusion | flops 7057326080 | bytes 14319616 | tf_op jit(solution)/shard_map/dot_general | solution.py:64
  363.3 12.1 %convolution_convert_fusion = bf16[2048,1536]{1,0:T(8,128)(2,1)} fusion(bf16[1536,1120]{1,0:T(8,128)(2,1)S(1)} %copy-done.16, bf16[2048,560]{0,1:T(8,128)(2,1)} %get-tuple-element.603, bf16[2048,560]{0,1:T(8,128)(2,1)S(1)} %copy-done.45), kind=kOutput, calls=%fused_computation.64 | convolution fusion | flops 7058751488 | bytes 14319616 | tf_op jit(solution)/shard_map/dot_general | solution.py:60
  382.6 8.0 %copy.165 = bf16[1536,1792]{1,0:T(8,128)(2,1)} copy(bf16[1536,1792]{0,1:T(8,128)(2,1)} %broadcast_dynamic-update-slice_fusion) | data formatting | bytes 11010048 | tf_op jit(solution)/shard_map/concatenate | solution.py:575
  395.6 76.6 %shard_map.257 = (f32[128,1536]{1,0:T(8,128)}, f32[128,1536]{1,0:T(8,128)}) custom-call(bf16[16,128,1536]{2,1,0:T(8,128)(2,1)} %bitcast.326, bf16[16,128,1536]{2,1,0:T(8,128)(2,1)} %bitcast.325), custom_call_target="tpu_custom_call" | custom-call | tf_op jit(solution)/shard_map/pallas_call | solution.py:378
  476.3 4.2 fusion.68
  483.1 6.0 while.59
  490.8 4.8 add_convert_fusion
  495.6 10.7 %all-to-all-start.1 = ((bf16[16,48,1792]{2,1,0:T(8,128)(2,1)}), bf16[16,48,1792]{2,1,0:T(8,128)(2,1)}, u32[]{:S(2)}, u32[]{:S(2)}) async-start(bf16[16,48,1792]{2,1,0:T(8,128)(2,1)} %add_convert_fusion), calls=%async_computation.1 | async-start | bytes 5505024 | tf_op jit(solution)/shard_map/all_to_all | solution.py:591
  507.4 6.0 while.60
  522.2 55.4 %shard_map.258 = f32[128,512]{1,0:T(8,128)} custom-call(bf16[16,128,512]{2,1,0:T(8,128)(2,1)} %bitcast.320), custom_call_target="tpu_custom_call" | custom-call | tf_op jit(solution)/shard_map/pallas_call | solution.py:378
  583.8 5.2 fusion.58
  593.5 4.4 convolution_convert_fusion.2
  598.0 77.5 %shard_map.259 = (f32[96,2048]{1,0:T(8,128)}, f32[96,1536]{1,0:T(8,128)}, f32[16,128]{1,0:T(8,128)}) custom-call(bf16[16,96,2048]{2,1,0:T(8,128)(2,1)} %bitcast.307, bf16[16,96,1536]{2,1,0:T(8,128)(2,1)} %bitcast.308, bf16[16,16,128]{2,1,0:T(8,128)(2,1)} %bitcast.367), custom_call_target="tpu_custom_call" | custom-call | tf_op jit(solution)/shard_map/pallas_call | solution.py:378
  (328 shorter events, 149.1 us)
Async XLA Ops:
  30.1 7.7 %copy-start.40 = (bf16[96]{0:T(256)(128)(2,1)S(1)}, bf16[96]{0:T(256)(128)(2,1)}, u32[]{:S(2)}) copy-start(bf16[96]{0:T(256)(128)(2,1)} %param.35) | copy-start | bytes 580
  30.1 8.4 %copy-start.28 = (bf16[96,1536]{1,0:T(8,128)(2,1)S(1)}, bf16[96,1536]{1,0:T(8,128)(2,1)}, u32[]{:S(2)}) copy-start(bf16[96,1536]{1,0:T(8,128)(2,1)} %param.28) | copy-start | bytes 884740
  30.1 8.3 %copy-start.33 = (bf16[96,256]{1,0:T(8,128)(2,1)S(1)}, bf16[96,256]{1,0:T(8,128)(2,1)}, u32[]{:S(2)}) copy-start(bf16[96,256]{1,0:T(8,128)(2,1)} %param.32) | copy-start | bytes 147460
  30.1 8.3 %copy-start.34 = (bf16[96,256]{1,0:T(8,128)(2,1)S(1)}, bf16[96,256]{1,0:T(8,128)(2,1)}, u32[]{:S(2)}) copy-start(bf16[96,256]{1,0:T(8,128)(2,1)} %param.30) | copy-start | bytes 147460
  30.1 111.5 %copy-start.10 = (bf16[2,64,1536]{2,1,0:T(8,128)(2,1)S(1)}, bf16[2,64,1536]{2,1,0:T(8,128)(2,1)}, u32[]{:S(2)}) copy-start(bf16[2,64,1536]{2,1,0:T(8,128)(2,1)} %param.25) | copy-start | bytes 1179652
  30.2 211.0 %all-to-all-start = ((bf16[16,48,1792]{2,1,0:T(8,128)(2,1)}), bf16[16,48,1792]{2,1,0:T(8,128)(2,1)}, u32[]{:S(2)}, u32[]{:S(2)}) async-start(bf16[16,48,1792]{2,1,0:T(8,128)(2,1)} %copy.149), calls=%async_computation | async-start | bytes 5505024 | tf_op jit(solution)/shard_map/all_to_all | solution.py:488
  146.1 84.4 %copy-start.13 = (f32[128,2048]{1,0:T(8,128)}, f32[128,2048]{1,0:T(8,128)S(1)}, u32[]{:S(2)}) copy-start(f32[128,2048]{1,0:T(8,128)S(1)} %convolution_add_fusion.5) | copy-start | bytes 3145732
  147.4 88.7 %copy-start.24 = (f32[64,128]{1,0:T(8,128)}, f32[64,128]{1,0:T(8,128)S(1)}, u32[]{:S(2)}) copy-start(f32[64,128]{1,0:T(8,128)S(1)} %get-tuple-element.660) | copy-start | bytes 98308
  147.4 88.7 %copy-start.26 = (f32[64,128]{1,0:T(8,128)}, f32[64,128]{1,0:T(8,128)S(1)}, u32[]{:S(2)}) copy-start(f32[64,128]{1,0:T(8,128)S(1)} %get-tuple-element.659) | copy-start | bytes 98308
  241.2 62.4 %collective-permute-start = (bf16[16,48,1792]{2,1,0:T(8,128)(2,1)}, bf16[16,48,1792]{2,1,0:T(8,128)(2,1)}, u32[]{:S(2)}, u32[]{:S(2)}) collective-permute-start(bf16[16,48,1792]{2,1,0:T(8,128)(2,1)} %all-to-all-done), channel_id=1, source_target_pairs={{0,16},{16,0},{1,17},{17,1},{2,18},{18,2},{3,19},{19,3},{4,20},{20... | collective-permute-start | bytes 8257544 | tf_op jit(solution)/shard_map/ppermute | solution.py:395
  244.9 9.6 %copy-start.3 = (bf16[1024,2,128]{2,0,1:T(8,128)(2,1)}, bf16[1024,2,128]{2,0,1:T(8,128)(2,1)S(1)}, u32[]{:S(2)}) copy-start(bf16[1024,2,128]{2,0,1:T(8,128)(2,1)S(1)} %get-tuple-element.1156) | copy-start | bytes 1572868
  245.0 55.9 %copy-start.41 = (f32[128]{0:T(128)}, f32[128]{0:T(128)S(1)}, u32[]{:S(2)}) copy-start(f32[128]{0:T(128)S(1)} %rsqrt.28) | copy-start | bytes 1540
  317.2 12.9 %copy-start.20 = (bf16[1536,512]{1,0:T(8,128)(2,1)S(1)}, bf16[1536,512]{1,0:T(8,128)(2,1)}, u32[]{:S(2)}) copy-start(bf16[1536,512]{1,0:T(8,128)(2,1)} %get-tuple-element.613) | copy-start | bytes 4718596
  317.2 37.1 %slice-start = ((s8[6291456]{0:T(1024)(128)(4,1)}), s8[4194304]{0:T(1024)(128)(4,1)S(1)}, s32[]{:S(2)}) async-start(s8[6291456]{0:T(1024)(128)(4,1)} %bitcast.322), calls=%async_computation.2 | async-start | bytes 8388608
  330.1 24.3 %slice-start.1 = ((s8[6291456]{0:T(1024)(128)(4,1)}), s8[2097152]{0:T(1024)(128)(4,1)S(1)}, s32[]{:S(2)}) async-start(s8[6291456]{0:T(1024)(128)(4,1)} %bitcast.322), calls=%async_computation.3 | async-start | bytes 4194304
  354.4 8.9 %copy-start.16 = (bf16[1536,1120]{1,0:T(8,128)(2,1)S(1)}, bf16[1536,1120]{1,0:T(8,128)(2,1)}, u32[]{:S(2)}) copy-start(bf16[1536,1120]{1,0:T(8,128)(2,1)} %concatenate.134) | copy-start | bytes 10321924
  354.4 8.9 %copy-start.45 = (bf16[2048,560]{0,1:T(8,128)(2,1)S(1)}, bf16[2048,560]{0,1:T(8,128)(2,1)}, u32[]{:S(2)}) copy-start(bf16[2048,560]{0,1:T(8,128)(2,1)} %get-tuple-element.602) | copy-start | bytes 6881284
  394.0 96.7 %collective-permute-start.1 = (bf16[16,48,1792]{2,1,0:T(8,128)(2,1)}, bf16[16,48,1792]{2,1,0:T(8,128)(2,1)}, u32[]{:S(2)}, u32[]{:S(2)}) collective-permute-start(bf16[16,48,1792]{2,1,0:T(8,128)(2,1)} %constant_dynamic-slice_fusion), channel_id=1, source_target_pairs={{0,16},{16,0},{1,17},{17,1},{2,18},{18,2},{3,19},{19,3},{4,20},{20... | collective-permute-start | bytes 8257544 | tf_op jit(solution)/shard_map/ppermute | solution.py:395
  395.6 76.6 %copy-start.7 = (f32[128,1536]{1,0:T(8,128)S(1)}, f32[128,1536]{1,0:T(8,128)}, u32[]{:S(2)}) copy-start(f32[128,1536]{1,0:T(8,128)} %copy-done.6) | copy-start | bytes 2359300
  395.6 78.0 %copy-start.22 = (bf16[2,64,1536]{2,1,0:T(8,128)(2,1)S(1)}, bf16[2,64,1536]{2,1,0:T(8,128)(2,1)}, u32[]{:S(2)}) copy-start(bf16[2,64,1536]{2,1,0:T(8,128)(2,1)} %param.39) | copy-start | bytes 1179652
  495.6 86.4 %all-to-all-start.1 = ((bf16[16,48,1792]{2,1,0:T(8,128)(2,1)}), bf16[16,48,1792]{2,1,0:T(8,128)(2,1)}, u32[]{:S(2)}, u32[]{:S(2)}) async-start(bf16[16,48,1792]{2,1,0:T(8,128)(2,1)} %add_convert_fusion), calls=%async_computation.1 | async-start | bytes 5505024 | tf_op jit(solution)/shard_map/all_to_all | solution.py:591
  520.7 58.7 %copy-start.1 = (f32[2,384,128]{2,1,0:T(8,128)S(1)}, f32[2,384,128]{2,1,0:T(8,128)}, u32[]{:S(2)}) copy-start(f32[2,384,128]{2,1,0:T(8,128)} %copy-done) | copy-start | bytes 1179652
  582.0 101.0 %collective-permute-start.2 = (bf16[16,48,1792]{2,1,0:T(8,128)(2,1)}, bf16[16,48,1792]{2,1,0:T(8,128)(2,1)}, u32[]{:S(2)}, u32[]{:S(2)}) collective-permute-start(bf16[16,48,1792]{2,1,0:T(8,128)(2,1)} %all-to-all-done.1), channel_id=1, source_target_pairs={{0,16},{16,0},{1,17},{17,1},{2,18},{18,2},{3,19},{19,3},{4,20},{20... | collective-permute-start | bytes 8257544 | tf_op jit(solution)/shard_map/ppermute | solution.py:395
  598.0 83.8 %copy-start.43 = (f32[128]{0:T(128)S(1)}, f32[128]{0:T(128)}, u32[]{:S(2)}) copy-start(f32[128]{0:T(128)} %multiply_multiply_fusion) | copy-start | bytes 1540
  (34 other events, 149.5 us)

commit v3 on v2

--- a/solution.py
+++ b/solution.py
@@ -147,6 +147,10 @@
         jnp.zeros(value_all.shape, F32),
     )
     return lax.fori_loop(0, block_total(length, rank_end, key_step), visit, initial)
+
+
+D = 1536
+COLS = 3 * MAIN + 256
 
 
 def place():
@@ -229,14 +233,32 @@
                 self.got(idx(zz, x, 1 - c))
                 self.got(idx(zz, 1 - x, 1 - c))
             when(self.inside(zz), arrive)
-    def end(self):
+    def from_z(self, zz):
+        z, x, c = self.z, self.x, self.c
+        b = idx(zz, x, c)
+        self.got(b)
+        s = jnp.where(zz < z, 1, -1)
+        d = jnp.abs(zz - z)
+        slot = jnp.where(zz < z, 0, 3) + d
+        when(self.inside(z + s), lambda: self.put(self.out.at[b], b, slot, (self.r, idx(z + s, x, c))))
+        self.put(self.out.at[b], b, 6 + zz, self.xdev())
+        self.put(self.out.at[b], b, 10 + 2 * zz + x, self.cdev())
+    def from_x(self, zz):
+        b = idx(zz, 1 - self.x, self.c)
+        self.got(b)
+        self.put(self.out.at[b], b, 10 + 2 * zz + 1 - self.x, self.cdev())
+    def from_c(self, zz):
+        self.got(idx(zz, self.x, 1 - self.c))
+        self.got(idx(zz, 1 - self.x, 1 - self.c))
+    def end(self, local=True):
         z = self.z
         for d in range(NZ - 1):
             when((z - d >= 0) & (z < NZ - 1), lambda d=d: self.sent(d))
             when((z + d < NZ) & (z > 0), lambda d=d: self.sent(3 + d))
         for k in range(6, 18):
             self.sent(k)
-        pltpu.make_async_copy(self.src, self.out.at[0], self.local).wait()
+        if local:
+            pltpu.make_async_copy(self.src, self.out.at[0], self.local).wait()
 
 def gather_kernel(n, with_side, *refs):
     srcs, outs = refs[:n], refs[n:2*n]
@@ -282,6 +304,12 @@
                 for s, zz in self.over(d):
                     k = 2 * zz + xx
                     when(self.inside(zz), lambda zz=zz, k=k, xx=xx: self.copy(self.part.at[idx(zz, xx, 1 - c)], self.rc.at[k], k, self.rcs.at[k], dev).start())
+    def send_c(self, zz):
+        z, x, c = self.z, self.x, self.c
+        dev = (self.r, idx(z, x, 1 - c))
+        for xx in (1 - x, x):
+            k = 2 * zz + xx
+            self.copy(self.part.at[idx(zz, xx, 1 - c)], self.rc.at[k], k, self.rcs.at[k], dev).start()
     def step_x(self, d):
         z, x, c = self.z, self.x, self.c
         dev = (self.r, idx(z, 1 - x, c))
@@ -385,6 +413,162 @@
     )(*parts)
 
 
+def dot(a, b):
+    return lax.dot_general(a, b, (((1,), (0,)), ((), ())), preferred_element_type=F32)
+def dot_nt(a, b):
+    return lax.dot_general(a, b, (((1,), (1,)), ((), ())), preferred_element_type=F32)
+def dot_tn(a, b):
+    return lax.dot_general(a, b, (((0,), (0,)), ((), ())), preferred_element_type=F32)
+
+def gated(g, u, gh):
+    sig = jax.nn.sigmoid(g)
+    silu = g * sig
+    return (gh * u * (sig * (1.0 + g * (1.0 - sig)))).astype(BF), (gh * silu).astype(BF), (silu * u).astype(BF)
+
+def mlp_kernel(spare, n2_ref, cot_ref, w_ref, gsum, osum, half_ref,
+               n2, cot, w, act, pg, po, rcg, rxg, rzg, rco, rxo, rzo, yb,
+               gsend, grecv, glocal, lsem, ssend, srcs, srxs, srzs, ysend, yrecv):
+    at = place()
+    r, z, x, c = at
+    loads = [pltpu.make_async_copy(w_ref, w, lsem.at[0]), pltpu.make_async_copy(cot_ref, cot, lsem.at[1])]
+    for l in loads: l.start()
+    greet(*at, with_y=True)
+    g = Gather(at, n2_ref, n2, gsend, grecv, glocal)
+    rg = Scatter(at, pg, rcg, rxg, rzg, ssend.at[0], srcs.at[0], srxs.at[0], srzs.at[0])
+    ro = Scatter(at, po, rco, rxo, rzo, ssend.at[1], srcs.at[1], srxs.at[1], srzs.at[1])
+    g.begin()
+    for l in loads: l.wait()
+    mid = (z > 0) & (z < NZ - 1)
+    p = [z,
+         jnp.where(z == 0, 1, jnp.where(z == 1, 0, jnp.where(z == 2, 3, 2))),
+         jnp.where(z == 0, 2, jnp.where(z == 1, 2, 1)),
+         jnp.where(z < 2, 3, 0)]
+
+    def tiles(zz):
+        rows = pl.ds(pl.multiple_of(4 * zz, 4), 4)
+        tok = pl.ds(pl.multiple_of(512 * zz, 512), 512)
+        @pl.loop(0, 2)
+        def _(t):
+            a = n2[rows].reshape(512, D)
+            k = cot[rows].reshape(512, D)
+            def col(base):
+                return pl.ds(pl.multiple_of(base + 256 * t, 256), 256)
+            dg, du, h = gated(dot(a, w[:, col(0)]), dot(a, w[:, col(MAIN)]), dot(k, w[:, col(2 * MAIN)]))
+            act[tok, col(0)] = dg
+            act[tok, col(MAIN)] = du
+            act[tok, col(2 * MAIN)] = h
+        a = n2[rows].reshape(512, D)
+        k = cot[rows].reshape(512, D)
+        pre = dot(a, w[:, 3 * MAIN : 3 * MAIN + 128])
+        gh = dot(k, w[:, 3 * MAIN + 128 :])
+        lane = lax.broadcasted_iota(jnp.int32, (512, 128), 1)
+        sig = jax.nn.sigmoid(pre)
+        silu = pre * sig
+        up = pltpu.roll(pre, 128 - spare, 1)
+        dg = gh * up * (sig * (1.0 + pre * (1.0 - sig)))
+        du = pltpu.roll(gh * silu, spare, 1)
+        act[tok, 3 * MAIN : 3 * MAIN + 128] = jnp.where(lane < spare, dg, jnp.where(lane < 2 * spare, du, 0.0)).astype(BF)
+        act[tok, 3 * MAIN + 128 :] = jnp.where(lane < spare, silu * up, 0.0).astype(BF)
+        @pl.loop(0, D // 256)
+        def _(t):
+            dr = pl.ds(pl.multiple_of(256 * t, 256), 256)
+            v = dot_nt(act[tok, : 2 * MAIN], w[dr, : 2 * MAIN]) + dot_nt(act[tok, 3 * MAIN : 3 * MAIN + 128], w[dr, 3 * MAIN : 3 * MAIN + 128])
+            pg[rows, :, dr] = v.astype(BF).reshape(4, 128, 256)
+            v = dot_nt(act[tok, 2 * MAIN : 3 * MAIN], w[dr, 2 * MAIN : 3 * MAIN]) + dot_nt(act[tok, 3 * MAIN + 128 :], w[dr, 3 * MAIN + 128 :])
+            po[rows, :, dr] = v.astype(BF).reshape(4, 128, 256)
+        rg.send_c(zz)
+        ro.send_c(zz)
+
+    g.from_z(p[1])
+    when(mid, lambda: g.from_z(p[2]))
+    g.from_x(p[0])
+    g.from_c(p[0])
+    pltpu.make_async_copy(n2_ref, n2.at[0], glocal).wait()
+    tiles(p[0])
+    g.from_z(jnp.where(mid, p[3], p[2]))
+    g.from_x(p[1])
+    g.from_c(p[1])
+    tiles(p[1])
+    when(~mid, lambda: g.from_z(p[3]))
+    g.from_x(p[2])
+    g.from_c(p[2])
+    tiles(p[2])
+    g.from_x(p[3])
+    g.from_c(p[3])
+    tiles(p[3])
+
+    ydev = (1 - r, idx(z, x, c))
+    own = D // 16
+    half = own // 2
+    def ycopy(j):
+        src = w.at[pl.ds(pl.multiple_of(own * j + half * (1 - r), half), half)]
+        return pltpu.make_async_remote_copy(src, yb.at[j], ysend.at[j], yrecv.at[j], device_id=ydev, device_id_type=MESH)
+    def grads(q):
+        dr = slice(384 * q, 384 * (q + 1))
+        row = slice(384 * q, 384 * (q + 1))
+        @pl.loop(0, 4)
+        def _(t):
+            col = pl.ds(pl.multiple_of(256 * t, 256), 256)
+            w[row, col] = dot_tn(n2[:, :, dr].reshape(2048, 384), act[:, col]).astype(BF)
+        @pl.loop(0, 2)
+        def _(t):
+            col = pl.ds(pl.multiple_of(2 * MAIN + 256 * t, 256), 256)
+            w[row, col] = dot_tn(cot[:, :, dr].reshape(2048, 384), act[:, col]).astype(BF)
+        w[row, 3 * MAIN : 3 * MAIN + 128] = dot_tn(n2[:, :, dr].reshape(2048, 384), act[:, 3 * MAIN : 3 * MAIN + 128]).astype(BF)
+        w[row, 3 * MAIN + 128 :] = dot_tn(cot[:, :, dr].reshape(2048, 384), act[:, 3 * MAIN + 128 :]).astype(BF)
+        for j in range(4 * q, 4 * q + 4):
+            ycopy(j).start()
+    def yadd(j):
+        ycopy(j).wait()
+        mine = w[pl.ds(pl.multiple_of(own * j + half * r, half), half)]
+        yb[j] = (mine.astype(F32) + yb[j].astype(F32)).astype(BF)
+        pltpu.make_async_copy(yb.at[j], half_ref.at[j], lsem.at[2]).start()
+
+    rg.step_x(3)
+    rg.step_x(2)
+    grads(0)
+    rg.step_z(3)
+    rg.step_x(1)
+    grads(1)
+    rg.step_z(2)
+    rg.step_x(0)
+    grads(2)
+    rg.step_z(1)
+    ro.step_x(3)
+    ro.step_x(2)
+    grads(3)
+    rg.finish(gsum)
+    ro.step_z(3)
+    ro.step_x(1)
+    for j in range(0, 4): yadd(j)
+    ro.step_z(2)
+    ro.step_x(0)
+    for j in range(4, 8): yadd(j)
+    ro.step_z(1)
+    for j in range(8, 12): yadd(j)
+    ro.finish(osum)
+    for j in range(12, 16): yadd(j)
+    pltpu.make_async_copy(yb, half_ref, lsem.at[2]).wait()
+    g.end(local=False)
+
+def mlp(n2, cot, w, spare, cid):
+    blk = n2.shape
+    dma = pltpu.SemaphoreType.DMA
+    full = (16,) + blk
+    return pl.pallas_call(
+        functools.partial(mlp_kernel, spare),
+        out_shape=[jax.ShapeDtypeStruct(blk, F32)] * 2 + [jax.ShapeDtypeStruct((16, D // 32, COLS), BF)],
+        in_specs=[pl.BlockSpec(memory_space=pl.ANY)] * 3,
+        out_specs=[pl.BlockSpec(memory_space=pltpu.VMEM)] * 2 + [pl.BlockSpec(memory_space=pl.ANY)],
+        scratch_shapes=[pltpu.VMEM(full, BF), pltpu.VMEM(full, BF), pltpu.VMEM((D, COLS), BF), pltpu.VMEM((16 * blk[0], COLS), BF),
+                        pltpu.VMEM(full, BF), pltpu.VMEM(full, BF)]
+        + [pltpu.VMEM((k,) + blk, BF) for k in (8, 4, 5, 8, 4, 5)]
+        + [pltpu.VMEM((16, D // 32, COLS), BF)]
+        + [dma((18,)), dma((16,)), dma(()), dma((3,)), dma((2, 16)), dma((2, 8)), dma((2, 4)), dma((2, 5)), dma((16,)), dma((16,))],
+        compiler_params=pltpu.CompilerParams(collective_id=cid, has_side_effects=True, vmem_limit_bytes=60 * 2**20),
+    )(n2, cot, w)
+
+
 def gather_all(arrays, cid, fast):
     if fast:
         return gather(arrays, cid)
@@ -415,6 +599,67 @@
 def own_half(x, dim, rank):
     half = x.shape[dim] // 2
     return lax.dynamic_slice_in_dim(x, rank * half, half, dim)
+
+
+def mlp_plain(normed_two, grad_all, columns, main, spare, own_rows):
+    group_count = lax.axis_size("group")
+    replica_rank = lax.axis_index("replica")
+    tokens, model_width = normed_two.shape
+    share = main + spare
+    rest = 3 * main
+    gate_up_w = jnp.concatenate(
+        (
+            columns[:, :main],
+            columns[:, rest : rest + spare],
+            columns[:, main : 2 * main],
+            columns[:, rest + spare : rest + 2 * spare],
+        ),
+        axis=1,
+    )
+    down_w = jnp.concatenate(
+        (columns[:, 2 * main : rest], columns[:, rest + 128 : rest + 128 + spare]), axis=1
+    )
+
+    normed_all = lax.all_gather(normed_two, "group", axis=0)
+    normed_all = normed_all.reshape(group_count * tokens, model_width)
+
+    pre = matmul(normed_all, gate_up_w)
+    gate_pre = pre[:, :share]
+    up_pre = pre[:, share:]
+    sigmoid_gate = jax.nn.sigmoid(gate_pre)
+    silu_gate = gate_pre * sigmoid_gate
+    hidden = (silu_gate * up_pre).astype(BF)
+    grad_hidden = matmul(grad_all, down_w)
+    grad_gate = (
+        grad_hidden * up_pre * (sigmoid_gate * (1.0 + gate_pre * (1.0 - sigmoid_gate)))
+    ).astype(BF)
+    grad_up = (grad_hidden * silu_gate).astype(BF)
+    gate_up_grad = jnp.concatenate((grad_gate, grad_up), axis=1)
+    sums = [
+        p.astype(BF).reshape(group_count, tokens, model_width)
+        for p in (matmul_nt(gate_up_grad, gate_up_w), matmul_nt(hidden, down_w))
+    ]
+    grad_normed_two, mlp_out = scatter_all(sums, 4, False)
+    down_term = matmul_tn(grad_all, hidden).astype(BF)
+    gate_up_term = matmul_tn(normed_all, gate_up_grad).astype(BF)
+    zeros = jnp.zeros((model_width, 128), BF)
+    terms = jnp.concatenate(
+        (
+            gate_up_term[:, :main],
+            gate_up_term[:, share : share + main],
+            down_term[:, :main],
+            gate_up_term[:, main:share],
+            gate_up_term[:, share + main :],
+            zeros[:, : 128 - 2 * spare],
+            down_term[:, main:],
+            zeros[:, : 128 - spare],
+        ),
+        axis=1,
+    ).reshape(group_count, own_rows, 3 * main + 256)
+    half_sum = own_half(terms, 1, replica_rank).astype(F32) + swap(
+        other_half(terms, 1, replica_rank)
+    ).astype(F32)
+    return (grad_normed_two, mlp_out, half_sum.astype(BF))
 
 
 def shards(
@@ -491,19 +736,6 @@
     second = jnp.where(replica_rank == 0, other_part, own_part)
     columns = jnp.concatenate((first, second), axis=1).reshape(model_width, 3 * main + 256)
     rest = 3 * main
-    gate_up_w = jnp.concatenate(
-        (
-            columns[:, :main],
-            columns[:, rest : rest + spare],
-            columns[:, main : 2 * main],
-            columns[:, rest + spare : rest + 2 * spare],
-        ),
-        axis=1,
-    )
-    down_w = jnp.concatenate(
-        (columns[:, 2 * main : rest], columns[:, rest + 128 : rest + 128 + spare]), axis=1
-    )
-
     grad_final = cotangent.reshape(tokens, model_width).astype(F32) * valid_rows
 
     inputs = hidden_in.reshape(tokens, model_width).astype(F32)
@@ -549,46 +781,16 @@
     attended_low = jnp.concatenate(attended_rows, axis=0).astype(BF)
     residual_mid = inputs + matmul(attended_low, out_w)
     normed_two_full, factor_two = normalize(residual_mid, gain_two)
-    (normed_all,) = gather_all([normed_two_full.astype(BF)], 3, fast)
-    normed_all = normed_all.reshape(group_count * tokens, model_width)
-
-    pre = matmul(normed_all, gate_up_w)
-    gate_pre = pre[:, :share]
-    up_pre = pre[:, share:]
-    sigmoid_gate = jax.nn.sigmoid(gate_pre)
-    silu_gate = gate_pre * sigmoid_gate
-    hidden = (silu_gate * up_pre).astype(BF)
-    grad_hidden = matmul(grad_all, down_w)
-    grad_gate = (
-        grad_hidden * up_pre * (sigmoid_gate * (1.0 + gate_pre * (1.0 - sigmoid_gate)))
-    ).astype(BF)
-    grad_up = (grad_hidden * silu_gate).astype(BF)
-    gate_up_grad = jnp.concatenate((grad_gate, grad_up), axis=1)
-    sums = [
-        p.astype(BF).reshape(group_count, tokens, model_width)
-        for p in (matmul_nt(gate_up_grad, gate_up_w), matmul_nt(hidden, down_w))
-    ]
-    grad_normed_two, mlp_out = scatter_all(sums, 4, fast)
-    down_term = matmul_tn(grad_all, hidden).astype(BF)
-    gate_up_term = matmul_tn(normed_all, gate_up_grad).astype(BF)
-    zeros = jnp.zeros((model_width, 128), BF)
-    terms = jnp.concatenate(
-        (
-            gate_up_term[:, :main],
-            gate_up_term[:, share : share + main],
-            down_term[:, :main],
-            gate_up_term[:, main:share],
-            gate_up_term[:, share + main :],
-            zeros[:, : 128 - 2 * spare],
-            down_term[:, main:],
-            zeros[:, : 128 - spare],
-        ),
-        axis=1,
-    ).reshape(group_count, own_rows, 3 * main + 256)
-    half_sum = own_half(terms, 1, replica_rank).astype(F32) + swap(
-        other_half(terms, 1, replica_rank)
-    ).astype(F32)
-    half_back = lax.all_to_all(half_sum.astype(BF), "group", 0, 0, tiled=True)
+    normed_two = normed_two_full.astype(BF)
+    if fast:
+        grad_normed_two, mlp_out, half_sum = mlp(
+            normed_two, grad_all.reshape(group_count, tokens, model_width), columns, spare, 3
+        )
+    else:
+        grad_normed_two, mlp_out, half_sum = mlp_plain(
+            normed_two, grad_all, columns, main, spare, own_rows
+        )
+    half_back = lax.all_to_all(half_sum, "group", 0, 0, tiled=True)
     half_other = swap(half_back)
     first = jnp.where(replica_rank == 0, half_back, half_other)
     second = jnp.where(replica_rank == 0, half_other, half_back)

time: 712 us -> 685 us (0.962)
  matrix products: 94.8 us -> 35.2 us
  waiting for transfers between devices: 1.99 us -> 51.9 us
  local copies, waits for them, and re-layouts: 108 us -> 83.8 us
  Pallas kernels: 431 us -> 444 us
    pallas_call x0 -> x1, Pallas kernels: none -> 138 us  [mlp(): pl.pallas_call(functools.partial(mlp_kernel, spare), out_shape=[jax.Shape...]
    pallas_call x3 -> x2, Pallas kernels: 209 us -> 129 us  [scatter(): pl.pallas_call(functools.partial(scatter_kernel, n, pair), out_shape=[jax...]
    ppermute x3 -> x2, waiting for transfers between devices: 1.99 us -> 51.9 us  [swap(): return lax.ppermute(x, 'replica', [(0, 1), (1, 0)])]
    pallas_call x3 -> x2, Pallas kernels: 222 us -> 177 us  [gather(): pl.pallas_call(functools.partial(gather_kernel, n, False), out_shape=[jax...]
    dot_general x4 -> x2, matrix products: 30.7 us -> 7.18 us  [matmul(): return jnp.dot(a, b, preferred_element_type=F32)]
    dot_general x4 -> x2, matrix products: 28.8 us -> 9.48 us  [matmul_nt(): lax.dot_general(a, b, (((1,), (1,)), ((), ())), preferred_element_type=F32)]
    concatenate x3 -> x0, local copies, waits for them, and re-layouts: 16.2 us -> none  [the longest x2 8.71 us: shards(): jnp.concatenate((gate_up_term[:, :main], gate_up_term[:, share:share + ma...]
    dot_general x4 -> x2, matrix products: 23.3 us -> 8.05 us  [matmul_tn(): lax.dot_general(a, b, (((0,), (0,)), ((), ())), preferred_element_type=F32)]
  transfers between devices with their start and end apart: 5 -> 4, of which waited for: 1 -> 1; matrix products, arithmetic and copies ran while one was open for 14% -> 12% of each run, Pallas kernels for 61% -> 45%
where the time goes in v3:
time: 685 us; the launch traced here: 673 us
  Pallas kernels  444 us (65%)
  local copies, waits for them, and re-layouts  83.8 us (12%)
  waiting for transfers between devices  51.9 us (8%)
  other arithmetic  37.1 us (5%)
  matrix products  35.2 us (5%)
  starting transfers between devices  17.1 us (2%)
    pallas_call x2, Pallas kernels, gather(): pl.pallas_call(functools.partial(gather_kernel, n, False), out_shape=[jax...  177 us
    pallas_call x1, Pallas kernels, mlp(): pl.pallas_call(functools.partial(mlp_kernel, spare), out_shape=[jax.Shape...  138 us
    pallas_call x2, Pallas kernels, scatter(): pl.pallas_call(functools.partial(scatter_kernel, n, pair), out_shape=[jax...  129 us
    ppermute x2, waiting for transfers between devices, swap(): return lax.ppermute(x, 'replica', [(0, 1), (1, 0)])  51.9 us
  transfers between devices with their start and end apart: 4, of which 1 were waited for; matrix products, arithmetic and copies ran while one was open for 12% of the time, Pallas kernels for 45%

profile of v3, /device:TPU:0, one launch (start us, length us, event | category | flops | bytes accessed | tf_op | source)
XLA Modules:
  0.0 673.1 jit_solution(13580467954911608408)
XLA Ops:
  9.8 3.5 copy_bitcast_fusion.1
  14.9 8.8 %concatenate.119 = bf16[96,16,1792]{2,0,1:T(8,128)(2,1)} concatenate(bf16[96,16,512]{2,0,1:T(8,128)(2,1)S(1)} %bitcast.309, bf16[96,16,512]{2,0,1:T(8,128)(2,1)} %get-tuple-element.629, bf16[96,16,512]{2,0,1:T(8,128)(2,1)S(1)} %get-tuple-element.628, bf16[96,16,48]{2,0,1:T(8,128)(2,1)S(1)} %copy-done.27, bf16[96,16,48]{2,0,1:T(8,128)(2,1)} %copy.99, ...), dimensions={2} | concatenate | bytes 11010048 | tf_op jit(solution)/shard_map/concatenate | solution.py:731
  23.6 3.5 dynamic-slice_bitcast_fusion
  27.2 7.5 %all-to-all-start = ((bf16[16,48,1792]{2,1,0:T(8,128)(2,1)}), bf16[16,48,1792]{2,1,0:T(8,128)(2,1)}, u32[]{:S(2)}, u32[]{:S(2)}) async-start(bf16[16,48,1792]{2,1,0:T(8,128)(2,1)} %dynamic-slice_bitcast_fusion), calls=%async_computation | async-start | bytes 5505024 | tf_op jit(solution)/shard_map/all_to_all | solution.py:733
  36.3 101.0 %shard_map.254 = (bf16[16,96,2048]{2,1,0:T(8,128)(2,1)}, bf16[16,16,128]{2,1,0:T(8,128)(2,1)}) custom-call(bf16[96,2048]{1,0:T(8,128)(2,1)} %pad_maximum_fusion.2.refs_0_, bf16[16,128]{1,0:T(8,128)(2,1)} %pad_bitcast_fusion.refs_1_), custom_call_target="tpu_custom_call" | custom-call | tf_op jit(solution)/shard_map/pallas_call | solution.py:280
  139.6 3.8 convolution_add_fusion.5
  149.6 76.1 %shard_map.255 = (bf16[16,128,512]{2,1,0:T(8,128)(2,1)}, bf16[16,128,1536]{2,1,0:T(8,128)(2,1)}, bf16[16,96,1536]{2,1,0:T(8,128)(2,1)}) custom-call(bf16[128,512]{1,0:T(8,128)(2,1)} %pad_maximum_fusion.3.refs_0_, bf16[128,1536]{1,0:T(8,128)(2,1)} %fusion.45.refs_1_, bf16[96,1536]{1,0:T(8,128)(2,1)} %refs_2_.1), custom_call_target="tpu_custom_call" | custom-call | tf_op jit(solution)/shard_map/pallas_call | solution.py:280
  225.7 3.1 copy.162
  245.4 3.4 multiply_reduce_fusion.2
  250.5 51.9 %collective-permute-done = bf16[16,48,1792]{2,1,0:T(8,128)(2,1)} collective-permute-done((bf16[16,48,1792]{2,1,0:T(8,128)(2,1)}, bf16[16,48,1792]{2,1,0:T(8,128)(2,1)}, u32[]{:S(2)}, u32[]{:S(2)}) %collective-permute-start) | collective-permute-done | bytes 2752544 | tf_op jit(solution)/shard_map/ppermute | solution.py:579
  302.4 3.0 broadcast_select_fusion.3
  305.4 2.9 pad_maximum_fusion
  308.3 137.9 %shard_map.256 = (f32[128,1536]{1,0:T(8,128)}, f32[128,1536]{1,0:T(8,128)}, bf16[16,48,1792]{2,1,0:T(8,128)(2,1)}) custom-call(bf16[128,1536]{1,0:T(8,128)(2,1)} %multiply_convert_fusion.1.n2_ref, bf16[16,128,1536]{2,1,0:T(8,128)(2,1)} %get-tuple-element.273.cot_ref, bf16[1536,1792]{1,0:T(8,128)(2,1)} %bitcast.302), custom_call_target="tpu_custom_call" | custom-call | tf_op jit(solution)/shard_map/pallas_call | solution.py:558
  450.2 4.2 fusion.66
  456.7 5.2 while.60
  463.8 4.5 all-to-all-start.1
  469.5 6.4 while.59
  487.4 51.8 %shard_map.257 = f32[128,512]{1,0:T(8,128)} custom-call(bf16[16,128,512]{2,1,0:T(8,128)(2,1)} %bitcast.308), custom_call_target="tpu_custom_call" | custom-call | tf_op jit(solution)/shard_map/pallas_call | solution.py:406
  543.8 3.5 collective-permute-start.1
  547.3 5.2 fusion.56
  553.8 3.6 convolution_convert_fusion.1
  557.4 4.5 convolution_convert_fusion
  561.9 76.9 %shard_map.258 = (f32[96,2048]{1,0:T(8,128)}, f32[96,1536]{1,0:T(8,128)}, f32[16,128]{1,0:T(8,128)}) custom-call(bf16[16,96,2048]{2,1,0:T(8,128)(2,1)} %bitcast.298, bf16[16,96,1536]{2,1,0:T(8,128)(2,1)} %bitcast.299, bf16[16,16,128]{2,1,0:T(8,128)(2,1)} %bitcast.347), custom_call_target="tpu_custom_call" | custom-call | tf_op jit(solution)/shard_map/pallas_call | solution.py:406
  646.3 3.0 broadcast_select_fusion.1
  (305 shorter events, 109.7 us)
Async XLA Ops:
  9.7 5.1 copy-start.27
  27.1 7.6 %copy-start.46 = (bf16[96]{0:T(256)(128)(2,1)S(1)}, bf16[96]{0:T(256)(128)(2,1)}, u32[]{:S(2)}) copy-start(bf16[96]{0:T(256)(128)(2,1)} %param.27) | copy-start | bytes 580
  27.1 7.6 %copy-start.47 = (bf16[96]{0:T(256)(128)(2,1)S(1)}, bf16[96]{0:T(256)(128)(2,1)}, u32[]{:S(2)}) copy-start(bf16[96]{0:T(256)(128)(2,1)} %param.29) | copy-start | bytes 580
  27.1 7.6 %copy-start.48 = (bf16[16]{0:T(256)(128)(2,1)S(1)}, bf16[16]{0:T(256)(128)(2,1)}, u32[]{:S(2)}) copy-start(bf16[16]{0:T(256)(128)(2,1)} %param.31) | copy-start | bytes 100
  27.1 7.7 %copy-start.49 = (bf16[16]{0:T(256)(128)(2,1)S(1)}, bf16[16]{0:T(256)(128)(2,1)}, u32[]{:S(2)}) copy-start(bf16[16]{0:T(256)(128)(2,1)} %param.33) | copy-start | bytes 100
  27.2 7.7 %copy-start.50 = (bf16[96]{0:T(256)(128)(2,1)S(1)}, bf16[96]{0:T(256)(128)(2,1)}, u32[]{:S(2)}) copy-start(bf16[96]{0:T(256)(128)(2,1)} %param.35) | copy-start | bytes 580
  27.2 8.4 %copy-start.37 = (bf16[96,1536]{1,0:T(8,128)(2,1)S(1)}, bf16[96,1536]{1,0:T(8,128)(2,1)}, u32[]{:S(2)}) copy-start(bf16[96,1536]{1,0:T(8,128)(2,1)} %param.28) | copy-start | bytes 884740
  27.2 8.3 %copy-start.40 = (bf16[96,256]{1,0:T(8,128)(2,1)S(1)}, bf16[96,256]{1,0:T(8,128)(2,1)}, u32[]{:S(2)}) copy-start(bf16[96,256]{1,0:T(8,128)(2,1)} %param.32) | copy-start | bytes 147460
  27.2 8.3 %copy-start.41 = (bf16[96,256]{1,0:T(8,128)(2,1)S(1)}, bf16[96,256]{1,0:T(8,128)(2,1)}, u32[]{:S(2)}) copy-start(bf16[96,256]{1,0:T(8,128)(2,1)} %param.30) | copy-start | bytes 147460
  27.2 111.8 %copy-start.18 = (bf16[2,64,1536]{2,1,0:T(8,128)(2,1)S(1)}, bf16[2,64,1536]{2,1,0:T(8,128)(2,1)}, u32[]{:S(2)}) copy-start(bf16[2,64,1536]{2,1,0:T(8,128)(2,1)} %param.25) | copy-start | bytes 1179652
  27.2 212.8 %all-to-all-start = ((bf16[16,48,1792]{2,1,0:T(8,128)(2,1)}), bf16[16,48,1792]{2,1,0:T(8,128)(2,1)}, u32[]{:S(2)}, u32[]{:S(2)}) async-start(bf16[16,48,1792]{2,1,0:T(8,128)(2,1)} %dynamic-slice_bitcast_fusion), calls=%async_computation | async-start | bytes 5505024 | tf_op jit(solution)/shard_map/all_to_all | solution.py:733
  139.6 5.5 copy-start.28
  144.7 90.7 %copy-start.33 = (f32[64,128]{1,0:T(8,128)}, f32[64,128]{1,0:T(8,128)S(1)}, u32[]{:S(2)}) copy-start(f32[64,128]{1,0:T(8,128)S(1)} %get-tuple-element.611) | copy-start | bytes 98308
  144.7 90.7 %copy-start.35 = (f32[64,128]{1,0:T(8,128)}, f32[64,128]{1,0:T(8,128)S(1)}, u32[]{:S(2)}) copy-start(f32[64,128]{1,0:T(8,128)S(1)} %get-tuple-element.610) | copy-start | bytes 98308
  144.9 84.0 %copy-start.44 = (f32[128]{0:T(128)}, f32[128]{0:T(128)S(1)}, u32[]{:S(2)}) copy-start(f32[128]{0:T(128)S(1)} %reshape.741) | copy-start | bytes 1540
  240.0 62.4 %collective-permute-start = (bf16[16,48,1792]{2,1,0:T(8,128)(2,1)}, bf16[16,48,1792]{2,1,0:T(8,128)(2,1)}, u32[]{:S(2)}, u32[]{:S(2)}) collective-permute-start(bf16[16,48,1792]{2,1,0:T(8,128)(2,1)} %all-to-all-done), channel_id=1, source_target_pairs={{0,16},{16,0},{1,17},{17,1},{2,18},{18,2},{3,19},{19,3},{4,20},{20... | collective-permute-start | bytes 8257544 | tf_op jit(solution)/shard_map/ppermute | solution.py:579
  308.3 137.9 %copy-start.15 = (f32[128,1536]{1,0:T(8,128)S(1)}, f32[128,1536]{1,0:T(8,128)}, u32[]{:S(2)}) copy-start(f32[128,1536]{1,0:T(8,128)} %copy-done.14) | copy-start | bytes 2359300
  308.3 139.3 %copy-start.29 = (bf16[2,64,1536]{2,1,0:T(8,128)(2,1)S(1)}, bf16[2,64,1536]{2,1,0:T(8,128)(2,1)}, u32[]{:S(2)}) copy-start(bf16[2,64,1536]{2,1,0:T(8,128)(2,1)} %param.39) | copy-start | bytes 1179652
  308.3 139.3 %copy-start.45 = (f32[128]{0:T(128)S(1)}, f32[128]{0:T(128)}, u32[]{:S(2)}) copy-start(f32[128]{0:T(128)} %copy-done.44) | copy-start | bytes 1540
  463.8 79.9 %all-to-all-start.1 = ((bf16[16,48,1792]{2,1,0:T(8,128)(2,1)}), bf16[16,48,1792]{2,1,0:T(8,128)(2,1)}, u32[]{:S(2)}, u32[]{:S(2)}) async-start(bf16[16,48,1792]{2,1,0:T(8,128)(2,1)} %get-tuple-element.285), calls=%async_computation.1 | async-start | bytes 5505024 | tf_op jit(solution)/shard_map/all_to_all | solution.py:793
  487.4 54.1 %copy-start.5 = (f32[2,384,128]{2,1,0:T(8,128)S(1)}, f32[2,384,128]{2,1,0:T(8,128)}, u32[]{:S(2)}) copy-start(f32[2,384,128]{2,1,0:T(8,128)} %get-tuple-element.277) | copy-start | bytes 1179652
  543.8 102.6 %collective-permute-start.1 = (bf16[16,48,1792]{2,1,0:T(8,128)(2,1)}, bf16[16,48,1792]{2,1,0:T(8,128)(2,1)}, u32[]{:S(2)}, u32[]{:S(2)}) collective-permute-start(bf16[16,48,1792]{2,1,0:T(8,128)(2,1)} %all-to-all-done.1), channel_id=1, source_target_pairs={{0,16},{16,0},{1,17},{17,1},{2,18},{18,2},{3,19},{19,3},{4,20},{20... | collective-permute-start | bytes 8257544 | tf_op jit(solution)/shard_map/ppermute | solution.py:579
  547.3 6.6 copy-start.13
  547.3 6.6 copy-start.21
  (34 other events, 76.7 us)

commit v4 on v3

--- a/solution.py
+++ b/solution.py
@@ -178,6 +178,14 @@
     ends = jnp.where((z > 0) & (z < NZ - 1), 1, 0)
     pl.semaphore_wait(bar, (4 if with_y else 3) + ends)
 
+def planes(z):
+    return (
+        z,
+        jnp.where(z == 0, 1, jnp.where(z == 1, 0, jnp.where(z == 2, 3, 2))),
+        jnp.where(z == 0, 2, jnp.where(z == 1, 2, 1)),
+        jnp.where(z < 2, 3, 0),
+    )
+
 def when(cond, fn):
     pl.when(cond)(fn)
 
@@ -185,6 +193,8 @@
     def __init__(self, at, src, out, send, recv, local):
         self.r, self.z, self.x, self.c = at
         self.src, self.out, self.send, self.recv, self.local = src, out, send, recv, local
+        self.mid = (self.z > 0) & (self.z < NZ - 1)
+        self.p = planes(self.z)
     def put(self, src, b, k, dev):
         pltpu.make_async_remote_copy(src, self.out.at[b], self.send.at[k], self.recv.at[b], device_id=dev, device_id_type=MESH).start()
     def sent(self, k):
@@ -204,35 +214,6 @@
         self.put(self.src, me, 10 + 2 * z + x, self.cdev())
         pltpu.make_async_copy(self.src, self.out.at[me], self.local).start()
     def inside(self, z): return (z >= 0) & (z < NZ)
-    def step_z(self, d):
-        z, x, c = self.z, self.x, self.c
-        for s in (-1, 1):
-            zz = z + s * d
-            def arrive(s=s, zz=zz):
-                b = idx(zz, x, c)
-                self.got(b)
-                if d < NZ - 1:
-                    when(self.inside(z - s), lambda: self.put(self.out.at[b], b, (0 if s == -1 else 3) + d, self.zdev(-s)))
-                self.put(self.out.at[b], b, 6 + zz, self.xdev())
-                self.put(self.out.at[b], b, 10 + 2 * zz + x, self.cdev())
-            when(self.inside(zz), arrive)
-    def step_x(self, d):
-        z, x, c = self.z, self.x, self.c
-        for s in ((-1, 1) if d else (1,)):
-            zz = z + s * d
-            def arrive(zz=zz):
-                b = idx(zz, 1 - x, c)
-                self.got(b)
-                self.put(self.out.at[b], b, 10 + 2 * zz + 1 - x, self.cdev())
-            when(self.inside(zz), arrive)
-    def step_c(self, d):
-        z, x, c = self.z, self.x, self.c
-        for s in ((-1, 1) if d else (1,)):
-            zz = z + s * d
-            def arrive(zz=zz):
-                self.got(idx(zz, x, 1 - c))
-                self.got(idx(zz, 1 - x, 1 - c))
-            when(self.inside(zz), arrive)
     def from_z(self, zz):
         z, x, c = self.z, self.x, self.c
         b = idx(zz, x, c)
@@ -243,6 +224,18 @@
         when(self.inside(z + s), lambda: self.put(self.out.at[b], b, slot, (self.r, idx(z + s, x, c))))
         self.put(self.out.at[b], b, 6 + zz, self.xdev())
         self.put(self.out.at[b], b, 10 + 2 * zz + x, self.cdev())
+    def first(self):
+        self.from_z(self.p[1])
+        when(self.mid, lambda: self.from_z(self.p[2]))
+        self.from_x(self.p[0])
+    def second(self):
+        self.from_z(jnp.where(self.mid, self.p[3], self.p[2]))
+        self.from_x(self.p[1])
+    def third(self):
+        when(~self.mid, lambda: self.from_z(self.p[3]))
+        self.from_x(self.p[2])
+    def fourth(self):
+        self.from_x(self.p[3])
     def from_x(self, zz):
         b = idx(zz, 1 - self.x, self.c)
         self.got(b)
@@ -260,25 +253,25 @@
         if local:
             pltpu.make_async_copy(self.src, self.out.at[0], self.local).wait()
 
-def gather_kernel(n, with_side, *refs):
+def gather_kernel(n, *refs):
     srcs, outs = refs[:n], refs[n:2*n]
     send, recv, local = refs[2*n:]
     at = place()
     greet(*at)
     eng = [Gather(at, srcs[i], outs[i], send.at[i], recv.at[i], local.at[i]) for i in range(n)]
     for e in eng: e.begin()
-    for d in range(1, NZ):
-        for e in eng: e.step_z(d)
-        for e in eng: e.step_x(d - 1)
-    for e in eng: e.step_x(NZ - 1)
+    for e in eng: e.first()
+    for e in eng: e.second()
+    for e in eng: e.third()
+    for e in eng: e.fourth()
     for d in range(NZ):
-        for e in eng: e.step_c(d)
+        for e in eng: e.from_c(d)
     for e in eng: e.end()
 
-def gather(arrays, cid, chunks=None):
+def gather(arrays, cid):
     n = len(arrays)
     return pl.pallas_call(
-        functools.partial(gather_kernel, n, False),
+        functools.partial(gather_kernel, n),
         out_shape=[jax.ShapeDtypeStruct((16,) + a.shape, a.dtype) for a in arrays],
         in_specs=[pl.BlockSpec(memory_space=pl.ANY)] * n,
         out_specs=[pl.BlockSpec(memory_space=pl.ANY)] * n,
@@ -413,6 +406,114 @@
     )(*parts)
 
 
+KS = (8, 1, 9, 2, 10, 3, 11, 4, 12, 5, 13, 6, 14, 7, 15)
+WINDOW = 4
+
+class Deal:
+    def __init__(self, at, ws, rem, buf, send, recv, ysend, yrecv, local):
+        self.r, self.z, self.x, self.c = at
+        self.me = idx(self.z, self.x, self.c)
+        self.ws, self.rem, self.buf = ws, rem, buf
+        self.send, self.recv, self.ysend, self.yrecv, self.local = send, recv, ysend, yrecv, local
+        self.half = ws[0].shape[0] // 2
+    def rows(self, j, h):
+        n = self.half
+        return self.buf.at[pl.ds(pl.multiple_of((2 * j + h) * n, n), n)]
+    def launch(self, k):
+        r, me, n = self.r, self.me, self.half
+        row = pl.ds(pl.multiple_of(r * n, n), n)
+        j = jnp.bitwise_xor(me, k)
+        dev = (r, j)
+        dst = self.rows(me, r)
+        col = pl.ds(pl.multiple_of(j * MAIN, MAIN), MAIN)
+        for i in range(3):
+            pltpu.make_async_remote_copy(self.ws[i].at[row, col], dst.at[:, pl.ds(i * MAIN, MAIN)], self.send.at[k], self.recv.at[k], device_id=dev, device_id_type=MESH).start()
+        pltpu.make_async_remote_copy(self.rem.at[j, row], dst.at[:, pl.ds(3 * MAIN, 256)], self.send.at[k], self.recv.at[k], device_id=dev, device_id_type=MESH).start()
+    def begin(self):
+        me, n = self.me, self.half
+        for k in KS[:WINDOW]:
+            self.launch(k)
+        col = pl.ds(pl.multiple_of(me * MAIN, MAIN), MAIN)
+        own = self.buf.at[pl.ds(pl.multiple_of(2 * me * n, 2 * n), 2 * n)]
+        for i in range(3):
+            pltpu.make_async_copy(self.ws[i].at[:, col], own.at[:, pl.ds(i * MAIN, MAIN)], self.local).start()
+        pltpu.make_async_copy(self.rem.at[me], own.at[:, pl.ds(3 * MAIN, 256)], self.local).start()
+    def step(self, i):
+        k = KS[i]
+        r, me = self.r, self.me
+        j = jnp.bitwise_xor(me, k)
+        blk = self.rows(j, r)
+        dev = (1 - r, me)
+        pltpu.make_async_remote_copy(blk, blk, self.send.at[k], self.recv.at[k], device_id=dev, device_id_type=MESH).wait_recv()
+        pltpu.make_async_remote_copy(blk, blk, self.ysend.at[k], self.yrecv.at[k], device_id=dev, device_id_type=MESH).start()
+        if i + WINDOW < 15:
+            self.launch(KS[i + WINDOW])
+    def end(self):
+        r, me = self.r, self.me
+        dev = (1 - r, me)
+        for k in range(1, 16):
+            j = jnp.bitwise_xor(me, k)
+            blk = self.rows(j, 1 - r)
+            pltpu.make_async_remote_copy(blk, blk, self.ysend.at[k], self.yrecv.at[k], device_id=dev, device_id_type=MESH).wait()
+            pltpu.make_async_remote_copy(blk, blk, self.send.at[k], self.recv.at[k], device_id=dev, device_id_type=MESH).wait_send()
+        own = self.buf.at[pl.ds(pl.multiple_of(2 * me * self.half, 2 * self.half), 2 * self.half)]
+        pltpu.make_async_copy(own, own, self.local).wait()
+
+def hail_all(r, z, x, c):
+    bar = pltpu.get_barrier_semaphore()
+    me = idx(z, x, c)
+    for k in range(1, 16):
+        pl.semaphore_signal(bar, inc=1, device_id=(r, lax.rem(me + k, 16)), device_id_type=MESH)
+    pl.semaphore_signal(bar, inc=1, device_id=(1 - r, me), device_id_type=MESH)
+    pl.semaphore_wait(bar, 16)
+
+def weights_kernel(wq, wk, wv, wg, wu, wd, rem, small, qkv_out, small_out, buf, qkv_own, gs, gr, gl, ss, sr, sl, ds, dr, ys, yr, dl, lsem):
+    at = place()
+    width = wq.shape[1]
+    kw = wk.shape[1]
+    loads = [pltpu.make_async_copy(w, qkv_own.at[:, pl.ds(o, n)], lsem.at[i]) for i, (w, o, n) in enumerate(((wq, 0, width), (wk, width, kw), (wv, width + kw, kw)))]
+    for l in loads: l.start()
+    hail_all(*at)
+    for l in loads: l.wait()
+    g = Gather(at, qkv_own, qkv_out, gs, gr, gl)
+    v = Gather(at, small, small_out, ss, sr, sl)
+    d = Deal(at, (wg, wu, wd), rem, buf, ds, dr, ys, yr, dl)
+    g.begin()
+    v.begin()
+    d.begin()
+    steps = iter(range(15))
+    def some(n):
+        for _ in range(n):
+            i = next(steps, None)
+            if i is not None:
+                d.step(i)
+    for phase, n in ((lambda e: e.first(), PACE[0]), (lambda e: e.second(), PACE[1]), (lambda e: e.third(), PACE[2]), (lambda e: e.fourth(), 15)):
+        phase(g)
+        phase(v)
+        some(n)
+    for e in (g, v):
+        for zz in range(NZ):
+            e.from_c(zz)
+        e.end()
+    d.end()
+
+PACE = (2, 2, 3)
+
+def weights(wq, wk, wv, wg, wu, wd, rem, small, cid):
+    any_ = pl.BlockSpec(memory_space=pl.ANY)
+    dma = pltpu.SemaphoreType.DMA
+    rows = wq.shape[0]
+    width = wq.shape[1] + 2 * wk.shape[1]
+    return pl.pallas_call(
+        weights_kernel,
+        out_shape=[jax.ShapeDtypeStruct((16, rows, width), BF), jax.ShapeDtypeStruct((16,) + small.shape, BF), jax.ShapeDtypeStruct((16 * rows, 3 * MAIN + 256), BF)],
+        in_specs=[any_] * 8,
+        out_specs=[any_] * 3,
+        scratch_shapes=[pltpu.VMEM((rows, width), BF), dma((18,)), dma((16,)), dma(()), dma((18,)), dma((16,)), dma(())] + [dma((16,))] * 4 + [dma(()), dma((3,))],
+        compiler_params=pltpu.CompilerParams(collective_id=cid, has_side_effects=True),
+    )(wq, wk, wv, wg, wu, wd, rem, small)
+
+
 def dot(a, b):
     return lax.dot_general(a, b, (((1,), (0,)), ((), ())), preferred_element_type=F32)
 def dot_nt(a, b):
@@ -599,6 +700,32 @@
 def own_half(x, dim, rank):
     half = x.shape[dim] // 2
     return lax.dynamic_slice_in_dim(x, rank * half, half, dim)
+
+
+def spare_blocks(ff, main, spare):
+    group_count = lax.axis_size("group")
+    rows = ff[0].shape[0]
+    ends = [w[:, main * group_count :].reshape(rows, group_count, spare) for w in ff]
+    gap = jnp.zeros((rows, group_count, 128 - 2 * spare), BF)
+    gap_down = jnp.zeros((rows, group_count, 128 - spare), BF)
+    return jnp.transpose(
+        jnp.concatenate([ends[0], ends[1], gap, ends[2], gap_down], axis=2), (1, 0, 2)
+    )
+
+
+def columns_plain(ff, main, spare):
+    group_count = lax.axis_size("group")
+    replica_rank = lax.axis_index("replica")
+    rows = ff[0].shape[0]
+    mains = [w[:, : main * group_count].reshape(rows, group_count, main) for w in ff]
+    blocks = jnp.concatenate(
+        [jnp.transpose(m, (1, 0, 2)) for m in mains] + [spare_blocks(ff, main, spare)], axis=2
+    )
+    own_part = lax.all_to_all(own_half(blocks, 1, replica_rank), "group", 0, 0, tiled=True)
+    other_part = swap(own_part)
+    first = jnp.where(replica_rank == 0, own_part, other_part)
+    second = jnp.where(replica_rank == 0, other_part, own_part)
+    return jnp.concatenate((first, second), axis=1).reshape(rows * group_count, 3 * main + 256)
 
 
 def mlp_plain(normed_two, grad_all, columns, main, spare, own_rows):
@@ -707,9 +834,18 @@
     sizes = [p.shape[0] for p in pieces]
     offsets = [sum(sizes[:i]) for i in range(len(sizes) + 1)]
     small = jnp.zeros((16 * 128,), BF).at[: offsets[-1]].set(jnp.concatenate(pieces))
-    qkv_w, small = gather_all(
-        [jnp.concatenate((w_query, w_key, w_value), axis=1), small.reshape(16, 128)], 1, fast
-    )
+    main = (hidden_units // 128 // group_count) * 128
+    spare = hidden_units // group_count - main
+    ff = (w_gate, w_up, w_down)
+    if fast:
+        qkv_w, small, columns = weights(
+            w_query, w_key, w_value, *ff, spare_blocks(ff, main, spare), small.reshape(16, 128), 1
+        )
+    else:
+        qkv_w, small = gather_all(
+            [jnp.concatenate((w_query, w_key, w_value), axis=1), small.reshape(16, 128)], 1, fast
+        )
+        columns = columns_plain(ff, main, spare)
     qkv_w = qkv_w.reshape(model_width, model_width + 2 * kv_width)
     small = small.reshape(group_count, 16 * 128)
     gain_one, query_b, key_b, value_b, gain_two = [
@@ -717,25 +853,6 @@
     ]
     qkv_b = jnp.concatenate((query_b, key_b, value_b))
 
-    main = (hidden_units // 128 // group_count) * 128
-    spare = hidden_units // group_count - main
-    mains = [
-        w[:, : main * group_count].reshape(own_rows, group_count, main) for w in (w_gate, w_up, w_down)
-    ]
-    spares = [
-        w[:, main * group_count :].reshape(own_rows, group_count, spare)
-        for w in (w_gate, w_up, w_down)
-    ]
-    gap = jnp.zeros((own_rows, group_count, 128 - 2 * spare), BF)
-    gap_down = jnp.zeros((own_rows, group_count, 128 - spare), BF)
-    blocks = jnp.concatenate(mains + [spares[0], spares[1], gap, spares[2], gap_down], axis=2)
-    blocks = jnp.transpose(own_half(blocks, 0, replica_rank), (1, 0, 2))
-    own_part = lax.all_to_all(blocks, "group", 0, 0, tiled=True)
-    other_part = swap(own_part)
-    first = jnp.where(replica_rank == 0, own_part, other_part)
-    second = jnp.where(replica_rank == 0, other_part, own_part)
-    columns = jnp.concatenate((first, second), axis=1).reshape(model_width, 3 * main + 256)
-    rest = 3 * main
     grad_final = cotangent.reshape(tokens, model_width).astype(F32) * valid_rows
 
     inputs = hidden_in.reshape(tokens, model_width).astype(F32)
@@ -790,6 +907,7 @@
         grad_normed_two, mlp_out, half_sum = mlp_plain(
             normed_two, grad_all, columns, main, spare, own_rows
         )
+    rest = 3 * main
     half_back = lax.all_to_all(half_sum, "group", 0, 0, tiled=True)
     half_other = swap(half_back)
     first = jnp.where(replica_rank == 0, half_back, half_other)

time: 685 us -> 588 us (0.86)
  waiting for transfers between devices: 51.9 us -> 0.01 us
  local copies, waits for them, and re-layouts: 83.8 us -> 58.9 us
  starting transfers between devices: 17.1 us -> 4.68 us
    ppermute x2 -> x1, waiting for transfers between devices: 51.9 us -> 0.01 us  [swap(): return lax.ppermute(x, 'replica', [(0, 1), (1, 0)])]
    pallas_call x2, Pallas kernels: 129 us -> 114 us  [scatter(): pl.pallas_call(functools.partial(scatter_kernel, n, pair), out_shape=[jax...]
    all_to_all x1 -> x0, starting transfers between devices: 7.55 us -> none  [shards(): own_part = lax.all_to_all(blocks, 'group', 0, 0, tiled=True)]
  transfers between devices with their start and end apart: 4 -> 2, of which waited for: 1 -> 0; matrix products, arithmetic and copies ran while one was open for 12% -> 11% of each run, Pallas kernels for 45% -> 20%
where the time goes in v4:
time: 588 us; the launch traced here: 577 us
  Pallas kernels  440 us (75%)
  local copies, waits for them, and re-layouts  58.9 us (10%)
  matrix products  35.7 us (6%)
  other arithmetic  34 us (6%)
    pallas_call x1, Pallas kernels, mlp(): pl.pallas_call(functools.partial(mlp_kernel, spare), out_shape=[jax.Shape...  144 us
    pallas_call x2, Pallas kernels, scatter(): pl.pallas_call(functools.partial(scatter_kernel, n, pair), out_shape=[jax...  114 us
    pallas_call x1, Pallas kernels, weights(): pl.pallas_call(weights_kernel, out_shape=[jax.ShapeDtypeStruct((16, rows,...  107 us
    pallas_call x1, Pallas kernels, gather(): pl.pallas_call(functools.partial(gather_kernel, n), out_shape=[jax.ShapeD...  75 us
  transfers between devices with their start and end apart: 2, of which 0 were waited for; matrix products, arithmetic and copies ran while one was open for 11% of the time, Pallas kernels for 20%

profile of v4, /device:TPU:0, one launch (start us, length us, event | category | flops | bytes accessed | tf_op | source)
XLA Modules:
  0.0 577.3 jit_solution(2499866472088707418)
XLA Ops:
  8.6 107.2 %shard_map.254 = (bf16[16,96,2048]{2,1,0:T(8,128)(2,1)}, bf16[16,16,128]{2,1,0:T(8,128)(2,1)}, bf16[1536,1792]{1,0:T(8,128)(2,1)}) custom-call(bf16[96,1536]{1,0:T(8,128)(2,1)} %wq.1, bf16[96,256]{1,0:T(8,128)(2,1)} %wk.1, bf16[96,256]{1,0:T(8,128)(2,1)} %wv.1, bf16[96,8960]{1,0:T(8,128)(2,1)} %wg.1, bf16[96,8960]{1,0:T(8,128)(2,1)} %wu.1, ...), custom_call_target="tpu_custom_call" | custom-call | tf_op jit(solution)/shard_map/pallas_call | solution.py:507
  118.6 3.9 convolution_add_fusion.5
  126.6 75.0 %shard_map.255 = (bf16[16,128,512]{2,1,0:T(8,128)(2,1)}, bf16[16,128,1536]{2,1,0:T(8,128)(2,1)}, bf16[16,96,1536]{2,1,0:T(8,128)(2,1)}) custom-call(bf16[128,512]{1,0:T(8,128)(2,1)} %pad_maximum_fusion.1.refs_0_, bf16[128,1536]{1,0:T(8,128)(2,1)} %fusion.45.refs_1_, bf16[96,1536]{1,0:T(8,128)(2,1)} %refs_2_.1), custom_call_target="tpu_custom_call" | custom-call | tf_op jit(solution)/shard_map/pallas_call | solution.py:273
  201.7 3.1 copy.150
  204.8 2.5 reshape.691
  207.3 2.3 slice_bitcast_fusion.3
  212.6 2.2 while.58
  217.2 2.3 while.57
  222.8 4.2 multiply_reduce_fusion.2
  229.0 143.7 %shard_map.256 = (f32[128,1536]{1,0:T(8,128)}, f32[128,1536]{1,0:T(8,128)}, bf16[16,48,1792]{2,1,0:T(8,128)(2,1)}) custom-call(bf16[128,1536]{1,0:T(8,128)(2,1)} %multiply_convert_fusion.1.n2_ref, bf16[16,128,1536]{2,1,0:T(8,128)(2,1)} %get-tuple-element.274.cot_ref, bf16[1536,1792]{1,0:T(8,128)(2,1)} %get-tuple-element.275.w_ref), custom_call_target="tpu_custom_call" | custom-call | tf_op jit(solution)/shard_map/pallas_call | solution.py:659
  372.8 4.6 all-to-all-start
  379.5 2.4 fusion.44
  381.8 4.2 fusion.66
  389.2 6.9 %while.59 = (s32[]{:T(128)}, f32[2,384,128]{2,1,0:T(8,128)S(1)}, f32[1024,2,128]{2,0,1:T(8,128)S(1)}, f32[1024,2,128]{2,0,1:T(8,128)}, s32[]{:T(128)}, /*index=5...) while((s32[]{:T(128)}, f32[2,384,128]{2,1,0:T(8,128)S(1)}, ...), condition=%wide.region_11.12_spmd.clone, body=%wide.region_10.11_spmd.clone.sunk | while | flops 506430976 | bytes 14051867 | solution.py:149
  393.9 2.2 fusion.169
  399.0 5.5 while.60
  402.1 2.2 fusion.182
  413.3 37.1 %shard_map.257 = f32[128,512]{1,0:T(8,128)} custom-call(bf16[16,128,512]{2,1,0:T(8,128)(2,1)} %bitcast.295), custom_call_target="tpu_custom_call" | custom-call | tf_op jit(solution)/shard_map/pallas_call | solution.py:399
  455.5 5.2 fusion.56
  461.6 3.6 convolution_convert_fusion.1
  465.3 4.5 convolution_convert_fusion
  469.8 76.6 %shard_map.258 = (f32[96,2048]{1,0:T(8,128)}, f32[96,1536]{1,0:T(8,128)}, f32[16,128]{1,0:T(8,128)}) custom-call(bf16[16,96,2048]{2,1,0:T(8,128)(2,1)} %bitcast.286, bf16[16,96,1536]{2,1,0:T(8,128)(2,1)} %bitcast.287, bf16[16,16,128]{2,1,0:T(8,128)(2,1)} %bitcast.331), custom_call_target="tpu_custom_call" | custom-call | tf_op jit(solution)/shard_map/pallas_call | solution.py:399
  553.9 3.0 broadcast_select_fusion.1
  569.0 3.0 maximum_convert_fusion.2
  (273 shorter events, 82.4 us)
Async XLA Ops:
  0.6 4.7 slice-start.1
  0.7 5.1 copy-start.37
  0.7 5.1 copy-start.38
  0.7 5.1 copy-start.39
  0.7 5.1 copy-start.40
  0.7 5.1 copy-start.41
  8.6 109.2 %copy-start.13 = (bf16[2,64,1536]{2,1,0:T(8,128)(2,1)S(1)}, bf16[2,64,1536]{2,1,0:T(8,128)(2,1)}, u32[]{:S(2)}) copy-start(bf16[2,64,1536]{2,1,0:T(8,128)(2,1)} %param.25) | copy-start | bytes 1179652
  122.5 3.3 copy-start.16
  122.5 3.2 copy-start.23
  212.5 3.5 copy-start.21
  219.6 153.2 %copy-start.4 = (bf16[1024,2,128]{2,0,1:T(8,128)(2,1)}, bf16[1024,2,128]{2,0,1:T(8,128)(2,1)S(1)}, u32[]{:S(2)}) copy-start(bf16[1024,2,128]{2,0,1:T(8,128)(2,1)S(1)} %get-tuple-element.1107) | copy-start | bytes 1572868
  219.6 3.1 copy-start.14
  222.7 4.2 copy-start.17
  222.8 4.2 copy-start.32
  372.7 4.7 copy-start.8
  372.8 6.7 %copy-start.24 = (bf16[2,64,1536]{2,1,0:T(8,128)(2,1)S(1)}, bf16[2,64,1536]{2,1,0:T(8,128)(2,1)}, u32[]{:S(2)}) copy-start(bf16[2,64,1536]{2,1,0:T(8,128)(2,1)} %param.39) | copy-start | bytes 1179652
  372.8 82.6 %all-to-all-start = ((bf16[16,48,1792]{2,1,0:T(8,128)(2,1)}), bf16[16,48,1792]{2,1,0:T(8,128)(2,1)}, u32[]{:S(2)}, u32[]{:S(2)}) async-start(bf16[16,48,1792]{2,1,0:T(8,128)(2,1)} %get-tuple-element.287), calls=%async_computation | async-start | bytes 5505024 | tf_op jit(solution)/shard_map/all_to_all | solution.py:911
  381.8 4.3 copy-start.6
  413.3 38.9 %copy-start.36 = (f32[2,64]{1,0:T(2,128)S(1)}, f32[2,64]{1,0:T(2,128)}, u32[]{:S(2)}) copy-start(f32[2,64]{1,0:T(2,128)} %copy-done.35) | copy-start | bytes 1540
  413.3 39.0 %copy-start.1 = (f32[2,384,128]{2,1,0:T(8,128)S(1)}, f32[2,384,128]{2,1,0:T(8,128)}, u32[]{:S(2)}) copy-start(f32[2,384,128]{2,1,0:T(8,128)} %copy-done) | copy-start | bytes 1179652
  455.3 5.4 copy-start.33
  455.3 6.3 %copy-start.7 = (f32[128,1536]{1,0:T(8,128)S(1)}, f32[128,1536]{1,0:T(8,128)}, u32[]{:S(2)}) copy-start(f32[128,1536]{1,0:T(8,128)} %copy-done.6) | copy-start | bytes 2359300
  455.4 6.3 %copy-start.18 = (bf16[128,1536]{1,0:T(8,128)(2,1)S(1)}, bf16[128,1536]{1,0:T(8,128)(2,1)}, u32[]{:S(2)}) copy-start(bf16[128,1536]{1,0:T(8,128)(2,1)} %copy-done.17) | copy-start | bytes 1179652
  455.4 98.5 %collective-permute-start = (bf16[16,48,1792]{2,1,0:T(8,128)(2,1)}, bf16[16,48,1792]{2,1,0:T(8,128)(2,1)}, u32[]{:S(2)}, u32[]{:S(2)}) collective-permute-start(bf16[16,48,1792]{2,1,0:T(8,128)(2,1)} %all-to-all-done), channel_id=1, source_target_pairs={{0,16},{16,0},{1,17},{17,1},{2,18},{18,2},{3,19},{19,3},{4,20},{20... | collective-permute-start | bytes 8257544 | tf_op jit(solution)/shard_map/ppermute | solution.py:680
  (22 other events, 35.4 us)

commit v5 on v4

--- a/solution.py
+++ b/solution.py
@@ -10,6 +10,8 @@
 MESH = pl.DeviceIdType.MESH
 NZ = 4
 MAIN = 512
+D = 1536
+COLS = 3 * MAIN + 256
 HEADS = 12
 KV_HEADS = 2
 HEAD_DIM = 128
@@ -149,8 +151,235 @@
     return lax.fori_loop(0, block_total(length, rank_end, key_step), visit, initial)
 
 
-D = 1536
-COLS = 3 * MAIN + 256
+def gather_plain(x):
+    return lax.all_gather(x, "group", axis=0, tiled=True)
+
+
+def scatter_sum(x):
+    return lax.psum_scatter(x, "group", scatter_dimension=0, tiled=True)
+
+
+def shards_plain(
+    hidden_in,
+    lengths,
+    gain_attn,
+    w_query,
+    b_query,
+    w_key,
+    b_key,
+    w_value,
+    b_value,
+    w_out,
+    gain_mlp,
+    w_gate,
+    w_up,
+    w_down,
+    cotangent,
+):
+    group_count = lax.axis_size("group")
+    group_rank = lax.axis_index("group")
+    slot_count, block_len, model_width = hidden_in.shape
+    kv_heads = KV_HEADS
+    head_dim = HEAD_DIM
+    kv_width = kv_heads * head_dim
+    repeat = HEADS // kv_heads
+    slot_span = block_len * group_count
+    key_step = min(512, slot_span)
+    score_scale = head_dim ** (-0.5)
+    tokens = slot_count * block_len
+    hidden_units = w_gate.shape[1]
+    own_rows = w_gate.shape[0]
+    share = hidden_units // group_count
+    positions = group_rank * block_len + jnp.arange(block_len, dtype=jnp.int32)
+    valid_rows = (positions[None, :] < lengths[:, None]).astype(F32).reshape(tokens, 1)
+    cos_table, sin_table = rope_tables(positions, head_dim)
+    cos_heads = cos_table[:, None, :]
+    sin_heads = sin_table[:, None, :]
+    rank_end = (group_rank + 1) * block_len
+    row_pos = jnp.tile(positions, repeat)
+
+    pieces = (gain_attn, b_query, b_key, b_value, gain_mlp)
+    sizes = [p.shape[0] for p in pieces]
+    small = gather_plain(jnp.concatenate(pieces)[None])
+    offsets = [sum(sizes[:i]) for i in range(len(sizes) + 1)]
+    gain_one, query_b, key_b, value_b, gain_two = [
+        small[:, offsets[i] : offsets[i + 1]].reshape(-1).astype(F32) for i in range(len(sizes))
+    ]
+    qkv_w = gather_plain(jnp.concatenate((w_query, w_key, w_value), axis=1))
+    out_w = gather_plain(w_out)
+    qkv_b = jnp.concatenate((query_b, key_b, value_b))
+
+    stacked = jnp.stack((w_gate, w_up, w_down)).reshape(3, own_rows, group_count, share)
+    stacked = jnp.transpose(stacked, (2, 1, 0, 3)).reshape(group_count, own_rows, 3 * share)
+    columns = lax.all_to_all(stacked, "group", 0, 0, tiled=True).reshape(model_width, 3 * share)
+    gate_up_w = columns[:, : 2 * share]
+    down_w = columns[:, 2 * share :]
+
+    grad_final = cotangent.reshape(tokens, model_width).astype(F32) * valid_rows
+    grad_all = gather_plain(grad_final.astype(BF))
+
+    inputs = hidden_in.reshape(tokens, model_width).astype(F32)
+    normed_full, factor_one = normalize(inputs, gain_one)
+    normed = normed_full.astype(BF)
+    qkv = matmul(normed, qkv_w) + qkv_b
+    query_rot = rotate(
+        qkv[:, :model_width].reshape(slot_count, block_len, HEADS, head_dim), cos_heads, sin_heads
+    ).astype(BF)
+    key_rot = rotate(
+        qkv[:, model_width : model_width + kv_width].reshape(
+            slot_count, block_len, kv_heads, head_dim
+        ),
+        cos_heads,
+        sin_heads,
+    ).astype(BF)
+    value_low = qkv[:, model_width + kv_width :].astype(BF)
+    pair = jnp.concatenate(
+        (key_rot.reshape(tokens, kv_width), value_low), axis=1
+    ).reshape(1, slot_count, block_len, 2 * kv_width)
+    pair_all = jnp.transpose(gather_plain(pair), (1, 0, 2, 3)).reshape(
+        slot_count, slot_span, 2, kv_heads, head_dim
+    )
+    key_all = pair_all[:, :, 0]
+    value_all = pair_all[:, :, 1]
+    query_groups = []
+    slot_totals = []
+    slot_attended = []
+    attended_rows = []
+    for s in range(slot_count):
+        query_rows = arrange(query_rot[s], kv_heads)
+        totals, numerator = attend_forward(
+            query_rows, key_all[s], value_all[s], row_pos, lengths[s], rank_end, key_step, score_scale
+        )
+        attended = numerator / totals[..., None]
+        query_groups.append(query_rows)
+        slot_totals.append(totals)
+        slot_attended.append(attended)
+        attended_rows.append(restore(attended, block_len))
+    attended_low = jnp.concatenate(attended_rows, axis=0).astype(BF)
+    residual_mid = inputs + matmul(attended_low, out_w)
+    normed_two_full, factor_two = normalize(residual_mid, gain_two)
+    normed_all = gather_plain(normed_two_full.astype(BF))
+
+    pre = matmul(normed_all, gate_up_w)
+    gate_pre = pre[:, :share]
+    up_pre = pre[:, share:]
+    sigmoid_gate = jax.nn.sigmoid(gate_pre)
+    silu_gate = gate_pre * sigmoid_gate
+    hidden = (silu_gate * up_pre).astype(BF)
+    grad_hidden = matmul(grad_all, down_w)
+    grad_gate = (
+        grad_hidden * up_pre * (sigmoid_gate * (1.0 + gate_pre * (1.0 - sigmoid_gate)))
+    ).astype(BF)
+    grad_up = (grad_hidden * silu_gate).astype(BF)
+    gate_up_grad = jnp.concatenate((grad_gate, grad_up), axis=1)
+    grad_normed_two = scatter_sum(matmul_nt(gate_up_grad, gate_up_w).astype(BF)).astype(F32)
+    mlp_out = scatter_sum(matmul_nt(hidden, down_w).astype(BF)).astype(F32)
+    down_term = matmul_tn(grad_all, hidden)
+    gate_up_term = matmul_tn(normed_all, gate_up_grad)
+    terms = jnp.concatenate((gate_up_term, down_term), axis=1).astype(BF)
+    back = lax.all_to_all(
+        terms.reshape(group_count, own_rows, 3 * share), "group", 0, 0, tiled=True
+    )
+    summed = back.astype(F32) + lax.ppermute(back, "replica", [(0, 1), (1, 0)]).astype(F32)
+    summed = jnp.transpose(summed.reshape(group_count, own_rows, 3, share), (2, 1, 0, 3))
+    gate_sum, up_sum, down_sum = summed.reshape(3, own_rows, hidden_units)
+
+    final_rows = residual_mid + mlp_out
+    layer_out = (final_rows * valid_rows).reshape(slot_count, block_len, model_width).astype(BF)
+    grad_mid_norm, grad_gain_two = norm_back(residual_mid, factor_two, gain_two, grad_normed_two)
+    grad_mid = grad_final + grad_mid_norm
+    grad_branch = grad_mid.astype(BF)
+    out_term = matmul_tn(attended_low, grad_branch)
+    grad_attended = matmul_nt(grad_branch, out_w)
+    grad_query_rows = []
+    grad_pairs = []
+    for s in range(slot_count):
+        slot_grad = grad_attended[s * block_len : (s + 1) * block_len].reshape(
+            block_len, HEADS, head_dim
+        )
+        grad_out = arrange(slot_grad, kv_heads)
+        totals = slot_totals[s]
+        grad_total = -jnp.sum(grad_out * slot_attended[s], axis=-1) / totals
+        grad_numer = (grad_out / totals[..., None]).astype(BF)
+        grad_query, grad_key, grad_value = attend_backward(
+            query_groups[s],
+            key_all[s],
+            value_all[s],
+            row_pos,
+            lengths[s],
+            rank_end,
+            key_step,
+            score_scale,
+            grad_numer,
+            grad_total,
+        )
+        query_back_rows = restore(grad_query * score_scale, block_len).reshape(
+            block_len, HEADS, head_dim
+        )
+        grad_query_rows.append(
+            rotate_back(query_back_rows, cos_heads, sin_heads).reshape(block_len, HEADS * head_dim)
+        )
+        grad_pairs.append(
+            jnp.concatenate(
+                (grad_key.reshape(slot_span, kv_width), grad_value.reshape(slot_span, kv_width)),
+                axis=1,
+            )
+        )
+    pair_grads = jnp.stack(grad_pairs).reshape(slot_count, group_count, block_len, 2 * kv_width)
+    pair_grads = jnp.transpose(pair_grads, (1, 0, 2, 3)).astype(BF)
+    pair_sum = scatter_sum(pair_grads).reshape(slot_count, block_len, 2 * kv_width).astype(F32)
+    grad_query_pre = jnp.concatenate(grad_query_rows, axis=0).astype(BF)
+    key_sum = pair_sum[..., :kv_width].reshape(slot_count, block_len, kv_heads, head_dim)
+    grad_key_pre = (
+        rotate_back(key_sum * score_scale, cos_heads, sin_heads).astype(BF).reshape(tokens, kv_width)
+    )
+    grad_value_pre = pair_sum[..., kv_width:].astype(BF).reshape(tokens, kv_width)
+    grad_qkv = jnp.concatenate((grad_query_pre, grad_key_pre, grad_value_pre), axis=1)
+    grad_normed = matmul_nt(grad_qkv, qkv_w)
+    grad_in_norm, grad_gain_one = norm_back(inputs, factor_one, gain_one, grad_normed)
+    grad_input = (grad_mid + grad_in_norm).reshape(slot_count, block_len, model_width)
+    qkv_term = matmul_tn(normed, grad_qkv)
+    qkv_bias = jnp.sum(grad_qkv.astype(F32), axis=0)
+
+    weight_share = scatter_sum(
+        jnp.concatenate((qkv_term, out_term), axis=1).astype(BF)
+    )
+    weight_sum = weight_share.astype(F32) + lax.ppermute(
+        weight_share, "replica", [(0, 1), (1, 0)]
+    ).astype(F32)
+    vectors = jnp.concatenate(
+        [
+            grad_gain_one.reshape(group_count, -1),
+            qkv_bias[:model_width].reshape(group_count, -1),
+            qkv_bias[model_width : model_width + kv_width].reshape(group_count, -1),
+            qkv_bias[model_width + kv_width :].reshape(group_count, -1),
+            grad_gain_two.reshape(group_count, -1),
+        ],
+        axis=1,
+    )
+    vector_sum = lax.psum(scatter_sum(vectors), "replica").reshape(-1)
+    gain_one_sum, query_bias_sum, key_bias_sum, value_bias_sum, gain_two_sum = [
+        vector_sum[offsets[i] : offsets[i + 1]] for i in range(len(sizes))
+    ]
+    ends = (0, model_width, model_width + kv_width, model_width + 2 * kv_width)
+    query_sum, key_sum_w, value_sum_w = [weight_sum[:, ends[i] : ends[i + 1]] for i in range(3)]
+    out_sum = weight_sum[:, ends[3] :]
+    return (
+        layer_out,
+        grad_input,
+        gain_one_sum,
+        query_sum,
+        query_bias_sum,
+        key_sum_w,
+        key_bias_sum,
+        value_sum_w,
+        value_bias_sum,
+        out_sum,
+        gain_two_sum,
+        gate_sum,
+        up_sum,
+        down_sum,
+    )
 
 
 def place():
@@ -670,36 +899,333 @@
     )(n2, cot, w)
 
 
-def gather_all(arrays, cid, fast):
-    if fast:
-        return gather(arrays, cid)
-    return [lax.all_gather(a, "group", axis=0) for a in arrays]
-
-
-def swap(x):
-    return lax.ppermute(x, "replica", [(0, 1), (1, 0)])
-
-
-def scatter_all(parts, cid, fast, pair=False):
-    if fast:
-        return scatter(parts, cid, pair)
-    sums = [
-        lax.psum_scatter(p, "group", scatter_dimension=0, tiled=True)[0].astype(F32) for p in parts
-    ]
-    if pair:
-        low = [p.astype(BF) for p in sums]
-        sums = [p.astype(F32) + swap(p).astype(F32) for p in low]
-    return sums
-
-
-def other_half(x, dim, rank):
-    half = x.shape[dim] // 2
-    return lax.dynamic_slice_in_dim(x, (1 - rank) * half, half, dim)
-
-
-def own_half(x, dim, rank):
-    half = x.shape[dim] // 2
-    return lax.dynamic_slice_in_dim(x, rank * half, half, dim)
+def spin(u, cos, sin):
+    return u * cos + pltpu.roll(u, HEAD_DIM // 2, 1) * sin
+
+def stack_heads(v):
+    n = v.shape[1] // HEAD_DIM
+    return jnp.concatenate([v[:, HEAD_DIM * i : HEAD_DIM * (i + 1)] for i in range(n)], axis=0)
+
+def spread_heads(v, rows):
+    n = v.shape[0] // rows
+    return jnp.concatenate([v[rows * i : rows * (i + 1)] for i in range(n)], axis=1)
+
+def exp_scores(q, k, first_row, block, length):
+    sc = dot_nt(q, k) * (HEAD_DIM ** -0.5)
+    key = lax.broadcasted_iota(jnp.int32, sc.shape, 1)
+    row = jnp.bitwise_and(lax.broadcasted_iota(jnp.int32, sc.shape, 0), block - 1) + first_row
+    return jnp.where((key <= row) & (key < length), jnp.exp(sc), 0.0)
+
+def rms(v, gain):
+    factor = lax.rsqrt(jnp.mean(v * v, axis=-1, keepdims=True) + EPSILON)
+    return v * factor * gain
+
+def attend_kernel(block, lens, x_ref, cot_ref, wqkv_ref, wo_ref, vec, cos_ref, sin_ref,
+                  q_out, normed_out, att_out, mid_out, n2_out, kv_out, cot_out, wo_out,
+                  wqkv, own, kv, wo, cs, cr, cl, ws, wr, wl, ks, kr, kl, lsem):
+    at = place()
+    width = HEADS * HEAD_DIM
+    kw = KV_HEADS * HEAD_DIM
+    load = pltpu.make_async_copy(wqkv_ref, wqkv, lsem.at[0])
+    load.start()
+    greet(*at)
+    gc = Gather(at, cot_ref, cot_out, cs, cr, cl)
+    gw = Gather(at, wo_ref, wo, ws, wr, wl)
+    gk = Gather(at, own, kv, ks, kr, kl)
+    gw.begin()
+    gc.begin()
+    x = x_ref[...].astype(F32)
+    normed_out[...] = rms(x, vec[0:1, :width]).astype(BF)
+    load.wait()
+    cos, sin = cos_ref[...], sin_ref[...]
+    def product(base):
+        return dot(normed_out[...], wqkv[:, pl.ds(pl.multiple_of(base, 256), 256)]) + vec[1:2, pl.ds(pl.multiple_of(base, 256), 256)]
+    pre = product(width)
+    own[:, :HEAD_DIM] = spin(pre[:, :HEAD_DIM], cos, sin).astype(BF)
+    own[:, HEAD_DIM : 2 * HEAD_DIM] = spin(pre[:, HEAD_DIM:], cos, sin).astype(BF)
+    own[:, kw:] = product(width + kw).astype(BF)
+    gk.begin()
+    @pl.loop(0, width // 256)
+    def _(t):
+        pre = product(t * 256)
+        for i in range(2):
+            col = pl.ds(pl.multiple_of(256 * t + HEAD_DIM * i, HEAD_DIM), HEAD_DIM)
+            q_out[:, col] = spin(pre[:, HEAD_DIM * i : HEAD_DIM * (i + 1)], cos, sin).astype(BF)
+    gk.first()
+    gw.first()
+    gc.first()
+    gk.second()
+    gw.second()
+    gc.second()
+    gk.third()
+    gk.fourth()
+    gw.third()
+    gc.third()
+    for zz in range(NZ):
+        gk.from_c(zz)
+    gk.end()
+    pltpu.make_async_copy(kv, kv_out, lsem.at[1]).start()
+    first_row = lax.axis_index("group") * block
+    span = 16 * block
+    @pl.loop(0, 4)
+    def _(u):
+        s, h = u // 2, lax.rem(u, 2)
+        rows = pl.ds(pl.multiple_of(block * s, block), block)
+        cols = pl.ds(pl.multiple_of(width // 2 * h, width // 2), width // 2)
+        q = stack_heads(q_out[rows, cols])
+        k = kv[:, rows, pl.ds(pl.multiple_of(HEAD_DIM * h, HEAD_DIM), HEAD_DIM)].reshape(span, HEAD_DIM)
+        v = kv[:, rows, pl.ds(pl.multiple_of(kw + HEAD_DIM * h, HEAD_DIM), HEAD_DIM)].reshape(span, HEAD_DIM)
+        e = exp_scores(q, k, first_row, block, lens[s])
+        total = jnp.sum(e, axis=-1, keepdims=True)
+        att_out[rows, cols] = spread_heads(dot(e.astype(BF), v) / total, block)
+    gw.fourth()
+    gc.fourth()
+    for zz in range(NZ):
+        gw.from_c(zz)
+    gw.end()
+    out_copy = pltpu.make_async_copy(wo, wo_out, lsem.at[2])
+    out_copy.start()
+    @pl.loop(0, width // 256)
+    def _(t):
+        col = pl.ds(pl.multiple_of(256 * t, 256), 256)
+        mid_out[:, col] = x_ref[:, col].astype(F32) + dot(att_out[...].astype(BF), wo[:, :, col].reshape(width, 256))
+    n2_out[...] = rms(mid_out[...], vec[2:3, :width]).astype(BF)
+    for zz in range(NZ):
+        gc.from_c(zz)
+    gc.end()
+    pltpu.make_async_copy(kv, kv_out, lsem.at[1]).wait()
+    out_copy.wait()
+
+def attend(lens, x, cot, wqkv, wo, vec, cos, sin, block, cid):
+    rows, width = x.shape
+    any_ = pl.BlockSpec(memory_space=pl.ANY)
+    vm = pl.BlockSpec(memory_space=pltpu.VMEM)
+    dma = pltpu.SemaphoreType.DMA
+    act = (rows, width)
+    kvw = 2 * KV_HEADS * HEAD_DIM
+    sds = jax.ShapeDtypeStruct
+    return pl.pallas_call(
+        functools.partial(attend_kernel, block),
+        out_shape=[sds(act, BF), sds(act, BF), sds(act, F32), sds(act, F32), sds(act, BF), sds((16, rows, kvw), BF), sds((16,) + act, BF), sds((16,) + wo.shape, BF)],
+        in_specs=[pl.BlockSpec(memory_space=pltpu.SMEM), vm, any_, any_, any_, vm, vm, vm],
+        out_specs=[vm] * 5 + [any_] * 3,
+        scratch_shapes=[pltpu.VMEM(wqkv.shape, BF), pltpu.VMEM((rows, kvw), BF), pltpu.VMEM((16, rows, kvw), BF), pltpu.VMEM((16,) + wo.shape, BF)]
+        + [dma((18,)), dma((16,)), dma(())] * 3 + [dma((3,))],
+        compiler_params=pltpu.CompilerParams(collective_id=cid, has_side_effects=True, vmem_limit_bytes=60 * 2**20),
+    )(lens, x, cot, wqkv, wo, vec, cos, sin)
+
+
+class Return:
+    def __init__(self, at, half_ref, main, spare, send, recv, ysend, yrecv, local):
+        self.r, self.z, self.x, self.c = at
+        self.me = idx(self.z, self.x, self.c)
+        self.src, self.main, self.spare = half_ref, main, spare
+        self.send, self.recv, self.ysend, self.yrecv, self.local = send, recv, ysend, yrecv, local
+        self.n = half_ref.shape[1]
+    def places(self, j, h):
+        row = pl.ds(pl.multiple_of(h * self.n, self.n), self.n)
+        col = pl.ds(pl.multiple_of(j * MAIN, MAIN), MAIN)
+        return [self.main.at[i, row, col] for i in range(3)] + [self.spare.at[j, row]]
+    def parts(self, j):
+        return [self.src.at[j, :, pl.ds(i * MAIN, MAIN)] for i in range(3)] + [self.src.at[j, :, pl.ds(3 * MAIN, 256)]]
+    def launch(self, k):
+        j = jnp.bitwise_xor(self.me, k)
+        for a, b in zip(self.parts(j), self.places(self.me, self.r)):
+            pltpu.make_async_remote_copy(a, b, self.send.at[k], self.recv.at[k], device_id=(self.r, j), device_id_type=MESH).start()
+    def forward(self, j, k):
+        for a in self.places(j, self.r):
+            pltpu.make_async_remote_copy(a, a, self.ysend.at[k], self.yrecv.at[k], device_id=(1 - self.r, self.me), device_id_type=MESH).start()
+    def begin(self, window):
+        self.window = window
+        for a, b in zip(self.parts(self.me), self.places(self.me, self.r)):
+            pltpu.make_async_copy(a, b, self.local).start()
+        for k in KS[:window]:
+            self.launch(k)
+    def whole(self, send, recv):
+        blk = self.src.at[0]
+        return pltpu.make_async_remote_copy(blk, blk, send, recv, device_id=(1 - self.r, self.me), device_id_type=MESH)
+    def own(self):
+        pltpu.make_async_copy(self.src.at[0], self.src.at[0], self.local).wait()
+        self.forward(self.me, 0)
+    def step(self, i):
+        k = KS[i]
+        self.whole(self.send.at[k], self.recv.at[k]).wait_recv()
+        self.forward(jnp.bitwise_xor(self.me, k), k)
+        if i + self.window < 15:
+            self.launch(KS[i + self.window])
+    def end(self):
+        for k in (0,) + KS:
+            self.whole(self.ysend.at[k], self.yrecv.at[k]).wait()
+            if k:
+                self.whole(self.send.at[k], self.recv.at[k]).wait_send()
+
+def norm_gradient(v, gain, upstream):
+    factor = lax.rsqrt(jnp.mean(v * v, axis=-1, keepdims=True) + EPSILON)
+    weighted = upstream * gain
+    inner = jnp.mean(weighted * v, axis=-1, keepdims=True)
+    return factor * weighted - v * (factor * factor * factor) * inner, jnp.sum(upstream * v * factor, axis=0, keepdims=True)
+
+def backward_kernel(block, window, lens, gn2, mlp_out, mid, cot, x_ref, att, q_ref, normed, vec, cos_ref, sin_ref, valid, sel, fold, selk, foldk, kv_ref, wo_ref, wqkv_ref, half_ref,
+                    layer_out, grad_input, qkv_out, wo_out, vec_out, g_main, g_spare,
+                    kv, wo, wqkv, gmid, branch, gatt, gqkv, pv,
+                    p_kv, c_kv, x_kv, z_kv, p_wo, c_wo, x_wo, z_wo, p_qk, c_qk, x_qk, z_qk, p_ve, c_ve, x_ve, z_ve,
+                    kvsum, y0, y1, y2, y3, y4, y5,
+                    ss, sc, sx, sz, rs, rr, rys, ryr, rl, ysem, lsem):
+    at = place()
+    r, z, x, c = at
+    width = HEADS * HEAD_DIM
+    kw = KV_HEADS * HEAD_DIM
+    loads = [pltpu.make_async_copy(a, b, lsem.at[i]) for i, (a, b) in enumerate(((wo_ref, wo), (kv_ref, kv), (wqkv_ref, wqkv)))]
+    for l in loads: l.start()
+    hail_all(*at)
+    back = Return(at, half_ref, g_main, g_spare, rs, rr, rys, ryr, rl)
+    back.begin(window)
+    sets = ((p_kv, c_kv, x_kv, z_kv), (p_wo, c_wo, x_wo, z_wo), (p_qk, c_qk, x_qk, z_qk), (p_ve, c_ve, x_ve, z_ve))
+    ek, eo, eq, ev = [Scatter(at, *b, ss.at[i], sc.at[i], sx.at[i], sz.at[i]) for i, b in enumerate(sets)]
+    steps = iter(range(15))
+    def some(n):
+        for _ in range(n):
+            i = next(steps, None)
+            if i is not None:
+                back.step(i)
+    ydev = (1 - r, idx(z, x, c))
+    def trade(i, out, a, b):
+        a[...] = out[...].astype(BF)
+        pltpu.make_async_remote_copy(a, b, ysem.at[2 * i], ysem.at[2 * i + 1], device_id=ydev, device_id_type=MESH).start()
+    def traded(i, out, a, b):
+        pltpu.make_async_remote_copy(a, b, ysem.at[2 * i], ysem.at[2 * i + 1], device_id=ydev, device_id_type=MESH).wait()
+        out[...] = a[...].astype(F32) + b[...].astype(F32)
+
+    grad_norm, gain_two = norm_gradient(mid[...], vec[2:3, :width], gn2[...])
+    gmid[...] = cot[...].astype(F32) + grad_norm
+    branch[...] = gmid[...].astype(BF)
+    loads[0].wait()
+    @pl.loop(0, 4)
+    def _(t):
+        blocks = pl.ds(pl.multiple_of(4 * t, 4), 4)
+        col = pl.ds(pl.multiple_of(384 * t, 384), 384)
+        low = att[:, col].astype(BF)
+        p_wo[blocks] = dot_tn(low, branch[...]).astype(BF).reshape(4, 96, width)
+        gatt[:, col] = dot_nt(branch[...], wo[blocks].reshape(384, width))
+    eo.begin()
+    eo.step_x(3)
+    eo.step_x(2)
+    back.own()
+    layer_out[...] = ((mid[...] + mlp_out[...]) * valid[...]).astype(BF)
+    loads[1].wait()
+    first_row = lax.axis_index("group") * block
+    span = 16 * block
+    def unit(u):
+        s, h = u // 2, lax.rem(u, 2)
+        rows = pl.ds(pl.multiple_of(block * s, block), block)
+        cols = pl.ds(pl.multiple_of(width // 2 * h, width // 2), width // 2)
+        kcol = pl.ds(pl.multiple_of(HEAD_DIM * h, HEAD_DIM), HEAD_DIM)
+        vcol = pl.ds(pl.multiple_of(kw + HEAD_DIM * h, HEAD_DIM), HEAD_DIM)
+        q = stack_heads(q_ref[rows, cols])
+        k = kv[:, rows, kcol].reshape(span, HEAD_DIM)
+        v = kv[:, rows, vcol].reshape(span, HEAD_DIM)
+        e = exp_scores(q, k, first_row, block, lens[s])
+        total = jnp.sum(e, axis=-1, keepdims=True)
+        ga = stack_heads(gatt[rows, cols])
+        gt = -jnp.sum(ga * stack_heads(att[rows, cols]), axis=-1, keepdims=True) / total
+        gn = (ga / total).astype(BF)
+        gs = (e * (dot_nt(gn, v) + gt)).astype(BF)
+        p_kv[:, rows, kcol] = dot_tn(gs, q).astype(BF).reshape(16, block, HEAD_DIM)
+        p_kv[:, rows, vcol] = dot_tn(e.astype(BF), gn).astype(BF).reshape(16, block, HEAD_DIM)
+        gq = dot(gs, k) * (HEAD_DIM ** -0.5)
+        cos, sin = cos_ref[:block], sin_ref[:block]
+        gqkv[rows, cols] = jnp.concatenate([spin(gq[block * i : block * (i + 1)], cos, -sin) for i in range(HEADS // KV_HEADS)], axis=1).astype(BF)
+    unit(0)
+    some(1)
+    eo.step_z(3)
+    eo.step_x(1)
+    unit(1)
+    some(1)
+    eo.step_z(2)
+    eo.step_x(0)
+    unit(2)
+    some(1)
+    eo.step_z(1)
+    unit(3)
+    ek.begin()
+    some(1)
+    ek.step_x(3)
+    ek.step_x(2)
+    eo.finish(wo_out)
+    trade(0, wo_out, y0, y1)
+    some(1)
+    ek.step_z(3)
+    ek.step_x(1)
+    some(1)
+    ek.step_z(2)
+    ek.step_x(0)
+    some(1)
+    ek.step_z(1)
+    some(1)
+    ek.finish(kvsum)
+    cos, sin = cos_ref[...], sin_ref[...]
+    for h in range(KV_HEADS):
+        kcol = slice(HEAD_DIM * h, HEAD_DIM * (h + 1))
+        gqkv[:, width + HEAD_DIM * h : width + HEAD_DIM * (h + 1)] = spin(kvsum[:, kcol] * (HEAD_DIM ** -0.5), cos, -sin).astype(BF)
+    gqkv[:, width + kw :] = kvsum[:, kw:].astype(BF)
+    loads[2].wait()
+    @pl.loop(0, 4)
+    def _(t):
+        blocks = pl.ds(pl.multiple_of(4 * t, 4), 4)
+        col = pl.ds(pl.multiple_of(384 * t, 384), 384)
+        p_qk[blocks] = dot_tn(normed[:, col], gqkv[...]).astype(BF).reshape(4, 96, width + 2 * kw)
+        gatt[:, col] = dot_nt(gqkv[...], wqkv[blocks].reshape(384, width + 2 * kw))
+    eq.begin()
+    eq.step_x(3)
+    eq.step_x(2)
+    grad_norm, gain_one = norm_gradient(x_ref[...].astype(F32), vec[0:1, :width], gatt[...])
+    grad_input[...] = gmid[...] + grad_norm
+    bias = jnp.sum(gqkv[...].astype(F32), axis=0, keepdims=True)
+    pv[...] = jnp.zeros_like(pv)
+    for i, (v, a, b) in enumerate(((gain_one, sel, fold), (bias[:, :width], sel, fold), (bias[:, width : width + kw], selk, foldk), (bias[:, width + kw :], selk, foldk), (gain_two, sel, fold))):
+        pv[:, i, :] = dot((a[...] * v).astype(BF), b[...])
+    p_ve[...] = pv[...].astype(BF)
+    ev.begin()
+    ev.step_x(3)
+    ev.step_x(2)
+    some(2)
+    for kind, d in (("z", 3), ("x", 1), ("z", 2), ("x", 0), ("z", 1)):
+        for e in (eq, ev):
+            (e.step_x if kind == "x" else e.step_z)(d)
+        some(1)
+    some(15)
+    eq.finish(qkv_out)
+    trade(1, qkv_out, y2, y3)
+    ev.finish(vec_out)
+    trade(2, vec_out, y4, y5)
+    traded(0, wo_out, y0, y1)
+    traded(1, qkv_out, y2, y3)
+    traded(2, vec_out, y4, y5)
+    back.end()
+
+def backward(lens, gn2, mlp_out, mid, cot, x, att, q, normed, vec, cos, sin, valid, sel, fold, selk, foldk, kv, wo, wqkv, half, block, cid, window=4):
+    any_ = pl.BlockSpec(memory_space=pl.ANY)
+    vm = pl.BlockSpec(memory_space=pltpu.VMEM)
+    dma = pltpu.SemaphoreType.DMA
+    sds = jax.ShapeDtypeStruct
+    rows, width = x.shape
+    wide = wqkv.shape[-1]
+    own = wo.shape[1]
+    kvw = kv.shape[-1]
+    VM = pltpu.VMEM
+    def four(blk):
+        return [VM((k,) + blk, BF) for k in (16, 8, 4, 5)]
+    return pl.pallas_call(
+        functools.partial(backward_kernel, block, window),
+        out_shape=[sds((rows, width), BF), sds((rows, width), F32), sds((own, wide), F32), sds((own, width), F32), sds((16, 128), F32), sds((3, own, 16 * MAIN), BF), sds((16, own, 256), BF)],
+        in_specs=[pl.BlockSpec(memory_space=pltpu.SMEM)] + [vm] * 16 + [any_] * 4,
+        out_specs=[vm] * 5 + [any_] * 2,
+        scratch_shapes=[VM(kv.shape, BF), VM(wo.shape, BF), VM(wqkv.shape, BF), VM((rows, width), F32), VM((rows, width), BF), VM((rows, width), F32), VM((rows, wide), BF), VM((16, 16, 128), F32)]
+        + four((rows, kvw)) + four((own, width)) + four((own, wide)) + four((16, 128))
+        + [VM((rows, kvw), F32)] + [VM((own, width), BF)] * 2 + [VM((own, wide), BF)] * 2 + [VM((16, 128), BF)] * 2
+        + [dma((4, 16)), dma((4, 8)), dma((4, 4)), dma((4, 5))] + [dma((16,))] * 4 + [dma(()), dma((6,)), dma((3,))],
+        compiler_params=pltpu.CompilerParams(collective_id=cid, has_side_effects=True, vmem_limit_bytes=60 * 2**20),
+    )(lens, gn2, mlp_out, mid, cot, x, att, q, normed, vec, cos, sin, valid, sel, fold, selk, foldk, kv, wo, wqkv, half)
 
 
 def spare_blocks(ff, main, spare):
@@ -713,83 +1239,15 @@
     )
 
 
-def columns_plain(ff, main, spare):
-    group_count = lax.axis_size("group")
-    replica_rank = lax.axis_index("replica")
-    rows = ff[0].shape[0]
-    mains = [w[:, : main * group_count].reshape(rows, group_count, main) for w in ff]
-    blocks = jnp.concatenate(
-        [jnp.transpose(m, (1, 0, 2)) for m in mains] + [spare_blocks(ff, main, spare)], axis=2
-    )
-    own_part = lax.all_to_all(own_half(blocks, 1, replica_rank), "group", 0, 0, tiled=True)
-    other_part = swap(own_part)
-    first = jnp.where(replica_rank == 0, own_part, other_part)
-    second = jnp.where(replica_rank == 0, other_part, own_part)
-    return jnp.concatenate((first, second), axis=1).reshape(rows * group_count, 3 * main + 256)
-
-
-def mlp_plain(normed_two, grad_all, columns, main, spare, own_rows):
-    group_count = lax.axis_size("group")
-    replica_rank = lax.axis_index("replica")
-    tokens, model_width = normed_two.shape
-    share = main + spare
-    rest = 3 * main
-    gate_up_w = jnp.concatenate(
-        (
-            columns[:, :main],
-            columns[:, rest : rest + spare],
-            columns[:, main : 2 * main],
-            columns[:, rest + spare : rest + 2 * spare],
-        ),
-        axis=1,
-    )
-    down_w = jnp.concatenate(
-        (columns[:, 2 * main : rest], columns[:, rest + 128 : rest + 128 + spare]), axis=1
-    )
-
-    normed_all = lax.all_gather(normed_two, "group", axis=0)
-    normed_all = normed_all.reshape(group_count * tokens, model_width)
-
-    pre = matmul(normed_all, gate_up_w)
-    gate_pre = pre[:, :share]
-    up_pre = pre[:, share:]
-    sigmoid_gate = jax.nn.sigmoid(gate_pre)
-    silu_gate = gate_pre * sigmoid_gate
-    hidden = (silu_gate * up_pre).astype(BF)
-    grad_hidden = matmul(grad_all, down_w)
-    grad_gate = (
-        grad_hidden * up_pre * (sigmoid_gate * (1.0 + gate_pre * (1.0 - sigmoid_gate)))
-    ).astype(BF)
-    grad_up = (grad_hidden * silu_gate).astype(BF)
-    gate_up_grad = jnp.concatenate((grad_gate, grad_up), axis=1)
-    sums = [
-        p.astype(BF).reshape(group_count, tokens, model_width)
-        for p in (matmul_nt(gate_up_grad, gate_up_w), matmul_nt(hidden, down_w))
-    ]
-    grad_normed_two, mlp_out = scatter_all(sums, 4, False)
-    down_term = matmul_tn(grad_all, hidden).astype(BF)
-    gate_up_term = matmul_tn(normed_all, gate_up_grad).astype(BF)
-    zeros = jnp.zeros((model_width, 128), BF)
-    terms = jnp.concatenate(
-        (
-            gate_up_term[:, :main],
-            gate_up_term[:, share : share + main],
-            down_term[:, :main],
-            gate_up_term[:, main:share],
-            gate_up_term[:, share + main :],
-            zeros[:, : 128 - 2 * spare],
-            down_term[:, main:],
-            zeros[:, : 128 - spare],
-        ),
-        axis=1,
-    ).reshape(group_count, own_rows, 3 * main + 256)
-    half_sum = own_half(terms, 1, replica_rank).astype(F32) + swap(
-        other_half(terms, 1, replica_rank)
-    ).astype(F32)
-    return (grad_normed_two, mlp_out, half_sum.astype(BF))
-
-
-def shards(
+def folding(group_count, width):
+    share = width // group_count
+    at = jnp.arange(width)
+    sel = (at[None, :] // share == jnp.arange(group_count)[:, None]).astype(F32)
+    fold = (at[:, None] % share == jnp.arange(128)[None, :]).astype(BF)
+    return sel, fold
+
+
+def shards_fast(
     hidden_in,
     lengths,
     gain_attn,
@@ -809,225 +1267,105 @@
     group_count = lax.axis_size("group")
     group_rank = lax.axis_index("group")
     slot_count, block_len, model_width = hidden_in.shape
-    kv_heads = KV_HEADS
-    head_dim = HEAD_DIM
-    kv_width = kv_heads * head_dim
-    repeat = HEADS // kv_heads
-    slot_span = block_len * group_count
-    key_step = min(512, slot_span)
-    score_scale = head_dim ** (-0.5)
+    kv_width = KV_HEADS * HEAD_DIM
     tokens = slot_count * block_len
     hidden_units = w_gate.shape[1]
     own_rows = w_gate.shape[0]
-    share = hidden_units // group_count
     positions = group_rank * block_len + jnp.arange(block_len, dtype=jnp.int32)
     valid_rows = (positions[None, :] < lengths[:, None]).astype(F32).reshape(tokens, 1)
-    cos_table, sin_table = rope_tables(positions, head_dim)
-    cos_heads = cos_table[:, None, :]
-    sin_heads = sin_table[:, None, :]
-    rank_end = (group_rank + 1) * block_len
-    row_pos = jnp.tile(positions, repeat)
-
-    fast = group_count == 16
-    replica_rank = lax.axis_index("replica")
+    cos_table, sin_table = rope_tables(positions, HEAD_DIM)
+    turn = jnp.where(jnp.arange(HEAD_DIM) < HEAD_DIM // 2, -1.0, 1.0)
+    cos_rows = jnp.tile(cos_table, (slot_count, 1))
+    sin_rows = jnp.tile(sin_table * turn, (slot_count, 1))
+
     pieces = (gain_attn, b_query, b_key, b_value, gain_mlp)
     sizes = [p.shape[0] for p in pieces]
     offsets = [sum(sizes[:i]) for i in range(len(sizes) + 1)]
-    small = jnp.zeros((16 * 128,), BF).at[: offsets[-1]].set(jnp.concatenate(pieces))
+    small = jnp.pad(jnp.concatenate(pieces), (0, 16 * 128 - offsets[-1])).reshape(16, 128)
     main = (hidden_units // 128 // group_count) * 128
     spare = hidden_units // group_count - main
     ff = (w_gate, w_up, w_down)
-    if fast:
-        qkv_w, small, columns = weights(
-            w_query, w_key, w_value, *ff, spare_blocks(ff, main, spare), small.reshape(16, 128), 1
-        )
-    else:
-        qkv_w, small = gather_all(
-            [jnp.concatenate((w_query, w_key, w_value), axis=1), small.reshape(16, 128)], 1, fast
-        )
-        columns = columns_plain(ff, main, spare)
-    qkv_w = qkv_w.reshape(model_width, model_width + 2 * kv_width)
+    qkv_w, small, columns = weights(
+        w_query, w_key, w_value, *ff, spare_blocks(ff, main, spare), small, 1
+    )
     small = small.reshape(group_count, 16 * 128)
     gain_one, query_b, key_b, value_b, gain_two = [
         small[:, offsets[i] : offsets[i + 1]].reshape(-1).astype(F32) for i in range(len(sizes))
     ]
-    qkv_b = jnp.concatenate((query_b, key_b, value_b))
-
-    grad_final = cotangent.reshape(tokens, model_width).astype(F32) * valid_rows
-
-    inputs = hidden_in.reshape(tokens, model_width).astype(F32)
-    normed_full, factor_one = normalize(inputs, gain_one)
-    normed = normed_full.astype(BF)
-    qkv = matmul(normed, qkv_w) + qkv_b
-    query_rot = rotate(
-        qkv[:, :model_width].reshape(slot_count, block_len, HEADS, head_dim), cos_heads, sin_heads
-    ).astype(BF)
-    key_rot = rotate(
-        qkv[:, model_width : model_width + kv_width].reshape(
-            slot_count, block_len, kv_heads, head_dim
-        ),
-        cos_heads,
-        sin_heads,
-    ).astype(BF)
-    value_low = qkv[:, model_width + kv_width :].astype(BF)
-    pair = jnp.concatenate(
-        (key_rot.reshape(tokens, kv_width), value_low), axis=1
-    )
-    pair_all, grad_all, out_w = gather_all([pair, grad_final.astype(BF), w_out], 2, fast)
-    out_w = out_w.reshape(model_width, model_width)
-    grad_all = grad_all.reshape(group_count * tokens, model_width)
-    pair_all = jnp.transpose(
-        pair_all.reshape(group_count, slot_count, block_len, 2 * kv_width), (1, 0, 2, 3)
-    ).reshape(slot_count, slot_span, 2, kv_heads, head_dim)
-    key_all = pair_all[:, :, 0]
-    value_all = pair_all[:, :, 1]
-    query_groups = []
-    slot_totals = []
-    slot_attended = []
-    attended_rows = []
-    for s in range(slot_count):
-        query_rows = arrange(query_rot[s], kv_heads)
-        totals, numerator = attend_forward(
-            query_rows, key_all[s], value_all[s], row_pos, lengths[s], rank_end, key_step, score_scale
-        )
-        attended = numerator / totals[..., None]
-        query_groups.append(query_rows)
-        slot_totals.append(totals)
-        slot_attended.append(attended)
-        attended_rows.append(restore(attended, block_len))
-    attended_low = jnp.concatenate(attended_rows, axis=0).astype(BF)
-    residual_mid = inputs + matmul(attended_low, out_w)
-    normed_two_full, factor_two = normalize(residual_mid, gain_two)
-    normed_two = normed_two_full.astype(BF)
-    if fast:
-        grad_normed_two, mlp_out, half_sum = mlp(
-            normed_two, grad_all.reshape(group_count, tokens, model_width), columns, spare, 3
-        )
-    else:
-        grad_normed_two, mlp_out, half_sum = mlp_plain(
-            normed_two, grad_all, columns, main, spare, own_rows
-        )
-    rest = 3 * main
-    half_back = lax.all_to_all(half_sum, "group", 0, 0, tiled=True)
-    half_other = swap(half_back)
-    first = jnp.where(replica_rank == 0, half_back, half_other)
-    second = jnp.where(replica_rank == 0, half_other, half_back)
-    back = jnp.transpose(jnp.concatenate((first, second), axis=1), (1, 0, 2))
-    gate_sum, up_sum, down_sum = [
+    gap = (0, 2 * kv_width)
+    vec = jnp.stack(
+        [jnp.pad(gain_one, gap), jnp.concatenate((query_b, key_b, value_b)), jnp.pad(gain_two, gap)]
+    )
+    vec = jnp.pad(vec, ((0, 5), (0, 0)))
+
+    rows_in = hidden_in.reshape(tokens, model_width)
+    grad_final = (cotangent.reshape(tokens, model_width).astype(F32) * valid_rows).astype(BF)
+    q_rows, normed, attended, mid, normed_two, pair_all, grad_all, out_w = attend(
+        lengths,
+        rows_in,
+        grad_final,
+        qkv_w.reshape(model_width, model_width + 2 * kv_width),
+        w_out,
+        vec,
+        cos_rows,
+        sin_rows,
+        block_len,
+        2,
+    )
+    grad_normed_two, mlp_out, half_sum = mlp(normed_two, grad_all, columns, spare, 3)
+    sel, fold = folding(group_count, model_width)
+    selk, foldk = folding(group_count, kv_width)
+    layer_out, grad_input, qkv_sum, out_sum, vector_sum, main_sum, spare_sum = backward(
+        lengths,
+        grad_normed_two,
+        mlp_out,
+        mid,
+        grad_final,
+        rows_in,
+        attended,
+        q_rows,
+        normed,
+        vec,
+        cos_rows,
+        sin_rows,
+        jnp.broadcast_to(valid_rows, (tokens, model_width)),
+        sel,
+        fold,
+        selk,
+        foldk,
+        pair_all,
+        out_w,
+        qkv_w,
+        half_sum,
+        block_len,
+        4,
+    )
+    ff_sums = [
         jnp.concatenate(
             (
-                back[:, :, i * main : (i + 1) * main].reshape(own_rows, group_count * main),
-                back[:, :, at : at + spare].reshape(own_rows, group_count * spare),
+                main_sum[i],
+                jnp.transpose(spare_sum[:, :, at : at + spare], (1, 0, 2)).reshape(own_rows, -1),
             ),
             axis=1,
         ).astype(F32)
-        for i, at in ((0, rest), (1, rest + spare), (2, rest + 128))
+        for i, at in ((0, 0), (1, spare), (2, 128))
     ]
-
-    final_rows = residual_mid + mlp_out
-    layer_out = (final_rows * valid_rows).reshape(slot_count, block_len, model_width).astype(BF)
-    grad_mid_norm, grad_gain_two = norm_back(residual_mid, factor_two, gain_two, grad_normed_two)
-    grad_mid = grad_final + grad_mid_norm
-    grad_branch = grad_mid.astype(BF)
-    out_term = matmul_tn(attended_low, grad_branch)
-    grad_attended = matmul_nt(grad_branch, out_w)
-    grad_query_rows = []
-    grad_pairs = []
-    for s in range(slot_count):
-        slot_grad = grad_attended[s * block_len : (s + 1) * block_len].reshape(
-            block_len, HEADS, head_dim
-        )
-        grad_out = arrange(slot_grad, kv_heads)
-        totals = slot_totals[s]
-        grad_total = -jnp.sum(grad_out * slot_attended[s], axis=-1) / totals
-        grad_numer = (grad_out / totals[..., None]).astype(BF)
-        grad_query, grad_key, grad_value = attend_backward(
-            query_groups[s],
-            key_all[s],
-            value_all[s],
-            row_pos,
-            lengths[s],
-            rank_end,
-            key_step,
-            score_scale,
-            grad_numer,
-            grad_total,
-        )
-        query_back_rows = restore(grad_query * score_scale, block_len).reshape(
-            block_len, HEADS, head_dim
-        )
-        grad_query_rows.append(
-            rotate_back(query_back_rows, cos_heads, sin_heads).reshape(block_len, HEADS * head_dim)
-        )
-        grad_pairs.append(
-            jnp.concatenate(
-                (grad_key.reshape(slot_span, kv_width), grad_value.reshape(slot_span, kv_width)),
-                axis=1,
-            )
-        )
-    pair_grads = jnp.stack(grad_pairs).reshape(slot_count, group_count, block_len, 2 * kv_width)
-    pair_grads = jnp.transpose(pair_grads, (1, 0, 2, 3)).astype(BF)
-    (pair_sum,) = scatter_all(
-        [pair_grads.reshape(group_count, tokens, 2 * kv_width)], 5, fast
-    )
-    pair_sum = pair_sum.reshape(slot_count, block_len, 2 * kv_width)
-    grad_query_pre = jnp.concatenate(grad_query_rows, axis=0).astype(BF)
-    key_sum = pair_sum[..., :kv_width].reshape(slot_count, block_len, kv_heads, head_dim)
-    grad_key_pre = (
-        rotate_back(key_sum * score_scale, cos_heads, sin_heads).astype(BF).reshape(tokens, kv_width)
-    )
-    grad_value_pre = pair_sum[..., kv_width:].astype(BF).reshape(tokens, kv_width)
-    grad_qkv = jnp.concatenate((grad_query_pre, grad_key_pre, grad_value_pre), axis=1)
-    grad_normed = matmul_nt(grad_qkv, qkv_w)
-    grad_in_norm, grad_gain_one = norm_back(inputs, factor_one, gain_one, grad_normed)
-    grad_input = (grad_mid + grad_in_norm).reshape(slot_count, block_len, model_width)
-    qkv_term = matmul_tn(normed, grad_qkv)
-    qkv_bias = jnp.sum(grad_qkv.astype(F32), axis=0)
-
-    vectors = jnp.concatenate(
-        [
-            grad_gain_one.reshape(group_count, -1),
-            qkv_bias[:model_width].reshape(group_count, -1),
-            qkv_bias[model_width : model_width + kv_width].reshape(group_count, -1),
-            qkv_bias[model_width + kv_width :].reshape(group_count, -1),
-            grad_gain_two.reshape(group_count, -1),
-        ],
-        axis=1,
-    )
-    vectors = jnp.concatenate(
-        (vectors, jnp.zeros((group_count, 16 * 128 - offsets[-1]), F32)), axis=1
-    ).reshape(group_count, 16, 128)
-    weight_sum, out_sum, vector_sum = scatter_all(
-        [
-            p.astype(BF).reshape(group_count, p.shape[0] // group_count, -1)
-            for p in (qkv_term, out_term)
-        ]
-        + [vectors.astype(BF)],
-        6,
-        fast,
-        pair=True,
-    )
-    vector_sum = vector_sum.reshape(-1)
     gain_one_sum, query_bias_sum, key_bias_sum, value_bias_sum, gain_two_sum = [
-        vector_sum[offsets[i] : offsets[i + 1]] for i in range(len(sizes))
+        vector_sum[i, : sizes[i]] for i in range(len(sizes))
     ]
-    ends = (0, model_width, model_width + kv_width, model_width + 2 * kv_width)
-    query_sum, key_sum_w, value_sum_w = [weight_sum[:, ends[i] : ends[i + 1]] for i in range(3)]
     return (
-        layer_out,
-        grad_input,
+        layer_out.reshape(hidden_in.shape),
+        grad_input.reshape(hidden_in.shape),
         gain_one_sum,
-        query_sum,
+        qkv_sum[:, :model_width],
         query_bias_sum,
-        key_sum_w,
+        qkv_sum[:, model_width : model_width + kv_width],
         key_bias_sum,
-        value_sum_w,
+        qkv_sum[:, model_width + kv_width :],
         value_bias_sum,
         out_sum,
         gain_two_sum,
-        gate_sum,
-        up_sum,
-        down_sum,
+        *ff_sums,
     )
 
 
@@ -1036,7 +1374,7 @@
     vec = P("group")
     mat = P("group", None)
     return jax.shard_map(
-        shards,
+        shards_fast if mesh.shape["group"] == 16 else shards_plain,
         mesh=mesh,
         in_specs=(act, P("replica"), vec, mat, vec, mat, vec, mat, vec, mat, vec, mat, mat, mat, act),
         out_specs=(act, act, vec, mat, vec, mat, vec, mat, vec, mat, vec, mat, mat, mat),

time: 588 us -> 518 us (0.88)
  matrix products: 35.7 us -> 0 us
  local copies, waits for them, and re-layouts: 58.9 us -> 29.7 us
  Pallas kernels: 440 us -> 468 us
  other arithmetic: 34 us -> 13.3 us
    dot_general x20 -> x0, matrix products: 35.7 us -> none  [the longest x2 9.46 us: matmul_nt(): lax.dot_general(a, b, (((1,), (1,)), ((), ())), preferred_element_type=F32)]
    pallas_call x3 -> x2, Pallas kernels: 189 us -> 220 us  [the longest x1 142 us: backward(): pl.pallas_call(functools.partial(backward_kernel, block, window), out_sha...]
    slice x23 -> x4, local copies, waits for them, and re-layouts: 17.6 us -> 1.69 us  [the longest x1 0.86 us: shards_fast(): qkv_sum[:, :model_width]]
    reshape x19 -> x4, local copies, waits for them, and re-layouts: 15.4 us -> 4.17 us  [the longest x3 3.57 us: shards_fast(): jnp.transpose(spare_sum[:, :, at:at + spare], (1, 0, 2))]
    convert_element_type x12 -> x9, other arithmetic: 11.5 us -> 12.3 us  [the longest x3 8.36 us: shards_fast(): ff_sums = [jnp.concatenate((main_sum[i], jnp.transpose(spare_sum[:, :, at...]
  transfers between devices with their start and end apart: 2 -> 0, of which waited for: 0 -> 0; matrix products, arithmetic and copies ran while one was open for 11% -> 0% of each run, Pallas kernels for 20% -> 0%
where the time goes in v5:
time: 518 us; the launch traced here: 512 us
  Pallas kernels  468 us (90%)
  local copies, waits for them, and re-layouts  29.7 us (6%)
  other arithmetic  13.3 us (3%)
    pallas_call x1, Pallas kernels, backward(): pl.pallas_call(functools.partial(backward_kernel, block, window), out_sha...  142 us
    pallas_call x1, Pallas kernels, mlp(): pl.pallas_call(functools.partial(mlp_kernel, spare), out_shape=[jax.Shape...  141 us
    pallas_call x1, Pallas kernels, weights(): pl.pallas_call(weights_kernel, out_shape=[jax.ShapeDtypeStruct((16, rows,...  107 us
    pallas_call x1, Pallas kernels, attend(): pl.pallas_call(functools.partial(attend_kernel, block), out_shape=[sds(ac...  78.7 us

profile of v5, /device:TPU:0, one launch (start us, length us, event | category | flops | bytes accessed | tf_op | source)
XLA Modules:
  0.0 512.3 jit_solution(9538732626882559697)
XLA Ops:
  0.6 0.9 slice.66
  2.0 0.9 slice.67
  3.4 0.9 slice.68
  4.8 2.0 concatenate.30
  7.5 107.2 %shard_map.254 = (bf16[16,96,2048]{2,1,0:T(8,128)(2,1)}, bf16[16,16,128]{2,1,0:T(8,128)(2,1)}, bf16[1536,1792]{1,0:T(8,128)(2,1)}) custom-call(bf16[96,1536]{1,0:T(8,128)(2,1)} %wq.1, bf16[96,256]{1,0:T(8,128)(2,1)} %wk.1, bf16[96,256]{1,0:T(8,128)(2,1)} %wv.1, bf16[96,8960]{1,0:T(8,128)(2,1)} %wg.1, bf16[96,8960]{1,0:T(8,128)(2,1)} %wu.1, ...), custom_call_target="tpu_custom_call" | custom-call | tf_op jit(solution)/shard_map/pallas_call | solution.py:736
  114.7 0.9 copy.46
  117.1 0.9 fusion.cot_ref.cot
  119.5 78.7 %shard_map.255 = (bf16[128,1536]{1,0:T(8,128)(2,1)}, bf16[128,1536]{1,0:T(8,128)(2,1)}, f32[128,1536]{1,0:T(8,128)}, f32[128,1536]{1,0:T(8,128)}, bf16[128,1536]...) custom-call(s32[2]{0:T(128)} %lens.3, ...), custom_call_target="tpu_custom_call" | custom-call | tf_op jit(solution)/shard_map/pallas_call | solution.py:1007
  198.2 140.6 %shard_map.256 = (f32[128,1536]{1,0:T(8,128)}, f32[128,1536]{1,0:T(8,128)}, bf16[16,48,1792]{2,1,0:T(8,128)(2,1)}) custom-call(bf16[128,1536]{1,0:T(8,128)(2,1)} %get-tuple-element.37.n2_ref, bf16[16,128,1536]{2,1,0:T(8,128)(2,1)} %get-tuple-element.38.cot_ref, bf16[1536,1792]{1,0:T(8,128)(2,1)} %get-tuple-element.39.w_ref), custom_call_target="tpu_custom_call" | custom-call | tf_op jit(solution)/shard_map/pallas_call | solution.py:888
  338.8 1.0 mul.52.valid
  339.8 1.0 fusion.1.fold
  342.9 141.5 %shard_map.257 = (bf16[128,1536]{1,0:T(8,128)(2,1)}, f32[128,1536]{1,0:T(8,128)}, f32[96,2048]{1,0:T(8,128)}, f32[96,1536]{1,0:T(8,128)}, f32[16,128]{1,0:T(8,12...) custom-call(s32[2]{0:T(128)} %lens.3, f32[128,1536]{1,0:T(8,128)} %get-tuple-element.40.gn2, ...), custom_call_target="tpu_custom_call" | custom-call | tf_op jit(solution)/shard_map/pallas_call | solution.py:1218
  484.4 3.9 slice_bitcast_fusion
  488.4 1.1 slice_bitcast_fusion.3
  489.5 1.8 copy.39
  491.3 1.7 copy.40
  493.0 3.5 maximum_convert_fusion.2
  496.5 1.8 copy.37
  498.3 1.7 copy.38
  500.1 2.9 maximum_convert_fusion.1
  503.3 2.0 maximum_convert_fusion
  506.8 1.3 slice_bitcast_fusion.6
  508.2 1.3 slice_bitcast_fusion.7
  510.2 0.9 copy.51
  (70 shorter events, 10.5 us)
Async XLA Ops:
  1.6 5.2 %copy-start.7 = (bf16[96]{0:T(256)(128)(2,1)S(1)}, bf16[96]{0:T(256)(128)(2,1)}, u32[]{:S(2)}) copy-start(bf16[96]{0:T(256)(128)(2,1)} %param.17) | copy-start | bytes 580
  1.6 5.2 %copy-start.8 = (bf16[96]{0:T(256)(128)(2,1)S(1)}, bf16[96]{0:T(256)(128)(2,1)}, u32[]{:S(2)}) copy-start(bf16[96]{0:T(256)(128)(2,1)} %param.19) | copy-start | bytes 580
  1.6 5.2 %copy-start.9 = (bf16[16]{0:T(256)(128)(2,1)S(1)}, bf16[16]{0:T(256)(128)(2,1)}, u32[]{:S(2)}) copy-start(bf16[16]{0:T(256)(128)(2,1)} %param.21) | copy-start | bytes 100
  1.6 5.2 %copy-start.10 = (bf16[16]{0:T(256)(128)(2,1)S(1)}, bf16[16]{0:T(256)(128)(2,1)}, u32[]{:S(2)}) copy-start(bf16[16]{0:T(256)(128)(2,1)} %param.23) | copy-start | bytes 100
  1.6 5.2 %copy-start.11 = (bf16[96]{0:T(256)(128)(2,1)S(1)}, bf16[96]{0:T(256)(128)(2,1)}, u32[]{:S(2)}) copy-start(bf16[96]{0:T(256)(128)(2,1)} %param.25) | copy-start | bytes 580
  6.8 110.2 %copy-start.6 = (s32[2]{0:T(128)S(1)}, s32[2]{0:T(128)}, u32[]{:S(2)}) copy-start(s32[2]{0:T(128)} %lens.3) | copy-start | bytes 28
  6.8 110.3 %copy-start.5 = (bf16[2,64,1536]{2,1,0:T(8,128)(2,1)S(1)}, bf16[2,64,1536]{2,1,0:T(8,128)(2,1)}, u32[]{:S(2)}) copy-start(bf16[2,64,1536]{2,1,0:T(8,128)(2,1)} %param.29) | copy-start | bytes 1179652
  484.4 4.0 copy-start
  503.0 2.3 copy-start.2
  503.3 6.2 %copy-start.4 = (bf16[128,1536]{1,0:T(8,128)(2,1)S(1)}, bf16[128,1536]{1,0:T(8,128)(2,1)}, u32[]{:S(2)}) copy-start(bf16[128,1536]{1,0:T(8,128)(2,1)} %get-tuple-element.49) | copy-start | bytes 1179652
  503.3 6.9 %copy-start.1 = (f32[128,1536]{1,0:T(8,128)S(1)}, f32[128,1536]{1,0:T(8,128)}, u32[]{:S(2)}) copy-start(f32[128,1536]{1,0:T(8,128)} %get-tuple-element.50) | copy-start | bytes 2359300
  503.3 7.8 %copy-start.3 = (f32[96,1536]{1,0:T(8,128)S(1)}, f32[96,1536]{1,0:T(8,128)}, u32[]{:S(2)}) copy-start(f32[96,1536]{1,0:T(8,128)} %get-tuple-element.101) | copy-start | bytes 1769476

commit v6 on v5

--- a/solution.py
+++ b/solution.py
@@ -481,32 +481,6 @@
             self.sent(k)
         if local:
             pltpu.make_async_copy(self.src, self.out.at[0], self.local).wait()
-
-def gather_kernel(n, *refs):
-    srcs, outs = refs[:n], refs[n:2*n]
-    send, recv, local = refs[2*n:]
-    at = place()
-    greet(*at)
-    eng = [Gather(at, srcs[i], outs[i], send.at[i], recv.at[i], local.at[i]) for i in range(n)]
-    for e in eng: e.begin()
-    for e in eng: e.first()
-    for e in eng: e.second()
-    for e in eng: e.third()
-    for e in eng: e.fourth()
-    for d in range(NZ):
-        for e in eng: e.from_c(d)
-    for e in eng: e.end()
-
-def gather(arrays, cid):
-    n = len(arrays)
-    return pl.pallas_call(
-        functools.partial(gather_kernel, n),
-        out_shape=[jax.ShapeDtypeStruct((16,) + a.shape, a.dtype) for a in arrays],
-        in_specs=[pl.BlockSpec(memory_space=pl.ANY)] * n,
-        out_specs=[pl.BlockSpec(memory_space=pl.ANY)] * n,
-        scratch_shapes=[pltpu.SemaphoreType.DMA((n, 18)), pltpu.SemaphoreType.DMA((n, 16)), pltpu.SemaphoreType.DMA((n,))],
-        compiler_params=pltpu.CompilerParams(collective_id=cid, has_side_effects=True),
-    )(*arrays)
 
 class Scatter:
     def __init__(self, at, part, rc, rx, rz, send, rcs, rxs, rzs):
@@ -583,57 +557,6 @@
         for zz in range(NZ):
             when(z != zz, lambda zz=zz: self.copy(self.part.at[0], self.part.at[0], 12 + zz, self.rcs.at[0], (self.r, 0)).wait_send())
 
-def scatter_steps(engines):
-    for e in engines: e.begin()
-    order = [("x", 3), ("x", 2), ("z", 3), ("x", 1), ("z", 2), ("x", 0), ("z", 1)]
-    for kind, d in order:
-        for e in engines:
-            (e.step_x if kind == "x" else e.step_z)(d)
-
-def scatter_kernel(n, pair, *refs):
-    ps, os = refs[:n], refs[n:2*n]
-    s = refs[2*n:]
-    vm = [s[4*i:4*i+4] for i in range(n)]
-    ysb = s[4*n:4*n+2*n] if pair else None
-    send, rcs, rxs, rzs, lsem, ysem = s[4*n+(2*n if pair else 0):]
-    at = place()
-    for i in range(n):
-        pltpu.make_async_copy(ps[i], vm[i][0], lsem.at[i]).start()
-    greet(*at, with_y=pair)
-    for i in range(n):
-        pltpu.make_async_copy(ps[i], vm[i][0], lsem.at[i]).wait()
-    engines = [Scatter(at, *vm[i], send.at[i], rcs.at[i], rxs.at[i], rzs.at[i]) for i in range(n)]
-    scatter_steps(engines)
-    r, z, x, c = at
-    for i, e in enumerate(engines):
-        e.finish(os[i])
-        if pair:
-            ysb[2*i][...] = os[i][...].astype(BF)
-            pltpu.make_async_remote_copy(ysb[2*i], ysb[2*i+1], ysem.at[2*i], ysem.at[2*i+1], device_id=(1 - r, idx(z, x, c)), device_id_type=MESH).start()
-    if pair:
-        for i, e in enumerate(engines):
-            pltpu.make_async_remote_copy(ysb[2*i], ysb[2*i+1], ysem.at[2*i], ysem.at[2*i+1], device_id=(1 - r, idx(z, x, c)), device_id_type=MESH).wait()
-            os[i][...] = ysb[2*i][...].astype(F32) + ysb[2*i+1][...].astype(F32)
-
-def scatter(parts, cid, pair=False):
-    n = len(parts)
-    scratch = []
-    for p in parts:
-        blk = p.shape[1:]
-        scratch += [pltpu.VMEM((k,) + blk, BF) for k in (16, 8, 4, 5)]
-    if pair:
-        for p in parts:
-            scratch += [pltpu.VMEM(p.shape[1:], BF)] * 2
-    dma = pltpu.SemaphoreType.DMA
-    return pl.pallas_call(
-        functools.partial(scatter_kernel, n, pair),
-        out_shape=[jax.ShapeDtypeStruct(p.shape[1:], F32) for p in parts],
-        in_specs=[pl.BlockSpec(memory_space=pl.ANY)] * n,
-        out_specs=[pl.BlockSpec(memory_space=pltpu.VMEM)] * n,
-        scratch_shapes=scratch + [dma((n, 16)), dma((n, 8)), dma((n, 4)), dma((n, 5)), dma((n,)), dma((2 * n,))],
-        compiler_params=pltpu.CompilerParams(collective_id=cid, has_side_effects=True, vmem_limit_bytes=60 * 2**20),
-    )(*parts)
-
 
 KS = (8, 1, 9, 2, 10, 3, 11, 4, 12, 5, 13, 6, 14, 7, 15)
 WINDOW = 4
@@ -696,52 +619,6 @@
     pl.semaphore_signal(bar, inc=1, device_id=(1 - r, me), device_id_type=MESH)
     pl.semaphore_wait(bar, 16)
 
-def weights_kernel(wq, wk, wv, wg, wu, wd, rem, small, qkv_out, small_out, buf, qkv_own, gs, gr, gl, ss, sr, sl, ds, dr, ys, yr, dl, lsem):
-    at = place()
-    width = wq.shape[1]
-    kw = wk.shape[1]
-    loads = [pltpu.make_async_copy(w, qkv_own.at[:, pl.ds(o, n)], lsem.at[i]) for i, (w, o, n) in enumerate(((wq, 0, width), (wk, width, kw), (wv, width + kw, kw)))]
-    for l in loads: l.start()
-    hail_all(*at)
-    for l in loads: l.wait()
-    g = Gather(at, qkv_own, qkv_out, gs, gr, gl)
-    v = Gather(at, small, small_out, ss, sr, sl)
-    d = Deal(at, (wg, wu, wd), rem, buf, ds, dr, ys, yr, dl)
-    g.begin()
-    v.begin()
-    d.begin()
-    steps = iter(range(15))
-    def some(n):
-        for _ in range(n):
-            i = next(steps, None)
-            if i is not None:
-                d.step(i)
-    for phase, n in ((lambda e: e.first(), PACE[0]), (lambda e: e.second(), PACE[1]), (lambda e: e.third(), PACE[2]), (lambda e: e.fourth(), 15)):
-        phase(g)
-        phase(v)
-        some(n)
-    for e in (g, v):
-        for zz in range(NZ):
-            e.from_c(zz)
-        e.end()
-    d.end()
-
-PACE = (2, 2, 3)
-
-def weights(wq, wk, wv, wg, wu, wd, rem, small, cid):
-    any_ = pl.BlockSpec(memory_space=pl.ANY)
-    dma = pltpu.SemaphoreType.DMA
-    rows = wq.shape[0]
-    width = wq.shape[1] + 2 * wk.shape[1]
-    return pl.pallas_call(
-        weights_kernel,
-        out_shape=[jax.ShapeDtypeStruct((16, rows, width), BF), jax.ShapeDtypeStruct((16,) + small.shape, BF), jax.ShapeDtypeStruct((16 * rows, 3 * MAIN + 256), BF)],
-        in_specs=[any_] * 8,
-        out_specs=[any_] * 3,
-        scratch_shapes=[pltpu.VMEM((rows, width), BF), dma((18,)), dma((16,)), dma(()), dma((18,)), dma((16,)), dma(())] + [dma((16,))] * 4 + [dma(()), dma((3,))],
-        compiler_params=pltpu.CompilerParams(collective_id=cid, has_side_effects=True),
-    )(wq, wk, wv, wg, wu, wd, rem, small)
-
 
 def dot(a, b):
     return lax.dot_general(a, b, (((1,), (0,)), ((), ())), preferred_element_type=F32)
@@ -920,51 +797,175 @@
     factor = lax.rsqrt(jnp.mean(v * v, axis=-1, keepdims=True) + EPSILON)
     return v * factor * gain
 
-def attend_kernel(block, lens, x_ref, cot_ref, wqkv_ref, wo_ref, vec, cos_ref, sin_ref,
-                  q_out, normed_out, att_out, mid_out, n2_out, kv_out, cot_out, wo_out,
-                  wqkv, own, kv, wo, cs, cr, cl, ws, wr, wl, ks, kr, kl, lsem):
+
+class GatherY(Gather):
+    def __init__(self, at, src, out, send, recv, local):
+        Gather.__init__(self, at, src, out, send, recv, local)
+        self.n = src.shape[0] // 2
+        self.ydev = (1 - self.r, idx(self.z, self.x, self.c))
+    def rows(self, h):
+        return pl.ds(pl.multiple_of(h * self.n, self.n), self.n)
+    def half(self, b, h):
+        return self.out.at[b, self.rows(h)]
+    def move(self, src, dst, k, q, dev):
+        return pltpu.make_async_remote_copy(src, dst, self.send.at[k], self.recv.at[q], device_id=dev, device_id_type=MESH)
+    def arrived(self, b, h):
+        self.move(self.half(b, h), self.half(b, h), 0, 2 * b + h, self.ydev).wait_recv()
+    def begin(self):
+        z, x, c, r = self.z, self.x, self.c, self.r
+        me = idx(z, x, c)
+        mine, dst = self.src.at[self.rows(r)], self.half(me, r)
+        for s in (1, -1):
+            when(self.inside(z + s), lambda s=s: self.move(mine, dst, 0 if s == 1 else 3, 2 * me + r, self.zdev(s)).start())
+        self.move(mine, dst, 6 + z, 2 * me + r, self.xdev()).start()
+        self.move(self.src, self.out.at[me], 18 + 2 * z + x, 2 * me, self.cdev()).start()
+        pltpu.make_async_copy(self.src, self.out.at[me], self.local).start()
+    def from_z(self, zz):
+        z, x, c, r = self.z, self.x, self.c, self.r
+        b = idx(zz, x, c)
+        q = 2 * b + r
+        self.arrived(b, r)
+        s = jnp.where(zz < z, 1, -1)
+        slot = jnp.where(zz < z, 0, 3) + jnp.abs(zz - z)
+        a = self.half(b, r)
+        when(self.inside(z + s), lambda: self.move(a, a, slot, q, (r, idx(z + s, x, c))).start())
+        self.move(a, a, 6 + zz, q, self.xdev()).start()
+        self.move(a, a, 18 + 2 * zz + x, q, self.cdev()).start()
+        self.move(a, a, 10 + 2 * zz + x, q, self.ydev).start()
+    def from_x(self, zz):
+        x, c, r = self.x, self.c, self.r
+        b = idx(zz, 1 - x, c)
+        q = 2 * b + r
+        self.arrived(b, r)
+        a = self.half(b, r)
+        self.move(a, a, 18 + 2 * zz + 1 - x, q, self.cdev()).start()
+        self.move(a, a, 10 + 2 * zz + 1 - x, q, self.ydev).start()
+    def from_y(self, zz):
+        x, c, r = self.x, self.c, self.r
+        def take(xx):
+            b = idx(zz, xx, c)
+            self.arrived(b, 1 - r)
+            a = self.half(b, 1 - r)
+            self.move(a, a, 26 + 2 * zz + xx, 2 * b + 1 - r, self.cdev()).start()
+        when(zz != self.z, lambda: take(x))
+        take(1 - x)
+    def from_c(self, zz):
+        x, c, r = self.x, self.c, self.r
+        b = idx(zz, x, 1 - c)
+        whole = self.out.at[b]
+        when(zz == self.z, lambda: self.move(whole, whole, 0, 2 * b, self.ydev).wait_recv())
+        def both(b):
+            self.arrived(b, r)
+            self.arrived(b, 1 - r)
+        when(zz != self.z, lambda: both(b))
+        both(idx(zz, 1 - x, 1 - c))
+    def end(self):
+        z, x = self.z, self.x
+        own = 2 * z + x
+        a = self.half(0, 0)
+        def sent(k, a=a):
+            self.move(a, a, k, 0, self.ydev).wait_send()
+        for d in range(NZ - 1):
+            when((z - d >= 0) & (z < NZ - 1), lambda d=d: sent(d))
+            when((z + d < NZ) & (z > 0), lambda d=d: sent(3 + d))
+        for k in range(6, 10):
+            sent(k)
+        for k in range(8):
+            def other(k=k):
+                sent(10 + k)
+                sent(18 + k)
+                sent(26 + k)
+            when(own != k, other)
+        sent(18 + own, self.out.at[0])
+        pltpu.make_async_copy(self.src, self.out.at[0], self.local).wait()
+
+def front_kernel(block, lens, x_ref, cos_ref, sin_ref, sel, fold, selk, foldk, small, wq, wk, wv, wg, wu, wd, rem, cot_ref, wo_ref,
+                 q_out, normed_out, att_out, mid_out, n2_out, vec, buf, qkv_out, kv_out, cot_out, wo_out,
+                 qkv_own, wqkv, small_all, own, kv, wo,
+                 qs, qr, ql, vs, vr, vl, ks, kr, kl, cs, cr, cl, ws, wr, wl, ds, dr, ys, yr, dl, lsem):
     at = place()
     width = HEADS * HEAD_DIM
     kw = KV_HEADS * HEAD_DIM
-    load = pltpu.make_async_copy(wqkv_ref, wqkv, lsem.at[0])
-    load.start()
-    greet(*at)
+    loads = [pltpu.make_async_copy(w, qkv_own.at[:, pl.ds(o, n)], lsem.at[i]) for i, (w, o, n) in enumerate(((wq, 0, width), (wk, width, kw), (wv, width + kw, kw)))]
+    for l in loads: l.start()
+    hail_all(*at)
+    for l in loads: l.wait()
+    gq = GatherY(at, qkv_own, wqkv, qs, qr, ql)
+    gv = Gather(at, small, small_all, vs, vr, vl)
+    gk = Gather(at, own, kv, ks, kr, kl)
     gc = Gather(at, cot_ref, cot_out, cs, cr, cl)
-    gw = Gather(at, wo_ref, wo, ws, wr, wl)
-    gk = Gather(at, own, kv, ks, kr, kl)
-    gw.begin()
+    gw = GatherY(at, wo_ref, wo, ws, wr, wl)
+    d = Deal(at, (wg, wu, wd), rem, buf, ds, dr, ys, yr, dl)
+    steps = iter(range(15))
+    def some(n):
+        for _ in range(n):
+            i = next(steps, None)
+            if i is not None:
+                d.step(i)
+    gq.begin()
+    gv.begin()
+    d.begin()
+    x = x_ref[...].astype(F32)
+    gq.first()
+    gv.first()
+    gq.second()
+    gv.second()
+    gq.from_y(gq.p[0])
+    some(EARLY[0])
+    gq.third()
+    gv.third()
+    gq.from_y(gq.p[1])
+    gq.fourth()
+    gv.fourth()
     gc.begin()
-    x = x_ref[...].astype(F32)
+    gq.from_y(gq.p[2])
+    gq.from_y(gq.p[3])
+    for zz in range(NZ):
+        gv.from_c(zz)
+        gq.from_c(zz)
+    gv.end()
+    gq.end()
+    keep = [pltpu.make_async_copy(wqkv, qkv_out, lsem.at[3]), pltpu.make_async_copy(kv, kv_out, lsem.at[4]), pltpu.make_async_copy(wo, wo_out, lsem.at[5])]
+    keep[0].start()
+    vec[...] = jnp.zeros_like(vec)
+    for i, row, first, a, b in ((0, 0, 0, sel, fold), (1, 1, 0, sel, fold), (2, 1, width, selk, foldk), (3, 1, width + kw, selk, foldk), (4, 2, 0, sel, fold)):
+        t = dot_nt(small_all[:, i, :].astype(BF), b[...])
+        vec[row : row + 1, first : first + a.shape[1]] = jnp.sum(t * a[...], axis=0, keepdims=True)
     normed_out[...] = rms(x, vec[0:1, :width]).astype(BF)
-    load.wait()
     cos, sin = cos_ref[...], sin_ref[...]
     def product(base):
-        return dot(normed_out[...], wqkv[:, pl.ds(pl.multiple_of(base, 256), 256)]) + vec[1:2, pl.ds(pl.multiple_of(base, 256), 256)]
+        return dot(normed_out[...], wqkv[:, :, pl.ds(pl.multiple_of(base, 256), 256)].reshape(width, 256)) + vec[1:2, pl.ds(pl.multiple_of(base, 256), 256)]
     pre = product(width)
     own[:, :HEAD_DIM] = spin(pre[:, :HEAD_DIM], cos, sin).astype(BF)
     own[:, HEAD_DIM : 2 * HEAD_DIM] = spin(pre[:, HEAD_DIM:], cos, sin).astype(BF)
     own[:, kw:] = product(width + kw).astype(BF)
     gk.begin()
+    gw.begin()
     @pl.loop(0, width // 256)
     def _(t):
         pre = product(t * 256)
         for i in range(2):
             col = pl.ds(pl.multiple_of(256 * t + HEAD_DIM * i, HEAD_DIM), HEAD_DIM)
             q_out[:, col] = spin(pre[:, HEAD_DIM * i : HEAD_DIM * (i + 1)], cos, sin).astype(BF)
+    some(EARLY[1])
+    gc.first()
     gk.first()
     gw.first()
-    gc.first()
+    some(EARLY[2])
     gk.second()
+    gc.second()
     gw.second()
-    gc.second()
+    gw.from_y(gw.p[0])
     gk.third()
+    some(EARLY[3])
     gk.fourth()
+    gc.third()
     gw.third()
-    gc.third()
+    gw.from_y(gw.p[1])
     for zz in range(NZ):
         gk.from_c(zz)
     gk.end()
-    pltpu.make_async_copy(kv, kv_out, lsem.at[1]).start()
+    keep[1].start()
     first_row = lax.axis_index("group") * block
     span = 16 * block
     @pl.loop(0, 4)
@@ -978,41 +979,52 @@
         e = exp_scores(q, k, first_row, block, lens[s])
         total = jnp.sum(e, axis=-1, keepdims=True)
         att_out[rows, cols] = spread_heads(dot(e.astype(BF), v) / total, block)
+    some(EARLY[4])
     gw.fourth()
     gc.fourth()
+    gw.from_y(gw.p[2])
+    gw.from_y(gw.p[3])
     for zz in range(NZ):
         gw.from_c(zz)
     gw.end()
-    out_copy = pltpu.make_async_copy(wo, wo_out, lsem.at[2])
-    out_copy.start()
+    keep[2].start()
     @pl.loop(0, width // 256)
     def _(t):
         col = pl.ds(pl.multiple_of(256 * t, 256), 256)
         mid_out[:, col] = x_ref[:, col].astype(F32) + dot(att_out[...].astype(BF), wo[:, :, col].reshape(width, 256))
     n2_out[...] = rms(mid_out[...], vec[2:3, :width]).astype(BF)
+    some(15)
     for zz in range(NZ):
         gc.from_c(zz)
     gc.end()
-    pltpu.make_async_copy(kv, kv_out, lsem.at[1]).wait()
-    out_copy.wait()
-
-def attend(lens, x, cot, wqkv, wo, vec, cos, sin, block, cid):
+    for k in keep:
+        k.wait()
+    d.end()
+
+EARLY = (2, 1, 1, 2, 3)
+
+def front(lens, x, cos, sin, sel, fold, selk, foldk, small, wq, wk, wv, wg, wu, wd, rem, cot, wo, block, cid):
     rows, width = x.shape
     any_ = pl.BlockSpec(memory_space=pl.ANY)
     vm = pl.BlockSpec(memory_space=pltpu.VMEM)
     dma = pltpu.SemaphoreType.DMA
     act = (rows, width)
+    own = wq.shape[0]
     kvw = 2 * KV_HEADS * HEAD_DIM
+    wide = width + kvw
     sds = jax.ShapeDtypeStruct
+    VM = pltpu.VMEM
     return pl.pallas_call(
-        functools.partial(attend_kernel, block),
-        out_shape=[sds(act, BF), sds(act, BF), sds(act, F32), sds(act, F32), sds(act, BF), sds((16, rows, kvw), BF), sds((16,) + act, BF), sds((16,) + wo.shape, BF)],
-        in_specs=[pl.BlockSpec(memory_space=pltpu.SMEM), vm, any_, any_, any_, vm, vm, vm],
-        out_specs=[vm] * 5 + [any_] * 3,
-        scratch_shapes=[pltpu.VMEM(wqkv.shape, BF), pltpu.VMEM((rows, kvw), BF), pltpu.VMEM((16, rows, kvw), BF), pltpu.VMEM((16,) + wo.shape, BF)]
-        + [dma((18,)), dma((16,)), dma(())] * 3 + [dma((3,))],
+        functools.partial(front_kernel, block),
+        out_shape=[sds(act, BF), sds(act, BF), sds(act, F32), sds(act, F32), sds(act, BF), sds((8, wide), F32),
+                   sds((16 * own, 3 * MAIN + 256), BF), sds((16, own, wide), BF), sds((16, rows, kvw), BF), sds((16,) + act, BF), sds((16,) + wo.shape, BF)],
+        in_specs=[pl.BlockSpec(memory_space=pltpu.SMEM)] + [vm] * 7 + [any_] * 10,
+        out_specs=[vm] * 6 + [any_] * 5,
+        scratch_shapes=[VM((own, wide), BF), VM((16, own, wide), BF), VM((16,) + small.shape, F32), VM((rows, kvw), BF), VM((16, rows, kvw), BF), VM((16,) + wo.shape, BF)]
+        + [dma((34,)), dma((32,)), dma(())] + [dma((18,)), dma((16,)), dma(())] * 3 + [dma((34,)), dma((32,)), dma(())]
+        + [dma((16,))] * 4 + [dma(()), dma((6,))],
         compiler_params=pltpu.CompilerParams(collective_id=cid, has_side_effects=True, vmem_limit_bytes=60 * 2**20),
-    )(lens, x, cot, wqkv, wo, vec, cos, sin)
+    )(lens, x, cos, sin, sel, fold, selk, foldk, small, wq, wk, wv, wg, wu, wd, rem, cot, wo)
 
 
 class Return:
@@ -1066,10 +1078,10 @@
     return factor * weighted - v * (factor * factor * factor) * inner, jnp.sum(upstream * v * factor, axis=0, keepdims=True)
 
 def backward_kernel(block, window, lens, gn2, mlp_out, mid, cot, x_ref, att, q_ref, normed, vec, cos_ref, sin_ref, valid, sel, fold, selk, foldk, kv_ref, wo_ref, wqkv_ref, half_ref,
-                    layer_out, grad_input, qkv_out, wo_out, vec_out, g_main, g_spare,
+                    layer_out, grad_input, q_out, pair_out, wo_out, vec_out, g_main, g_spare,
                     kv, wo, wqkv, gmid, branch, gatt, gqkv, pv,
-                    p_kv, c_kv, x_kv, z_kv, p_wo, c_wo, x_wo, z_wo, p_qk, c_qk, x_qk, z_qk, p_ve, c_ve, x_ve, z_ve,
-                    kvsum, y0, y1, y2, y3, y4, y5,
+                    p_kv, c_kv, x_kv, z_kv, p_wo, c_wo, x_wo, z_wo, p_qk, c_qk, x_qk, z_qk, p_pw, c_pw, x_pw, z_pw, p_ve, c_ve, x_ve, z_ve,
+                    kvsum, y0, y1, y2, y3, y4, y5, y6, y7,
                     ss, sc, sx, sz, rs, rr, rys, ryr, rl, ysem, lsem):
     at = place()
     r, z, x, c = at
@@ -1080,8 +1092,8 @@
     hail_all(*at)
     back = Return(at, half_ref, g_main, g_spare, rs, rr, rys, ryr, rl)
     back.begin(window)
-    sets = ((p_kv, c_kv, x_kv, z_kv), (p_wo, c_wo, x_wo, z_wo), (p_qk, c_qk, x_qk, z_qk), (p_ve, c_ve, x_ve, z_ve))
-    ek, eo, eq, ev = [Scatter(at, *b, ss.at[i], sc.at[i], sx.at[i], sz.at[i]) for i, b in enumerate(sets)]
+    sets = ((p_kv, c_kv, x_kv, z_kv), (p_wo, c_wo, x_wo, z_wo), (p_qk, c_qk, x_qk, z_qk), (p_pw, c_pw, x_pw, z_pw), (p_ve, c_ve, x_ve, z_ve))
+    ek, eo, eq, ep, ev = [Scatter(at, *b, ss.at[i], sc.at[i], sx.at[i], sz.at[i]) for i, b in enumerate(sets)]
     steps = iter(range(15))
     def some(n):
         for _ in range(n):
@@ -1148,18 +1160,30 @@
     eo.step_z(1)
     unit(3)
     ek.begin()
-    some(1)
     ek.step_x(3)
     ek.step_x(2)
+    some(1)
+    loads[2].wait()
+    @pl.loop(0, 4)
+    def _(t):
+        blocks = pl.ds(pl.multiple_of(4 * t, 4), 4)
+        col = pl.ds(pl.multiple_of(384 * t, 384), 384)
+        p_qk[blocks] = dot_tn(normed[:, col], gqkv[:, :width]).astype(BF).reshape(4, 96, width)
+    ek.step_z(3)
+    ek.step_x(1)
+    eq.begin()
     eo.finish(wo_out)
     trade(0, wo_out, y0, y1)
-    some(1)
-    ek.step_z(3)
-    ek.step_x(1)
-    some(1)
     ek.step_z(2)
     ek.step_x(0)
+    eq.step_x(3)
+    eq.step_x(2)
     some(1)
+    @pl.loop(0, 4)
+    def _(t):
+        blocks = pl.ds(pl.multiple_of(4 * t, 4), 4)
+        col = pl.ds(pl.multiple_of(384 * t, 384), 384)
+        gatt[:, col] = dot_nt(gqkv[:, :width], wqkv[blocks, :, :width].reshape(384, width))
     ek.step_z(1)
     some(1)
     ek.finish(kvsum)
@@ -1168,16 +1192,18 @@
         kcol = slice(HEAD_DIM * h, HEAD_DIM * (h + 1))
         gqkv[:, width + HEAD_DIM * h : width + HEAD_DIM * (h + 1)] = spin(kvsum[:, kcol] * (HEAD_DIM ** -0.5), cos, -sin).astype(BF)
     gqkv[:, width + kw :] = kvsum[:, kw:].astype(BF)
-    loads[2].wait()
     @pl.loop(0, 4)
     def _(t):
         blocks = pl.ds(pl.multiple_of(4 * t, 4), 4)
         col = pl.ds(pl.multiple_of(384 * t, 384), 384)
-        p_qk[blocks] = dot_tn(normed[:, col], gqkv[...]).astype(BF).reshape(4, 96, width + 2 * kw)
-        gatt[:, col] = dot_nt(gqkv[...], wqkv[blocks].reshape(384, width + 2 * kw))
-    eq.begin()
-    eq.step_x(3)
-    eq.step_x(2)
+        p_pw[blocks] = dot_tn(normed[:, col], gqkv[:, width:]).astype(BF).reshape(4, 96, 2 * kw)
+        gatt[:, col] += dot_nt(gqkv[:, width:], wqkv[blocks, :, width:].reshape(384, 2 * kw))
+    ep.begin()
+    ep.step_x(3)
+    ep.step_x(2)
+    eq.step_z(3)
+    eq.step_x(1)
+    some(1)
     grad_norm, gain_one = norm_gradient(x_ref[...].astype(F32), vec[0:1, :width], gatt[...])
     grad_input[...] = gmid[...] + grad_norm
     bias = jnp.sum(gqkv[...].astype(F32), axis=0, keepdims=True)
@@ -1188,19 +1214,25 @@
     ev.begin()
     ev.step_x(3)
     ev.step_x(2)
-    some(2)
+    some(1)
+    late = (ep, ev)
     for kind, d in (("z", 3), ("x", 1), ("z", 2), ("x", 0), ("z", 1)):
-        for e in (eq, ev):
+        for e in late:
             (e.step_x if kind == "x" else e.step_z)(d)
+        if (kind, d) not in (("z", 3), ("x", 1)):
+            (eq.step_x if kind == "x" else eq.step_z)(d)
         some(1)
     some(15)
-    eq.finish(qkv_out)
-    trade(1, qkv_out, y2, y3)
+    eq.finish(q_out)
+    trade(1, q_out, y2, y3)
+    ep.finish(pair_out)
+    trade(2, pair_out, y4, y5)
     ev.finish(vec_out)
-    trade(2, vec_out, y4, y5)
+    trade(3, vec_out, y6, y7)
     traded(0, wo_out, y0, y1)
-    traded(1, qkv_out, y2, y3)
-    traded(2, vec_out, y4, y5)
+    traded(1, q_out, y2, y3)
+    traded(2, pair_out, y4, y5)
+    traded(3, vec_out, y6, y7)
     back.end()
 
 def backward(lens, gn2, mlp_out, mid, cot, x, att, q, normed, vec, cos, sin, valid, sel, fold, selk, foldk, kv, wo, wqkv, half, block, cid, window=4):
@@ -1217,13 +1249,13 @@
         return [VM((k,) + blk, BF) for k in (16, 8, 4, 5)]
     return pl.pallas_call(
         functools.partial(backward_kernel, block, window),
-        out_shape=[sds((rows, width), BF), sds((rows, width), F32), sds((own, wide), F32), sds((own, width), F32), sds((16, 128), F32), sds((3, own, 16 * MAIN), BF), sds((16, own, 256), BF)],
+        out_shape=[sds((rows, width), BF), sds((rows, width), F32), sds((own, width), F32), sds((own, wide - width), F32), sds((own, width), F32), sds((16, 128), F32), sds((3, own, 16 * MAIN), BF), sds((16, own, 256), BF)],
         in_specs=[pl.BlockSpec(memory_space=pltpu.SMEM)] + [vm] * 16 + [any_] * 4,
-        out_specs=[vm] * 5 + [any_] * 2,
+        out_specs=[vm] * 6 + [any_] * 2,
         scratch_shapes=[VM(kv.shape, BF), VM(wo.shape, BF), VM(wqkv.shape, BF), VM((rows, width), F32), VM((rows, width), BF), VM((rows, width), F32), VM((rows, wide), BF), VM((16, 16, 128), F32)]
-        + four((rows, kvw)) + four((own, width)) + four((own, wide)) + four((16, 128))
-        + [VM((rows, kvw), F32)] + [VM((own, width), BF)] * 2 + [VM((own, wide), BF)] * 2 + [VM((16, 128), BF)] * 2
-        + [dma((4, 16)), dma((4, 8)), dma((4, 4)), dma((4, 5))] + [dma((16,))] * 4 + [dma(()), dma((6,)), dma((3,))],
+        + four((rows, kvw)) + four((own, width)) + four((own, width)) + four((own, wide - width)) + four((16, 128))
+        + [VM((rows, kvw), F32)] + [VM((own, width), BF)] * 4 + [VM((own, wide - width), BF)] * 2 + [VM((16, 128), BF)] * 2
+        + [dma((5, 16)), dma((5, 8)), dma((5, 4)), dma((5, 5))] + [dma((16,))] * 4 + [dma(()), dma((8,)), dma((3,))],
         compiler_params=pltpu.CompilerParams(collective_id=cid, has_side_effects=True, vmem_limit_bytes=60 * 2**20),
     )(lens, gn2, mlp_out, mid, cot, x, att, q, normed, vec, cos, sin, valid, sel, fold, selk, foldk, kv, wo, wqkv, half)
 
@@ -1280,42 +1312,39 @@
 
     pieces = (gain_attn, b_query, b_key, b_value, gain_mlp)
     sizes = [p.shape[0] for p in pieces]
-    offsets = [sum(sizes[:i]) for i in range(len(sizes) + 1)]
-    small = jnp.pad(jnp.concatenate(pieces), (0, 16 * 128 - offsets[-1])).reshape(16, 128)
+    small = jnp.stack([jnp.pad(p.astype(F32), (0, 128 - p.shape[0])) for p in pieces])
+    small = jnp.pad(small, ((0, 8 - len(pieces)), (0, 0)))
     main = (hidden_units // 128 // group_count) * 128
     spare = hidden_units // group_count - main
     ff = (w_gate, w_up, w_down)
-    qkv_w, small, columns = weights(
-        w_query, w_key, w_value, *ff, spare_blocks(ff, main, spare), small, 1
-    )
-    small = small.reshape(group_count, 16 * 128)
-    gain_one, query_b, key_b, value_b, gain_two = [
-        small[:, offsets[i] : offsets[i + 1]].reshape(-1).astype(F32) for i in range(len(sizes))
-    ]
-    gap = (0, 2 * kv_width)
-    vec = jnp.stack(
-        [jnp.pad(gain_one, gap), jnp.concatenate((query_b, key_b, value_b)), jnp.pad(gain_two, gap)]
-    )
-    vec = jnp.pad(vec, ((0, 5), (0, 0)))
-
+    sel, fold = folding(group_count, model_width)
+    selk, foldk = folding(group_count, kv_width)
     rows_in = hidden_in.reshape(tokens, model_width)
     grad_final = (cotangent.reshape(tokens, model_width).astype(F32) * valid_rows).astype(BF)
-    q_rows, normed, attended, mid, normed_two, pair_all, grad_all, out_w = attend(
+    (
+        q_rows, normed, attended, mid, normed_two, vec, columns, qkv_w, pair_all, grad_all, out_w
+    ) = front(
         lengths,
         rows_in,
-        grad_final,
-        qkv_w.reshape(model_width, model_width + 2 * kv_width),
-        w_out,
-        vec,
         cos_rows,
         sin_rows,
+        sel,
+        fold,
+        selk,
+        foldk,
+        small,
+        w_query,
+        w_key,
+        w_value,
+        *ff,
+        spare_blocks(ff, main, spare),
+        grad_final,
+        w_out,
         block_len,
-        2,
+        1,
     )
     grad_normed_two, mlp_out, half_sum = mlp(normed_two, grad_all, columns, spare, 3)
-    sel, fold = folding(group_count, model_width)
-    selk, foldk = folding(group_count, kv_width)
-    layer_out, grad_input, qkv_sum, out_sum, vector_sum, main_sum, spare_sum = backward(
+    layer_out, grad_input, query_sum, pair_sum, out_sum, vector_sum, main_sum, spare_sum = backward(
         lengths,
         grad_normed_two,
         mlp_out,
@@ -1357,11 +1386,11 @@
         layer_out.reshape(hidden_in.shape),
         grad_input.reshape(hidden_in.shape),
         gain_one_sum,
-        qkv_sum[:, :model_width],
+        query_sum,
         query_bias_sum,
-        qkv_sum[:, model_width : model_width + kv_width],
+        pair_sum[:, :kv_width],
         key_bias_sum,
-        qkv_sum[:, model_width + kv_width :],
+        pair_sum[:, kv_width:],
         value_bias_sum,
         out_sum,
         gain_two_sum,

time: 518 us -> 489 us (0.944)
  Pallas kernels: 468 us -> 438 us
    pallas_call x2 -> x1, Pallas kernels: 186 us -> 165 us  [front(): pl.pallas_call(functools.partial(front_kernel, block), out_shape=[sds(act...]
    pallas_call x1, Pallas kernels: 142 us -> 134 us  [backward(): pl.pallas_call(functools.partial(backward_kernel, block, window), out_sha...]
where the time goes in v6:
time: 489 us; the launch traced here: 483 us
  Pallas kernels  438 us (90%)
  local copies, waits for them, and re-layouts  29.5 us (6%)
  other arithmetic  14.9 us (3%)
    pallas_call x1, Pallas kernels, front(): pl.pallas_call(functools.partial(front_kernel, block), out_shape=[sds(act...  165 us
    pallas_call x1, Pallas kernels, mlp(): pl.pallas_call(functools.partial(mlp_kernel, spare), out_shape=[jax.Shape...  139 us
    pallas_call x1, Pallas kernels, backward(): pl.pallas_call(functools.partial(backward_kernel, block, window), out_sha...  134 us

profile of v6, /device:TPU:0, one launch (start us, length us, event | category | flops | bytes accessed | tf_op | source)
XLA Modules:
  0.0 483.2 jit_solution(12254689685738876946)
XLA Ops:
  4.2 1.9 fusion.cot_ref.cot
  7.6 1.0 fusion.1.fold
  10.6 0.9 slice.48
  12.0 0.9 slice.49
  13.8 2.0 concatenate.24
  15.8 165.4 %shard_map.254 = (bf16[128,1536]{1,0:T(8,128)(2,1)}, bf16[128,1536]{1,0:T(8,128)(2,1)}, f32[128,1536]{1,0:T(8,128)}, f32[128,1536]{1,0:T(8,128)}, bf16[128,1536]...) custom-call(s32[2]{0:T(128)} %lens.3, ...), custom_call_target="tpu_custom_call" | custom-call | tf_op jit(solution)/shard_map/pallas_call | solution.py:1017
  181.2 138.7 %shard_map.255 = (f32[128,1536]{1,0:T(8,128)}, f32[128,1536]{1,0:T(8,128)}, bf16[16,48,1792]{2,1,0:T(8,128)(2,1)}) custom-call(bf16[128,1536]{1,0:T(8,128)(2,1)} %get-tuple-element.36.n2_ref, bf16[16,128,1536]{2,1,0:T(8,128)(2,1)} %get-tuple-element.37.cot_ref, bf16[1536,1792]{1,0:T(8,128)(2,1)} %get-tuple-element.38.w_ref), custom_call_target="tpu_custom_call" | custom-call | tf_op jit(solution)/shard_map/pallas_call | solution.py:765
  319.9 1.0 mul.59.valid
  320.9 133.5 %shard_map.256 = (bf16[128,1536]{1,0:T(8,128)(2,1)}, f32[128,1536]{1,0:T(8,128)}, f32[96,1536]{1,0:T(8,128)}, f32[96,512]{1,0:T(8,128)}, f32[96,1536]{1,0:T(8,12...) custom-call(s32[2]{0:T(128)} %lens.3, f32[128,1536]{1,0:T(8,128)} %get-tuple-element.39.gn2, ...), custom_call_target="tpu_custom_call" | custom-call | tf_op jit(solution)/shard_map/pallas_call | solution.py:1250
  454.4 3.9 slice_bitcast_fusion
  458.4 1.1 slice_bitcast_fusion.3
  459.5 1.8 copy.39
  461.3 1.7 copy.40
  463.0 3.5 maximum_convert_fusion.2
  466.5 1.8 copy.37
  468.4 1.7 copy.38
  470.1 2.9 maximum_convert_fusion.1
  473.3 2.0 maximum_convert_fusion
  475.3 1.6 fusion.16
  476.9 1.3 slice_bitcast_fusion.6
  478.2 1.3 slice_bitcast_fusion.7
  480.3 0.9 copy.49
  481.1 0.8 copy.50
  482.0 0.8 copy.51
  (44 shorter events, 9.4 us)
Async XLA Ops:
  0.6 12.7 %slice-start = ((bf16[96,8960]{1,0:T(8,128)(2,1)}), bf16[96,768]{1,0:T(8,128)(2,1)S(1)}, s32[]{:S(2)}) async-start(bf16[96,8960]{1,0:T(8,128)(2,1)} %wd.1), calls=%async_computation | async-start | bytes 294912 | tf_op jit(solution)/shard_map/slice | solution.py:1266
  454.4 4.0 copy-start
  473.0 6.5 %copy-start.4 = (bf16[128,1536]{1,0:T(8,128)(2,1)S(1)}, bf16[128,1536]{1,0:T(8,128)(2,1)}, u32[]{:S(2)}) copy-start(bf16[128,1536]{1,0:T(8,128)(2,1)} %get-tuple-element.50) | copy-start | bytes 1179652
  473.2 7.1 %copy-start.1 = (f32[128,1536]{1,0:T(8,128)S(1)}, f32[128,1536]{1,0:T(8,128)}, u32[]{:S(2)}) copy-start(f32[128,1536]{1,0:T(8,128)} %get-tuple-element.51) | copy-start | bytes 2359300
  473.3 7.8 %copy-start.3 = (f32[96,1536]{1,0:T(8,128)S(1)}, f32[96,1536]{1,0:T(8,128)}, u32[]{:S(2)}) copy-start(f32[96,1536]{1,0:T(8,128)} %get-tuple-element.96) | copy-start | bytes 1769476
  473.3 8.6 %copy-start.2 = (f32[96,1536]{1,0:T(8,128)S(1)}, f32[96,1536]{1,0:T(8,128)}, u32[]{:S(2)}) copy-start(f32[96,1536]{1,0:T(8,128)} %get-tuple-element.102) | copy-start | bytes 1769476

commit v7 on v6

--- a/solution.py
+++ b/solution.py
@@ -2,6 +2,7 @@
 
 import jax
 import jax.numpy as jnp
+import numpy as np
 from jax import lax
 from jax.experimental import pallas as pl
 from jax.experimental.pallas import tpu as pltpu
@@ -11,7 +12,7 @@
 NZ = 4
 MAIN = 512
 D = 1536
-COLS = 3 * MAIN + 256
+COLS = 3 * MAIN + 384
 HEADS = 12
 KV_HEADS = 2
 HEAD_DIM = 128
@@ -561,55 +562,86 @@
 KS = (8, 1, 9, 2, 10, 3, 11, 4, 12, 5, 13, 6, 14, 7, 15)
 WINDOW = 4
 
+def has(j):
+    return lax.rem(j, 3) == 0
+
+def spare_at(j):
+    return pl.ds(pl.multiple_of(16 * MAIN + 128 * (j // 3), 128), 128)
+
 class Deal:
-    def __init__(self, at, ws, rem, buf, send, recv, ysend, yrecv, local):
+    def __init__(self, at, ws, buf, sems, local):
         self.r, self.z, self.x, self.c = at
         self.me = idx(self.z, self.x, self.c)
-        self.ws, self.rem, self.buf = ws, rem, buf
-        self.send, self.recv, self.ysend, self.yrecv, self.local = send, recv, ysend, yrecv, local
-        self.half = ws[0].shape[0] // 2
+        self.ws, self.buf, self.sems, self.local = ws, buf, sems, local
+        self.n = ws[0].shape[0] // 2
     def rows(self, j, h):
-        n = self.half
-        return self.buf.at[pl.ds(pl.multiple_of((2 * j + h) * n, n), n)]
+        return pl.ds(pl.multiple_of((2 * j + h) * self.n, self.n), self.n)
+    def block(self, j, h, spare):
+        return self.buf.at[self.rows(j, h), pl.ds(3 * MAIN, 384) if spare else pl.ds(0, 3 * MAIN)]
+    def copy(self, a, b, kind, k, dev):
+        send, recv = self.sems[2 * kind : 2 * kind + 2]
+        return pltpu.make_async_remote_copy(a, b, send.at[k], recv.at[k], device_id=dev, device_id_type=MESH)
     def launch(self, k):
-        r, me, n = self.r, self.me, self.half
+        r, me, n = self.r, self.me, self.n
         row = pl.ds(pl.multiple_of(r * n, n), n)
         j = jnp.bitwise_xor(me, k)
-        dev = (r, j)
         dst = self.rows(me, r)
-        col = pl.ds(pl.multiple_of(j * MAIN, MAIN), MAIN)
         for i in range(3):
-            pltpu.make_async_remote_copy(self.ws[i].at[row, col], dst.at[:, pl.ds(i * MAIN, MAIN)], self.send.at[k], self.recv.at[k], device_id=dev, device_id_type=MESH).start()
-        pltpu.make_async_remote_copy(self.rem.at[j, row], dst.at[:, pl.ds(3 * MAIN, 256)], self.send.at[k], self.recv.at[k], device_id=dev, device_id_type=MESH).start()
+            self.copy(self.ws[i].at[row, pl.ds(pl.multiple_of(j * MAIN, MAIN), MAIN)], self.buf.at[dst, pl.ds(i * MAIN, MAIN)], 0, k, (r, j)).start()
+        def spare():
+            for i in range(3):
+                self.copy(self.ws[i].at[row, spare_at(j)], self.buf.at[dst, pl.ds(3 * MAIN + 128 * i, 128)], 1, k, (r, j)).start()
+        when(has(j), spare)
+    def locals(self, spare):
+        me, n = self.me, self.n
+        row = pl.ds(pl.multiple_of(2 * me * n, 2 * n), 2 * n)
+        col = spare_at(me) if spare else pl.ds(pl.multiple_of(me * MAIN, MAIN), MAIN)
+        for i in range(3):
+            to = pl.ds(3 * MAIN + 128 * i, 128) if spare else pl.ds(i * MAIN, MAIN)
+            yield pltpu.make_async_copy(self.ws[i].at[:, col], self.buf.at[row, to], self.local.at[1 if spare else 0])
     def begin(self):
-        me, n = self.me, self.half
         for k in KS[:WINDOW]:
             self.launch(k)
-        col = pl.ds(pl.multiple_of(me * MAIN, MAIN), MAIN)
-        own = self.buf.at[pl.ds(pl.multiple_of(2 * me * n, 2 * n), 2 * n)]
-        for i in range(3):
-            pltpu.make_async_copy(self.ws[i].at[:, col], own.at[:, pl.ds(i * MAIN, MAIN)], self.local).start()
-        pltpu.make_async_copy(self.rem.at[me], own.at[:, pl.ds(3 * MAIN, 256)], self.local).start()
+        for l in self.locals(False):
+            l.start()
+        def spare():
+            for l in self.locals(True):
+                l.start()
+        when(has(self.me), spare)
     def step(self, i):
         k = KS[i]
         r, me = self.r, self.me
         j = jnp.bitwise_xor(me, k)
-        blk = self.rows(j, r)
         dev = (1 - r, me)
-        pltpu.make_async_remote_copy(blk, blk, self.send.at[k], self.recv.at[k], device_id=dev, device_id_type=MESH).wait_recv()
-        pltpu.make_async_remote_copy(blk, blk, self.ysend.at[k], self.yrecv.at[k], device_id=dev, device_id_type=MESH).start()
+        def pass_on(spare):
+            blk = self.block(j, r, spare)
+            self.copy(blk, blk, spare, k, dev).wait_recv()
+            self.copy(blk, blk, 2 + spare, k, dev).start()
+        pass_on(0)
+        when(has(me), lambda: pass_on(1))
         if i + WINDOW < 15:
             self.launch(KS[i + WINDOW])
     def end(self):
-        r, me = self.r, self.me
+        r, me, n = self.r, self.me, self.n
         dev = (1 - r, me)
-        for k in range(1, 16):
+        for k in KS:
             j = jnp.bitwise_xor(me, k)
-            blk = self.rows(j, 1 - r)
-            pltpu.make_async_remote_copy(blk, blk, self.ysend.at[k], self.yrecv.at[k], device_id=dev, device_id_type=MESH).wait()
-            pltpu.make_async_remote_copy(blk, blk, self.send.at[k], self.recv.at[k], device_id=dev, device_id_type=MESH).wait_send()
-        own = self.buf.at[pl.ds(pl.multiple_of(2 * me * self.half, 2 * self.half), 2 * self.half)]
-        pltpu.make_async_copy(own, own, self.local).wait()
+            def done(spare):
+                blk = self.block(j, 1 - r, spare)
+                self.copy(blk, blk, 2 + spare, k, dev).wait()
+            def sent(spare):
+                blk = self.block(j, r, spare)
+                self.copy(blk, blk, spare, k, dev).wait_send()
+            done(0)
+            sent(0)
+            when(has(me), lambda: done(1))
+            when(has(j), lambda: sent(1))
+        row = pl.ds(pl.multiple_of(2 * me * n, 2 * n), 2 * n)
+        def own(spare):
+            blk = self.buf.at[row, pl.ds(3 * MAIN, 384) if spare else pl.ds(0, 3 * MAIN)]
+            pltpu.make_async_copy(blk, blk, self.local.at[spare]).wait()
+        own(0)
+        when(has(me), lambda: own(1))
 
 def hail_all(r, z, x, c):
     bar = pltpu.get_barrier_semaphore()
@@ -632,19 +664,25 @@
     silu = g * sig
     return (gh * u * (sig * (1.0 + g * (1.0 - sig)))).astype(BF), (gh * silu).astype(BF), (silu * u).astype(BF)
 
-def mlp_kernel(spare, n2_ref, cot_ref, w_ref, gsum, osum, half_ref,
+def mlp_kernel(n2_ref, cot_ref, w_ref, gsum, osum, half_ref,
                n2, cot, w, act, pg, po, rcg, rxg, rzg, rco, rxo, rzo, yb,
-               gsend, grecv, glocal, lsem, ssend, srcs, srxs, srzs, ysend, yrecv):
+               gsend, grecv, glocal, lsem, ssend, srcs, srxs, srzs, ysend, yrecv, xsend, xrecv):
     at = place()
     r, z, x, c = at
-    loads = [pltpu.make_async_copy(w_ref, w, lsem.at[0]), pltpu.make_async_copy(cot_ref, cot, lsem.at[1])]
+    me = idx(z, x, c)
+    extra = has(me)
+    MM, SP = pl.ds(0, 3 * MAIN), pl.ds(3 * MAIN, 384)
+    loads = [pltpu.make_async_copy(w_ref.at[:, MM], w.at[:, MM], lsem.at[0]), pltpu.make_async_copy(cot_ref, cot, lsem.at[1])]
     for l in loads: l.start()
+    load_spare = pltpu.make_async_copy(w_ref.at[:, SP], w.at[:, SP], lsem.at[3])
+    when(extra, load_spare.start)
     greet(*at, with_y=True)
     g = Gather(at, n2_ref, n2, gsend, grecv, glocal)
     rg = Scatter(at, pg, rcg, rxg, rzg, ssend.at[0], srcs.at[0], srxs.at[0], srzs.at[0])
     ro = Scatter(at, po, rco, rxo, rzo, ssend.at[1], srcs.at[1], srxs.at[1], srzs.at[1])
     g.begin()
     for l in loads: l.wait()
+    when(extra, load_spare.wait)
     mid = (z > 0) & (z < NZ - 1)
     p = [z,
          jnp.where(z == 0, 1, jnp.where(z == 1, 0, jnp.where(z == 2, 3, 2))),
@@ -664,25 +702,26 @@
             act[tok, col(0)] = dg
             act[tok, col(MAIN)] = du
             act[tok, col(2 * MAIN)] = h
-        a = n2[rows].reshape(512, D)
-        k = cot[rows].reshape(512, D)
-        pre = dot(a, w[:, 3 * MAIN : 3 * MAIN + 128])
-        gh = dot(k, w[:, 3 * MAIN + 128 :])
-        lane = lax.broadcasted_iota(jnp.int32, (512, 128), 1)
-        sig = jax.nn.sigmoid(pre)
-        silu = pre * sig
-        up = pltpu.roll(pre, 128 - spare, 1)
-        dg = gh * up * (sig * (1.0 + pre * (1.0 - sig)))
-        du = pltpu.roll(gh * silu, spare, 1)
-        act[tok, 3 * MAIN : 3 * MAIN + 128] = jnp.where(lane < spare, dg, jnp.where(lane < 2 * spare, du, 0.0)).astype(BF)
-        act[tok, 3 * MAIN + 128 :] = jnp.where(lane < spare, silu * up, 0.0).astype(BF)
-        @pl.loop(0, D // 256)
-        def _(t):
-            dr = pl.ds(pl.multiple_of(256 * t, 256), 256)
-            v = dot_nt(act[tok, : 2 * MAIN], w[dr, : 2 * MAIN]) + dot_nt(act[tok, 3 * MAIN : 3 * MAIN + 128], w[dr, 3 * MAIN : 3 * MAIN + 128])
-            pg[rows, :, dr] = v.astype(BF).reshape(4, 128, 256)
-            v = dot_nt(act[tok, 2 * MAIN : 3 * MAIN], w[dr, 2 * MAIN : 3 * MAIN]) + dot_nt(act[tok, 3 * MAIN + 128 :], w[dr, 3 * MAIN + 128 :])
-            po[rows, :, dr] = v.astype(BF).reshape(4, 128, 256)
+        def spare():
+            pre = dot(n2[rows].reshape(512, D), w[:, 3 * MAIN : 3 * MAIN + 256])
+            dg, du, h = gated(pre[:, :128], pre[:, 128:], dot(cot[rows].reshape(512, D), w[:, 3 * MAIN + 256 :]))
+            act[tok, 3 * MAIN : 3 * MAIN + 128] = dg
+            act[tok, 3 * MAIN + 128 : 3 * MAIN + 256] = du
+            act[tok, 3 * MAIN + 256 :] = h
+        when(extra, spare)
+        def out_tiles(more):
+            @pl.loop(0, D // 256)
+            def _(t):
+                dr = pl.ds(pl.multiple_of(256 * t, 256), 256)
+                v = dot_nt(act[tok, : 2 * MAIN], w[dr, : 2 * MAIN])
+                u = dot_nt(act[tok, 2 * MAIN : 3 * MAIN], w[dr, 2 * MAIN : 3 * MAIN])
+                if more:
+                    v += dot_nt(act[tok, 3 * MAIN : 3 * MAIN + 256], w[dr, 3 * MAIN : 3 * MAIN + 256])
+                    u += dot_nt(act[tok, 3 * MAIN + 256 :], w[dr, 3 * MAIN + 256 :])
+                pg[rows, :, dr] = v.astype(BF).reshape(4, 128, 256)
+                po[rows, :, dr] = u.astype(BF).reshape(4, 128, 256)
+        when(extra, lambda: out_tiles(True))
+        when(~extra, lambda: out_tiles(False))
         rg.send_c(zz)
         ro.send_c(zz)
 
@@ -707,9 +746,11 @@
     ydev = (1 - r, idx(z, x, c))
     own = D // 16
     half = own // 2
-    def ycopy(j):
-        src = w.at[pl.ds(pl.multiple_of(own * j + half * (1 - r), half), half)]
-        return pltpu.make_async_remote_copy(src, yb.at[j], ysend.at[j], yrecv.at[j], device_id=ydev, device_id_type=MESH)
+    def ycopy(j, spare):
+        cols = SP if spare else MM
+        src = w.at[pl.ds(pl.multiple_of(own * j + half * (1 - r), half), half), cols]
+        a, b = (xsend, xrecv) if spare else (ysend, yrecv)
+        return pltpu.make_async_remote_copy(src, yb.at[j, :, cols], a.at[j], b.at[j], device_id=ydev, device_id_type=MESH)
     def grads(q):
         dr = slice(384 * q, 384 * (q + 1))
         row = slice(384 * q, 384 * (q + 1))
@@ -721,15 +762,23 @@
         def _(t):
             col = pl.ds(pl.multiple_of(2 * MAIN + 256 * t, 256), 256)
             w[row, col] = dot_tn(cot[:, :, dr].reshape(2048, 384), act[:, col]).astype(BF)
-        w[row, 3 * MAIN : 3 * MAIN + 128] = dot_tn(n2[:, :, dr].reshape(2048, 384), act[:, 3 * MAIN : 3 * MAIN + 128]).astype(BF)
-        w[row, 3 * MAIN + 128 :] = dot_tn(cot[:, :, dr].reshape(2048, 384), act[:, 3 * MAIN + 128 :]).astype(BF)
         for j in range(4 * q, 4 * q + 4):
-            ycopy(j).start()
+            ycopy(j, 0).start()
+        def spare():
+            w[row, 3 * MAIN : 3 * MAIN + 256] = dot_tn(n2[:, :, dr].reshape(2048, 384), act[:, 3 * MAIN : 3 * MAIN + 256]).astype(BF)
+            w[row, 3 * MAIN + 256 :] = dot_tn(cot[:, :, dr].reshape(2048, 384), act[:, 3 * MAIN + 256 :]).astype(BF)
+            for j in range(4 * q, 4 * q + 4):
+                ycopy(j, 1).start()
+        when(extra, spare)
     def yadd(j):
-        ycopy(j).wait()
-        mine = w[pl.ds(pl.multiple_of(own * j + half * r, half), half)]
-        yb[j] = (mine.astype(F32) + yb[j].astype(F32)).astype(BF)
-        pltpu.make_async_copy(yb.at[j], half_ref.at[j], lsem.at[2]).start()
+        def add(spare):
+            cols = SP if spare else MM
+            ycopy(j, spare).wait()
+            mine = w[pl.ds(pl.multiple_of(own * j + half * r, half), half), cols]
+            yb[j, :, cols] = (mine.astype(F32) + yb[j, :, cols].astype(F32)).astype(BF)
+            pltpu.make_async_copy(yb.at[j, :, cols], half_ref.at[j, :, cols], lsem.at[4 if spare else 2]).start()
+        add(0)
+        when(extra, lambda: add(1))
 
     rg.step_x(3)
     rg.step_x(2)
@@ -755,15 +804,16 @@
     for j in range(8, 12): yadd(j)
     ro.finish(osum)
     for j in range(12, 16): yadd(j)
-    pltpu.make_async_copy(yb, half_ref, lsem.at[2]).wait()
+    pltpu.make_async_copy(yb.at[:, :, MM], half_ref.at[:, :, MM], lsem.at[2]).wait()
+    when(extra, lambda: pltpu.make_async_copy(yb.at[:, :, SP], half_ref.at[:, :, SP], lsem.at[4]).wait())
     g.end(local=False)
 
-def mlp(n2, cot, w, spare, cid):
+def mlp(n2, cot, w, cid):
     blk = n2.shape
     dma = pltpu.SemaphoreType.DMA
     full = (16,) + blk
     return pl.pallas_call(
-        functools.partial(mlp_kernel, spare),
+        mlp_kernel,
         out_shape=[jax.ShapeDtypeStruct(blk, F32)] * 2 + [jax.ShapeDtypeStruct((16, D // 32, COLS), BF)],
         in_specs=[pl.BlockSpec(memory_space=pl.ANY)] * 3,
         out_specs=[pl.BlockSpec(memory_space=pltpu.VMEM)] * 2 + [pl.BlockSpec(memory_space=pl.ANY)],
@@ -771,7 +821,7 @@
                         pltpu.VMEM(full, BF), pltpu.VMEM(full, BF)]
         + [pltpu.VMEM((k,) + blk, BF) for k in (8, 4, 5, 8, 4, 5)]
         + [pltpu.VMEM((16, D // 32, COLS), BF)]
-        + [dma((18,)), dma((16,)), dma(()), dma((3,)), dma((2, 16)), dma((2, 8)), dma((2, 4)), dma((2, 5)), dma((16,)), dma((16,))],
+        + [dma((18,)), dma((16,)), dma(()), dma((5,)), dma((2, 16)), dma((2, 8)), dma((2, 4)), dma((2, 5))] + [dma((16,))] * 4,
         compiler_params=pltpu.CompilerParams(collective_id=cid, has_side_effects=True, vmem_limit_bytes=60 * 2**20),
     )(n2, cot, w)
 
@@ -879,23 +929,29 @@
         sent(18 + own, self.out.at[0])
         pltpu.make_async_copy(self.src, self.out.at[0], self.local).wait()
 
-def front_kernel(block, lens, x_ref, cos_ref, sin_ref, sel, fold, selk, foldk, small, wq, wk, wv, wg, wu, wd, rem, cot_ref, wo_ref,
+def front_kernel(block, lens, x_ref, cot_ref, v0, v1, v2, v3, v4, sel, fold, selk, foldk, rope_ref, wq, wk, wv, wg, wu, wd, wo_ref,
                  q_out, normed_out, att_out, mid_out, n2_out, vec, buf, qkv_out, kv_out, cot_out, wo_out,
-                 qkv_own, wqkv, small_all, own, kv, wo,
-                 qs, qr, ql, vs, vr, vl, ks, kr, kl, cs, cr, cl, ws, wr, wl, ds, dr, ys, yr, dl, lsem):
+                 rope, cot_own, small, qkv_own, wqkv, small_all, own, kv, wo,
+                 qs, qr, ql, vs, vr, vl, ks, kr, kl, cs, cr, cl, ws, wr, wl, d0, d1, d2, d3, d4, d5, d6, d7, dl, lsem):
     at = place()
     width = HEADS * HEAD_DIM
     kw = KV_HEADS * HEAD_DIM
     loads = [pltpu.make_async_copy(w, qkv_own.at[:, pl.ds(o, n)], lsem.at[i]) for i, (w, o, n) in enumerate(((wq, 0, width), (wk, width, kw), (wv, width + kw, kw)))]
+    first_row = lax.axis_index("group") * block
+    loads.append(pltpu.make_async_copy(rope_ref.at[:, pl.ds(pl.multiple_of(first_row, block), block)], rope, lsem.at[6]))
     for l in loads: l.start()
+    small[...] = jnp.zeros_like(small)
+    for i, v in enumerate((v0, v1, v2, v3, v4)):
+        small[i : i + 1, : v.shape[1]] = v[...].astype(F32)
+    cot_own[...] = (cot_ref[...].astype(F32) * row_mask(lens, first_row, block, (cot_ref.shape[0], 1))).astype(BF)
     hail_all(*at)
     for l in loads: l.wait()
     gq = GatherY(at, qkv_own, wqkv, qs, qr, ql)
     gv = Gather(at, small, small_all, vs, vr, vl)
     gk = Gather(at, own, kv, ks, kr, kl)
-    gc = Gather(at, cot_ref, cot_out, cs, cr, cl)
+    gc = Gather(at, cot_own, cot_out, cs, cr, cl)
     gw = GatherY(at, wo_ref, wo, ws, wr, wl)
-    d = Deal(at, (wg, wu, wd), rem, buf, ds, dr, ys, yr, dl)
+    d = Deal(at, (wg, wu, wd), buf, (d0, d1, d2, d3, d4, d5, d6, d7), dl)
     steps = iter(range(15))
     def some(n):
         for _ in range(n):
@@ -932,7 +988,7 @@
         t = dot_nt(small_all[:, i, :].astype(BF), b[...])
         vec[row : row + 1, first : first + a.shape[1]] = jnp.sum(t * a[...], axis=0, keepdims=True)
     normed_out[...] = rms(x, vec[0:1, :width]).astype(BF)
-    cos, sin = cos_ref[...], sin_ref[...]
+    cos, sin = [jnp.concatenate((rope[i], rope[i]), axis=0) for i in range(2)]
     def product(base):
         return dot(normed_out[...], wqkv[:, :, pl.ds(pl.multiple_of(base, 256), 256)].reshape(width, 256)) + vec[1:2, pl.ds(pl.multiple_of(base, 256), 256)]
     pre = product(width)
@@ -966,7 +1022,6 @@
         gk.from_c(zz)
     gk.end()
     keep[1].start()
-    first_row = lax.axis_index("group") * block
     span = 16 * block
     @pl.loop(0, 4)
     def _(u):
@@ -1003,7 +1058,7 @@
 
 EARLY = (2, 1, 1, 2, 3)
 
-def front(lens, x, cos, sin, sel, fold, selk, foldk, small, wq, wk, wv, wg, wu, wd, rem, cot, wo, block, cid):
+def front(lens, x, cot, vectors, sel, fold, selk, foldk, rope, wq, wk, wv, wg, wu, wd, wo, block, cid):
     rows, width = x.shape
     any_ = pl.BlockSpec(memory_space=pl.ANY)
     vm = pl.BlockSpec(memory_space=pltpu.VMEM)
@@ -1017,59 +1072,87 @@
     return pl.pallas_call(
         functools.partial(front_kernel, block),
         out_shape=[sds(act, BF), sds(act, BF), sds(act, F32), sds(act, F32), sds(act, BF), sds((8, wide), F32),
-                   sds((16 * own, 3 * MAIN + 256), BF), sds((16, own, wide), BF), sds((16, rows, kvw), BF), sds((16,) + act, BF), sds((16,) + wo.shape, BF)],
-        in_specs=[pl.BlockSpec(memory_space=pltpu.SMEM)] + [vm] * 7 + [any_] * 10,
+                   sds((16 * own, 3 * MAIN + 384), BF), sds((16, own, wide), BF), sds((16, rows, kvw), BF), sds((16,) + act, BF), sds((16,) + wo.shape, BF)],
+        in_specs=[pl.BlockSpec(memory_space=pltpu.SMEM)] + [vm] * 11 + [any_] * 8,
         out_specs=[vm] * 6 + [any_] * 5,
-        scratch_shapes=[VM((own, wide), BF), VM((16, own, wide), BF), VM((16,) + small.shape, F32), VM((rows, kvw), BF), VM((16, rows, kvw), BF), VM((16,) + wo.shape, BF)]
+        scratch_shapes=[VM((2, block, HEAD_DIM), F32), VM(act, BF), VM((8, 128), F32), VM((own, wide), BF), VM((16, own, wide), BF), VM((16, 8, 128), F32), VM((rows, kvw), BF), VM((16, rows, kvw), BF), VM((16,) + wo.shape, BF)]
         + [dma((34,)), dma((32,)), dma(())] + [dma((18,)), dma((16,)), dma(())] * 3 + [dma((34,)), dma((32,)), dma(())]
-        + [dma((16,))] * 4 + [dma(()), dma((6,))],
+        + [dma((16,))] * 8 + [dma((2,)), dma((7,))],
         compiler_params=pltpu.CompilerParams(collective_id=cid, has_side_effects=True, vmem_limit_bytes=60 * 2**20),
-    )(lens, x, cos, sin, sel, fold, selk, foldk, small, wq, wk, wv, wg, wu, wd, rem, cot, wo)
+    )(lens, x, cot, *vectors, sel, fold, selk, foldk, rope, wq, wk, wv, wg, wu, wd, wo)
 
 
 class Return:
-    def __init__(self, at, half_ref, main, spare, send, recv, ysend, yrecv, local):
+    def __init__(self, at, half_ref, out, sems, local):
         self.r, self.z, self.x, self.c = at
         self.me = idx(self.z, self.x, self.c)
-        self.src, self.main, self.spare = half_ref, main, spare
-        self.send, self.recv, self.ysend, self.yrecv, self.local = send, recv, ysend, yrecv, local
+        self.src, self.out, self.sems, self.local = half_ref, out, sems, local
         self.n = half_ref.shape[1]
-    def places(self, j, h):
-        row = pl.ds(pl.multiple_of(h * self.n, self.n), self.n)
-        col = pl.ds(pl.multiple_of(j * MAIN, MAIN), MAIN)
-        return [self.main.at[i, row, col] for i in range(3)] + [self.spare.at[j, row]]
-    def parts(self, j):
-        return [self.src.at[j, :, pl.ds(i * MAIN, MAIN)] for i in range(3)] + [self.src.at[j, :, pl.ds(3 * MAIN, 256)]]
+    def places(self, j, spare):
+        row = pl.ds(pl.multiple_of(self.r * self.n, self.n), self.n)
+        col = spare_at(j) if spare else pl.ds(pl.multiple_of(j * MAIN, MAIN), MAIN)
+        return [self.out.at[i, row, col] for i in range(3)]
+    def parts(self, j, spare):
+        if spare:
+            return [self.src.at[j, :, pl.ds(3 * MAIN + 128 * i, 128)] for i in range(3)]
+        return [self.src.at[j, :, pl.ds(i * MAIN, MAIN)] for i in range(3)]
+    def copy(self, a, b, kind, k, dev):
+        send, recv = self.sems[2 * kind : 2 * kind + 2]
+        return pltpu.make_async_remote_copy(a, b, send.at[k], recv.at[k], device_id=dev, device_id_type=MESH)
     def launch(self, k):
         j = jnp.bitwise_xor(self.me, k)
-        for a, b in zip(self.parts(j), self.places(self.me, self.r)):
-            pltpu.make_async_remote_copy(a, b, self.send.at[k], self.recv.at[k], device_id=(self.r, j), device_id_type=MESH).start()
-    def forward(self, j, k):
-        for a in self.places(j, self.r):
-            pltpu.make_async_remote_copy(a, a, self.ysend.at[k], self.yrecv.at[k], device_id=(1 - self.r, self.me), device_id_type=MESH).start()
+        def go(spare):
+            for a, b in zip(self.parts(j, spare), self.places(self.me, spare)):
+                self.copy(a, b, spare, k, (self.r, j)).start()
+        go(0)
+        when(has(self.me), lambda: go(1))
+    def forward(self, j, k, spare):
+        for a in self.places(j, spare):
+            self.copy(a, a, 2 + spare, k, (1 - self.r, self.me)).start()
     def begin(self, window):
         self.window = window
-        for a, b in zip(self.parts(self.me), self.places(self.me, self.r)):
-            pltpu.make_async_copy(a, b, self.local).start()
+        def go(spare):
+            for a, b in zip(self.parts(self.me, spare), self.places(self.me, spare)):
+                pltpu.make_async_copy(a, b, self.local.at[spare]).start()
+        go(0)
+        when(has(self.me), lambda: go(1))
         for k in KS[:window]:
             self.launch(k)
-    def whole(self, send, recv):
-        blk = self.src.at[0]
-        return pltpu.make_async_remote_copy(blk, blk, send, recv, device_id=(1 - self.r, self.me), device_id_type=MESH)
+    def sized(self, spare):
+        return self.src.at[0, :, pl.ds(3 * MAIN, 384) if spare else pl.ds(0, 3 * MAIN)]
+    def whole(self, kind, k):
+        blk = self.sized(kind % 2)
+        return self.copy(blk, blk, kind, k, (1 - self.r, self.me))
     def own(self):
-        pltpu.make_async_copy(self.src.at[0], self.src.at[0], self.local).wait()
-        self.forward(self.me, 0)
+        def go(spare):
+            blk = self.sized(spare)
+            pltpu.make_async_copy(blk, blk, self.local.at[spare]).wait()
+            self.forward(self.me, 0, spare)
+        go(0)
+        when(has(self.me), lambda: go(1))
     def step(self, i):
         k = KS[i]
-        self.whole(self.send.at[k], self.recv.at[k]).wait_recv()
-        self.forward(jnp.bitwise_xor(self.me, k), k)
+        j = jnp.bitwise_xor(self.me, k)
+        def go(spare):
+            self.whole(spare, k).wait_recv()
+            self.forward(j, k, spare)
+        go(0)
+        when(has(j), lambda: go(1))
         if i + self.window < 15:
             self.launch(KS[i + self.window])
     def end(self):
         for k in (0,) + KS:
-            self.whole(self.ysend.at[k], self.yrecv.at[k]).wait()
+            j = jnp.bitwise_xor(self.me, k)
+            self.whole(2, k).wait()
+            when(has(j), lambda: self.whole(3, k).wait())
             if k:
-                self.whole(self.send.at[k], self.recv.at[k]).wait_send()
+                self.whole(0, k).wait_send()
+                when(has(self.me), lambda: self.whole(1, k).wait_send())
+
+def row_mask(lens, first_row, block, shape):
+    row = lax.broadcasted_iota(jnp.int32, shape, 0)
+    place = jnp.bitwise_and(row, block - 1) + first_row
+    return jnp.where(place < jnp.where(row < block, lens[0], lens[1]), 1.0, 0.0)
 
 def norm_gradient(v, gain, upstream):
     factor = lax.rsqrt(jnp.mean(v * v, axis=-1, keepdims=True) + EPSILON)
@@ -1077,20 +1160,22 @@
     inner = jnp.mean(weighted * v, axis=-1, keepdims=True)
     return factor * weighted - v * (factor * factor * factor) * inner, jnp.sum(upstream * v * factor, axis=0, keepdims=True)
 
-def backward_kernel(block, window, lens, gn2, mlp_out, mid, cot, x_ref, att, q_ref, normed, vec, cos_ref, sin_ref, valid, sel, fold, selk, foldk, kv_ref, wo_ref, wqkv_ref, half_ref,
-                    layer_out, grad_input, q_out, pair_out, wo_out, vec_out, g_main, g_spare,
-                    kv, wo, wqkv, gmid, branch, gatt, gqkv, pv,
+def backward_kernel(block, window, lens, gn2, mlp_out, mid, cot, x_ref, att, q_ref, normed, vec, sel, fold, selk, foldk, rope_ref, kv_ref, wo_ref, wqkv_ref, half_ref,
+                    layer_out, grad_input, q_out, pair_out, wo_out, vec_out, g_out,
+                    rope, kv, wo, wqkv, gmid, branch, gatt, gqkv, pv,
                     p_kv, c_kv, x_kv, z_kv, p_wo, c_wo, x_wo, z_wo, p_qk, c_qk, x_qk, z_qk, p_pw, c_pw, x_pw, z_pw, p_ve, c_ve, x_ve, z_ve,
                     kvsum, y0, y1, y2, y3, y4, y5, y6, y7,
-                    ss, sc, sx, sz, rs, rr, rys, ryr, rl, ysem, lsem):
+                    ss, sc, sx, sz, r0, r1, r2, r3, r4, r5, r6, r7, rl, ysem, lsem):
     at = place()
     r, z, x, c = at
     width = HEADS * HEAD_DIM
     kw = KV_HEADS * HEAD_DIM
     loads = [pltpu.make_async_copy(a, b, lsem.at[i]) for i, (a, b) in enumerate(((wo_ref, wo), (kv_ref, kv), (wqkv_ref, wqkv)))]
+    first_row = lax.axis_index("group") * block
+    loads.append(pltpu.make_async_copy(rope_ref.at[:, pl.ds(pl.multiple_of(first_row, block), block)], rope, lsem.at[3]))
     for l in loads: l.start()
     hail_all(*at)
-    back = Return(at, half_ref, g_main, g_spare, rs, rr, rys, ryr, rl)
+    back = Return(at, half_ref, g_out, (r0, r1, r2, r3, r4, r5, r6, r7), rl)
     back.begin(window)
     sets = ((p_kv, c_kv, x_kv, z_kv), (p_wo, c_wo, x_wo, z_wo), (p_qk, c_qk, x_qk, z_qk), (p_pw, c_pw, x_pw, z_pw), (p_ve, c_ve, x_ve, z_ve))
     ek, eo, eq, ep, ev = [Scatter(at, *b, ss.at[i], sc.at[i], sx.at[i], sz.at[i]) for i, b in enumerate(sets)]
@@ -1109,7 +1194,8 @@
         out[...] = a[...].astype(F32) + b[...].astype(F32)
 
     grad_norm, gain_two = norm_gradient(mid[...], vec[2:3, :width], gn2[...])
-    gmid[...] = cot[...].astype(F32) + grad_norm
+    valid = row_mask(lens, first_row, block, (cot.shape[0], 1))
+    gmid[...] = cot[...].astype(F32) * valid + grad_norm
     branch[...] = gmid[...].astype(BF)
     loads[0].wait()
     @pl.loop(0, 4)
@@ -1123,9 +1209,9 @@
     eo.step_x(3)
     eo.step_x(2)
     back.own()
-    layer_out[...] = ((mid[...] + mlp_out[...]) * valid[...]).astype(BF)
+    layer_out[...] = ((mid[...] + mlp_out[...]) * valid).astype(BF)
     loads[1].wait()
-    first_row = lax.axis_index("group") * block
+    loads[3].wait()
     span = 16 * block
     def unit(u):
         s, h = u // 2, lax.rem(u, 2)
@@ -1145,7 +1231,7 @@
         p_kv[:, rows, kcol] = dot_tn(gs, q).astype(BF).reshape(16, block, HEAD_DIM)
         p_kv[:, rows, vcol] = dot_tn(e.astype(BF), gn).astype(BF).reshape(16, block, HEAD_DIM)
         gq = dot(gs, k) * (HEAD_DIM ** -0.5)
-        cos, sin = cos_ref[:block], sin_ref[:block]
+        cos, sin = rope[0], rope[1]
         gqkv[rows, cols] = jnp.concatenate([spin(gq[block * i : block * (i + 1)], cos, -sin) for i in range(HEADS // KV_HEADS)], axis=1).astype(BF)
     unit(0)
     some(1)
@@ -1187,7 +1273,7 @@
     ek.step_z(1)
     some(1)
     ek.finish(kvsum)
-    cos, sin = cos_ref[...], sin_ref[...]
+    cos, sin = [jnp.concatenate((rope[i], rope[i]), axis=0) for i in range(2)]
     for h in range(KV_HEADS):
         kcol = slice(HEAD_DIM * h, HEAD_DIM * (h + 1))
         gqkv[:, width + HEAD_DIM * h : width + HEAD_DIM * (h + 1)] = spin(kvsum[:, kcol] * (HEAD_DIM ** -0.5), cos, -sin).astype(BF)
@@ -1235,7 +1321,7 @@
     traded(3, vec_out, y6, y7)
     back.end()
 
-def backward(lens, gn2, mlp_out, mid, cot, x, att, q, normed, vec, cos, sin, valid, sel, fold, selk, foldk, kv, wo, wqkv, half, block, cid, window=4):
+def backward(lens, gn2, mlp_out, mid, cot, x, att, q, normed, vec, sel, fold, selk, foldk, rope, kv, wo, wqkv, half, ff, block, cid, window=4):
     any_ = pl.BlockSpec(memory_space=pl.ANY)
     vm = pl.BlockSpec(memory_space=pltpu.VMEM)
     dma = pltpu.SemaphoreType.DMA
@@ -1249,34 +1335,32 @@
         return [VM((k,) + blk, BF) for k in (16, 8, 4, 5)]
     return pl.pallas_call(
         functools.partial(backward_kernel, block, window),
-        out_shape=[sds((rows, width), BF), sds((rows, width), F32), sds((own, width), F32), sds((own, wide - width), F32), sds((own, width), F32), sds((16, 128), F32), sds((3, own, 16 * MAIN), BF), sds((16, own, 256), BF)],
-        in_specs=[pl.BlockSpec(memory_space=pltpu.SMEM)] + [vm] * 16 + [any_] * 4,
-        out_specs=[vm] * 6 + [any_] * 2,
-        scratch_shapes=[VM(kv.shape, BF), VM(wo.shape, BF), VM(wqkv.shape, BF), VM((rows, width), F32), VM((rows, width), BF), VM((rows, width), F32), VM((rows, wide), BF), VM((16, 16, 128), F32)]
+        out_shape=[sds((rows, width), BF), sds((rows, width), F32), sds((own, width), F32), sds((own, wide - width), F32), sds((own, width), F32), sds((16, 128), F32), sds((3, own, ff), BF)],
+        in_specs=[pl.BlockSpec(memory_space=pltpu.SMEM)] + [vm] * 13 + [any_] * 5,
+        out_specs=[vm] * 6 + [any_],
+        scratch_shapes=[VM((2, block, HEAD_DIM), F32), VM(kv.shape, BF), VM(wo.shape, BF), VM(wqkv.shape, BF), VM((rows, width), F32), VM((rows, width), BF), VM((rows, width), F32), VM((rows, wide), BF), VM((16, 16, 128), F32)]
         + four((rows, kvw)) + four((own, width)) + four((own, width)) + four((own, wide - width)) + four((16, 128))
         + [VM((rows, kvw), F32)] + [VM((own, width), BF)] * 4 + [VM((own, wide - width), BF)] * 2 + [VM((16, 128), BF)] * 2
-        + [dma((5, 16)), dma((5, 8)), dma((5, 4)), dma((5, 5))] + [dma((16,))] * 4 + [dma(()), dma((8,)), dma((3,))],
+        + [dma((5, 16)), dma((5, 8)), dma((5, 4)), dma((5, 5))] + [dma((16,))] * 8 + [dma((2,)), dma((8,)), dma((4,))],
         compiler_params=pltpu.CompilerParams(collective_id=cid, has_side_effects=True, vmem_limit_bytes=60 * 2**20),
-    )(lens, gn2, mlp_out, mid, cot, x, att, q, normed, vec, cos, sin, valid, sel, fold, selk, foldk, kv, wo, wqkv, half)
-
-
-def spare_blocks(ff, main, spare):
-    group_count = lax.axis_size("group")
-    rows = ff[0].shape[0]
-    ends = [w[:, main * group_count :].reshape(rows, group_count, spare) for w in ff]
-    gap = jnp.zeros((rows, group_count, 128 - 2 * spare), BF)
-    gap_down = jnp.zeros((rows, group_count, 128 - spare), BF)
-    return jnp.transpose(
-        jnp.concatenate([ends[0], ends[1], gap, ends[2], gap_down], axis=2), (1, 0, 2)
-    )
+    )(lens, gn2, mlp_out, mid, cot, x, att, q, normed, vec, sel, fold, selk, foldk, rope, kv, wo, wqkv, half)
 
 
 def folding(group_count, width):
     share = width // group_count
-    at = jnp.arange(width)
-    sel = (at[None, :] // share == jnp.arange(group_count)[:, None]).astype(F32)
-    fold = (at[:, None] % share == jnp.arange(128)[None, :]).astype(BF)
+    at = np.arange(width)
+    sel = (at[None, :] // share == np.arange(group_count)[:, None]).astype(np.float32)
+    fold = (at[:, None] % share == np.arange(128)[None, :]).astype(BF)
     return sel, fold
+
+
+def rope_constants(span):
+    freqs = np.float32(THETA) ** (-np.arange(0, HEAD_DIM, 2, dtype=np.float32) / HEAD_DIM)
+    angles = np.arange(span, dtype=np.float32)[:, None] * freqs[None, :].astype(np.float32)
+    sin = np.sin(angles)
+    return np.stack(
+        (np.concatenate((np.cos(angles),) * 2, axis=1), np.concatenate((-sin, sin), axis=1))
+    ).astype(np.float32)
 
 
 def shards_fast(
@@ -1297,90 +1381,66 @@
     cotangent,
 ):
     group_count = lax.axis_size("group")
-    group_rank = lax.axis_index("group")
     slot_count, block_len, model_width = hidden_in.shape
     kv_width = KV_HEADS * HEAD_DIM
     tokens = slot_count * block_len
     hidden_units = w_gate.shape[1]
-    own_rows = w_gate.shape[0]
-    positions = group_rank * block_len + jnp.arange(block_len, dtype=jnp.int32)
-    valid_rows = (positions[None, :] < lengths[:, None]).astype(F32).reshape(tokens, 1)
-    cos_table, sin_table = rope_tables(positions, HEAD_DIM)
-    turn = jnp.where(jnp.arange(HEAD_DIM) < HEAD_DIM // 2, -1.0, 1.0)
-    cos_rows = jnp.tile(cos_table, (slot_count, 1))
-    sin_rows = jnp.tile(sin_table * turn, (slot_count, 1))
-
     pieces = (gain_attn, b_query, b_key, b_value, gain_mlp)
-    sizes = [p.shape[0] for p in pieces]
-    small = jnp.stack([jnp.pad(p.astype(F32), (0, 128 - p.shape[0])) for p in pieces])
-    small = jnp.pad(small, ((0, 8 - len(pieces)), (0, 0)))
-    main = (hidden_units // 128 // group_count) * 128
-    spare = hidden_units // group_count - main
-    ff = (w_gate, w_up, w_down)
     sel, fold = folding(group_count, model_width)
     selk, foldk = folding(group_count, kv_width)
+    rope = rope_constants(group_count * block_len)
     rows_in = hidden_in.reshape(tokens, model_width)
-    grad_final = (cotangent.reshape(tokens, model_width).astype(F32) * valid_rows).astype(BF)
+    grad_rows = cotangent.reshape(tokens, model_width)
     (
         q_rows, normed, attended, mid, normed_two, vec, columns, qkv_w, pair_all, grad_all, out_w
     ) = front(
         lengths,
         rows_in,
-        cos_rows,
-        sin_rows,
+        grad_rows,
+        [p[None] for p in pieces],
         sel,
         fold,
         selk,
         foldk,
-        small,
+        rope,
         w_query,
         w_key,
         w_value,
-        *ff,
-        spare_blocks(ff, main, spare),
-        grad_final,
+        w_gate,
+        w_up,
+        w_down,
         w_out,
         block_len,
         1,
     )
-    grad_normed_two, mlp_out, half_sum = mlp(normed_two, grad_all, columns, spare, 3)
-    layer_out, grad_input, query_sum, pair_sum, out_sum, vector_sum, main_sum, spare_sum = backward(
+    grad_normed_two, mlp_out, half_sum = mlp(normed_two, grad_all, columns, 3)
+    layer_out, grad_input, query_sum, pair_sum, out_sum, vector_sum, ff_sum = backward(
         lengths,
         grad_normed_two,
         mlp_out,
         mid,
-        grad_final,
+        grad_rows,
         rows_in,
         attended,
         q_rows,
         normed,
         vec,
-        cos_rows,
-        sin_rows,
-        jnp.broadcast_to(valid_rows, (tokens, model_width)),
         sel,
         fold,
         selk,
         foldk,
+        rope,
         pair_all,
         out_w,
         qkv_w,
         half_sum,
+        hidden_units,
         block_len,
         4,
     )
-    ff_sums = [
-        jnp.concatenate(
-            (
-                main_sum[i],
-                jnp.transpose(spare_sum[:, :, at : at + spare], (1, 0, 2)).reshape(own_rows, -1),
-            ),
-            axis=1,
-        ).astype(F32)
-        for i, at in ((0, 0), (1, spare), (2, 128))
-    ]
+    ff_sums = [ff_sum[i].astype(F32) for i in range(3)]
     gain_one_sum, query_bias_sum, key_bias_sum, value_bias_sum, gain_two_sum = [
-        vector_sum[i, : sizes[i]] for i in range(len(sizes))
+        vector_sum[i, : p.shape[0]] for i, p in enumerate(pieces)
     ]
     return (
         layer_out.reshape(hidden_in.shape),

time: 489 us -> 460 us (0.941)
  the two profiles are of different devices: /device:TPU:0 before, /device:TPU:22 now
where the time goes in v7:
time: 460 us; the launch traced here: 452 us
  Pallas kernels  437 us (95%)
  local copies, waits for them, and re-layouts  7.47 us (2%)
  other arithmetic  6.87 us (1%)
    pallas_call x1, Pallas kernels, front(): pl.pallas_call(functools.partial(front_kernel, block), out_shape=[sds(act...  152 us
    pallas_call x1, Pallas kernels, mlp(): pl.pallas_call(mlp_kernel, out_shape=[jax.ShapeDtypeStruct(blk, F32)] * 2...  144 us
    pallas_call x1, Pallas kernels, backward(): pl.pallas_call(functools.partial(backward_kernel, block, window), out_sha...  140 us

profile of v7, /device:TPU:22, one launch (start us, length us, event | category | flops | bytes accessed | tf_op | source)
XLA Modules:
  0.0 452.1 jit_solution(18014653475259579164)
XLA Ops:
  0.6 152.4 %shard_map.299 = (bf16[128,1536]{1,0:T(8,128)(2,1)}, bf16[128,1536]{1,0:T(8,128)(2,1)}, f32[128,1536]{1,0:T(8,128)}, f32[128,1536]{1,0:T(8,128)}, bf16[128,1536]...) custom-call(s32[2]{0:T(128)} %lens.3, ...), custom_call_target="tpu_custom_call" | custom-call | tf_op jit(solution)/shard_map/pallas_call | solution.py:1072
  153.0 143.9 %shard_map.300 = (f32[128,1536]{1,0:T(8,128)}, f32[128,1536]{1,0:T(8,128)}, bf16[16,48,1920]{2,1,0:T(8,128)(2,1)}) custom-call(bf16[128,1536]{1,0:T(8,128)(2,1)} %get-tuple-element.35.n2_ref, bf16[16,128,1536]{2,1,0:T(8,128)(2,1)} %get-tuple-element.36.cot_ref, bf16[1536,1920]{1,0:T(8,128)(2,1)} %get-tuple-element.37.w_ref), custom_call_target="tpu_custom_call" | custom-call | tf_op jit(solution)/shard_map/pallas_call | solution.py:815
  296.9 140.3 %shard_map.301 = (bf16[128,1536]{1,0:T(8,128)(2,1)}, f32[128,1536]{1,0:T(8,128)}, f32[96,1536]{1,0:T(8,128)}, f32[96,512]{1,0:T(8,128)}, f32[96,1536]{1,0:T(8,12...) custom-call(s32[2]{0:T(128)} %lens.3, f32[128,1536]{1,0:T(8,128)} %get-tuple-element.38.gn2, ...), custom_call_target="tpu_custom_call" | custom-call | tf_op jit(solution)/shard_map/pallas_call | solution.py:1336
  437.3 1.3 slice_bitcast_fusion.1
  438.5 1.3 slice_bitcast_fusion
  439.9 1.6 fusion
  441.5 0.0 copy-start.3
  441.5 0.0 copy-start
  441.5 0.0 copy-start.2
  441.5 6.9 %bitcast_convert_fusion = (f32[96,8960]{1,0:T(8,128)}, f32[96,8960]{1,0:T(8,128)}, f32[96,8960]{1,0:T(8,128)}) fusion(bf16[3,96,8960]{2,1,0:T(8,128)(2,1)} %get-tuple-element.55), kind=kLoop, calls=%fused_computation | loop fusion | flops 2580480 | bytes 15482880 | tf_op jit(solution)/shard_map/convert_element_type | solution.py:1441
  448.4 0.0 copy-start.1
  448.4 0.0 copy-done.3
  448.4 0.7 copy.38
  449.1 0.0 copy-done
  449.1 0.9 copy.39
  450.0 0.0 copy-done.2
  450.0 0.8 copy.40
  450.8 0.0 copy-done.1
  450.8 0.8 copy.41
Async XLA Ops:
  441.5 6.9 %copy-start.3 = (bf16[128,1536]{1,0:T(8,128)(2,1)S(1)}, bf16[128,1536]{1,0:T(8,128)(2,1)}, u32[]{:S(2)}) copy-start(bf16[128,1536]{1,0:T(8,128)(2,1)} %get-tuple-element.49) | copy-start | bytes 1179652
  441.5 7.6 %copy-start = (f32[128,1536]{1,0:T(8,128)S(1)}, f32[128,1536]{1,0:T(8,128)}, u32[]{:S(2)}) copy-start(f32[128,1536]{1,0:T(8,128)} %get-tuple-element.50) | copy-start | bytes 2359300
  441.5 8.5 %copy-start.2 = (f32[96,1536]{1,0:T(8,128)S(1)}, f32[96,1536]{1,0:T(8,128)}, u32[]{:S(2)}) copy-start(f32[96,1536]{1,0:T(8,128)} %get-tuple-element.83) | copy-start | bytes 1769476
  448.4 2.5 copy-start.1

commit v8 on v7

--- a/solution.py
+++ b/solution.py
@@ -420,18 +420,21 @@
     pl.when(cond)(fn)
 
 class Gather:
-    def __init__(self, at, src, out, send, recv, local):
+    def __init__(self, at, src, out, send, recv, local, part=None):
         self.r, self.z, self.x, self.c = at
         self.src, self.out, self.send, self.recv, self.local = src, out, send, recv, local
+        self.part = part
         self.mid = (self.z > 0) & (self.z < NZ - 1)
         self.p = planes(self.z)
+    def blk(self, b):
+        return self.out.at[b] if self.part is None else self.out.at[b, self.part]
     def put(self, src, b, k, dev):
-        pltpu.make_async_remote_copy(src, self.out.at[b], self.send.at[k], self.recv.at[b], device_id=dev, device_id_type=MESH).start()
+        pltpu.make_async_remote_copy(src, self.blk(b), self.send.at[k], self.recv.at[b], device_id=dev, device_id_type=MESH).start()
     def sent(self, k):
         b = 0
-        pltpu.make_async_remote_copy(self.out.at[b], self.out.at[b], self.send.at[k], self.recv.at[b], device_id=(self.r, 0), device_id_type=MESH).wait_send()
+        pltpu.make_async_remote_copy(self.blk(b), self.blk(b), self.send.at[k], self.recv.at[b], device_id=(self.r, 0), device_id_type=MESH).wait_send()
     def got(self, b):
-        pltpu.make_async_remote_copy(self.out.at[b], self.out.at[b], self.send.at[0], self.recv.at[b], device_id=(self.r, 0), device_id_type=MESH).wait_recv()
+        pltpu.make_async_remote_copy(self.blk(b), self.blk(b), self.send.at[0], self.recv.at[b], device_id=(self.r, 0), device_id_type=MESH).wait_recv()
     def zdev(self, s): return (self.r, idx(self.z + s, self.x, self.c))
     def xdev(self): return (self.r, idx(self.z, 1 - self.x, self.c))
     def cdev(self): return (self.r, idx(self.z, self.x, 1 - self.c))
@@ -442,7 +445,7 @@
             when(self.inside(z + s), lambda s=s: self.put(self.src, me, 0 if s == 1 else 3, self.zdev(s)))
         self.put(self.src, me, 6 + z, self.xdev())
         self.put(self.src, me, 10 + 2 * z + x, self.cdev())
-        pltpu.make_async_copy(self.src, self.out.at[me], self.local).start()
+        pltpu.make_async_copy(self.src, self.blk(me), self.local).start()
     def inside(self, z): return (z >= 0) & (z < NZ)
     def from_z(self, zz):
         z, x, c = self.z, self.x, self.c
@@ -451,9 +454,9 @@
         s = jnp.where(zz < z, 1, -1)
         d = jnp.abs(zz - z)
         slot = jnp.where(zz < z, 0, 3) + d
-        when(self.inside(z + s), lambda: self.put(self.out.at[b], b, slot, (self.r, idx(z + s, x, c))))
-        self.put(self.out.at[b], b, 6 + zz, self.xdev())
-        self.put(self.out.at[b], b, 10 + 2 * zz + x, self.cdev())
+        when(self.inside(z + s), lambda: self.put(self.blk(b), b, slot, (self.r, idx(z + s, x, c))))
+        self.put(self.blk(b), b, 6 + zz, self.xdev())
+        self.put(self.blk(b), b, 10 + 2 * zz + x, self.cdev())
     def first(self):
         self.from_z(self.p[1])
         when(self.mid, lambda: self.from_z(self.p[2]))
@@ -469,7 +472,7 @@
     def from_x(self, zz):
         b = idx(zz, 1 - self.x, self.c)
         self.got(b)
-        self.put(self.out.at[b], b, 10 + 2 * zz + 1 - self.x, self.cdev())
+        self.put(self.blk(b), b, 10 + 2 * zz + 1 - self.x, self.cdev())
     def from_c(self, zz):
         self.got(idx(zz, self.x, 1 - self.c))
         self.got(idx(zz, 1 - self.x, 1 - self.c))
@@ -481,7 +484,7 @@
         for k in range(6, 18):
             self.sent(k)
         if local:
-            pltpu.make_async_copy(self.src, self.out.at[0], self.local).wait()
+            pltpu.make_async_copy(self.src, self.blk(0), self.local).wait()
 
 class Scatter:
     def __init__(self, at, part, rc, rx, rz, send, rcs, rxs, rzs):
@@ -507,17 +510,17 @@
         for xx in (1 - x, x):
             k = 2 * zz + xx
             self.copy(self.part.at[idx(zz, xx, 1 - c)], self.rc.at[k], k, self.rcs.at[k], dev).start()
-    def step_x(self, d):
+    def x_plane(self, zz):
         z, x, c = self.z, self.x, self.c
         dev = (self.r, idx(z, 1 - x, c))
+        k = 2 * zz + 1 - x
+        b = idx(zz, 1 - x, c)
+        self.copy(self.rc.at[k], self.rc.at[k], 0, self.rcs.at[k], dev).wait_recv()
+        self.part[b] = (self.part[b].astype(F32) + self.rc[k].astype(F32)).astype(BF)
+        self.copy(self.part.at[b], self.rx.at[zz], 8 + zz, self.rxs.at[zz], dev).start()
+    def step_x(self, d):
         for s, zz in self.over(d):
-            def go(zz=zz):
-                k = 2 * zz + 1 - x
-                b = idx(zz, 1 - x, c)
-                self.copy(self.rc.at[k], self.rc.at[k], 0, self.rcs.at[k], dev).wait_recv()
-                self.part[b] = (self.part[b].astype(F32) + self.rc[k].astype(F32)).astype(BF)
-                self.copy(self.part.at[b], self.rx.at[zz], 8 + zz, self.rxs.at[zz], dev).start()
-            when(self.inside(zz), go)
+            when(self.inside(zz), lambda zz=zz: self.x_plane(zz))
     def step_z(self, d):
         z, x, c = self.z, self.x, self.c
         for s, zz in self.over(d):
@@ -557,6 +560,84 @@
             self.copy(self.part.at[0], self.part.at[0], k, self.rcs.at[0], (self.r, 0)).wait_send()
         for zz in range(NZ):
             when(z != zz, lambda zz=zz: self.copy(self.part.at[0], self.part.at[0], 12 + zz, self.rcs.at[0], (self.r, 0)).wait_send())
+
+class ScatterY(Scatter):
+    def __init__(self, at, part, rc, ry, rx, rz, send, rcs, rys, rxs, rzs, ysem):
+        Scatter.__init__(self, at, part, rc, rx, rz, send, rcs, rxs, rzs)
+        self.ry, self.rys, self.ysem = ry, rys, ysem
+        self.n = part.shape[1] // 2
+        self.ydev = (1 - self.r, idx(self.z, self.x, self.c))
+        self.mine = self.rows(self.r)
+    def rows(self, h):
+        return pl.ds(pl.multiple_of(h * self.n, self.n), self.n)
+    def step_y(self, d):
+        x, c, r = self.x, self.c, self.r
+        for xx in (1 - x, x):
+            for s, zz in self.over(d):
+                def go(zz=zz, xx=xx):
+                    k = 2 * zz + xx
+                    b = idx(zz, xx, c)
+                    self.copy(self.rc.at[k], self.rc.at[k], 0, self.rcs.at[k], self.ydev).wait_recv()
+                    self.part[b] = (self.part[b].astype(F32) + self.rc[k].astype(F32)).astype(BF)
+                    self.copy(self.part.at[b, self.rows(1 - r)], self.ry.at[k], 16 + k, self.rys.at[k], self.ydev).start()
+                when(self.inside(zz), go)
+    def both(self, zz, xx):
+        k = 2 * zz + xx
+        self.copy(self.ry.at[k], self.ry.at[k], 0, self.rys.at[k], self.ydev).wait_recv()
+        return self.part[idx(zz, xx, self.c), self.mine].astype(F32) + self.ry[k].astype(F32)
+    def step_x(self, d):
+        z, x, c = self.z, self.x, self.c
+        dev = (self.r, idx(z, 1 - x, c))
+        for s, zz in self.over(d):
+            def go(zz=zz):
+                b = idx(zz, 1 - x, c)
+                self.part[b, self.mine] = self.both(zz, 1 - x).astype(BF)
+                self.copy(self.part.at[b, self.mine], self.rx.at[zz], 8 + zz, self.rxs.at[zz], dev).start()
+            when(self.inside(zz), go)
+    def arrived(self, ref, sem):
+        self.copy(ref, ref, 0, sem, self.ydev).wait_recv()
+    def step_z(self, d):
+        z, x, c = self.z, self.x, self.c
+        for s, zz in self.over(d):
+            def go(zz=zz, s=s):
+                b = idx(zz, x, c)
+                v = self.both(zz, x)
+                self.arrived(self.rx.at[zz], self.rxs.at[zz])
+                self.part[b, self.mine] = (v + self.rx[zz].astype(F32)).astype(BF)
+                def more():
+                    self.arrived(self.rz.at[zz], self.rzs.at[zz])
+                    self.part[b, self.mine] = (self.part[b, self.mine].astype(F32) + self.rz[zz].astype(F32)).astype(BF)
+                when(self.inside(z - s), more)
+                slot = jnp.where(zz == z + s, NZ, zz) if s == -1 else zz
+                self.copy(self.part.at[b, self.mine], self.rz.at[slot], 12 + zz, self.rzs.at[slot], (self.r, idx(z + s, x, c))).start()
+            when(self.inside(zz), go)
+    def finish(self, out, low):
+        z, x, r = self.z, self.x, self.r
+        v = self.both(z, x)
+        self.arrived(self.rx.at[z], self.rxs.at[z])
+        out[self.mine] = v + self.rx[z].astype(F32)
+        def lo():
+            self.arrived(self.rz.at[z], self.rzs.at[z])
+            out[self.mine] += self.rz[z].astype(F32)
+        when(z > 0, lo)
+        def hi():
+            self.arrived(self.rz.at[NZ], self.rzs.at[NZ])
+            out[self.mine] += self.rz[NZ].astype(F32)
+        when(z < NZ - 1, hi)
+        low[self.mine] = out[self.mine].astype(BF)
+        a = low.at[self.mine]
+        pltpu.make_async_remote_copy(a, a, self.ysem.at[0], self.ysem.at[1], device_id=self.ydev, device_id_type=MESH).start()
+    def traded(self, out, low):
+        a = low.at[self.rows(1 - self.r)]
+        pltpu.make_async_remote_copy(a, a, self.ysem.at[0], self.ysem.at[1], device_id=self.ydev, device_id_type=MESH).wait()
+        out[...] = low[...].astype(F32)
+        half = self.part.at[0, self.mine]
+        for k in range(8):
+            self.copy(self.part.at[0], self.part.at[0], k, self.rcs.at[0], self.ydev).wait_send()
+        for k in list(range(16, 24)) + list(range(8, 12)):
+            self.copy(half, half, k, self.rcs.at[0], self.ydev).wait_send()
+        for zz in range(NZ):
+            when(self.z != zz, lambda zz=zz: self.copy(half, half, 12 + zz, self.rcs.at[0], self.ydev).wait_send())
 
 
 KS = (8, 1, 9, 2, 10, 3, 11, 4, 12, 5, 13, 6, 14, 7, 15)
@@ -739,6 +820,7 @@
     g.from_x(p[2])
     g.from_c(p[2])
     tiles(p[2])
+    rg.x_plane(p[2])
     g.from_x(p[3])
     g.from_c(p[3])
     tiles(p[3])
@@ -780,26 +862,24 @@
         add(0)
         when(extra, lambda: add(1))
 
-    rg.step_x(3)
-    rg.step_x(2)
+    rg.x_plane(p[3])
+    rg.x_plane(p[1])
     grads(0)
     rg.step_z(3)
-    rg.step_x(1)
+    rg.step_z(2)
+    rg.x_plane(p[0])
+    ro.x_plane(p[3])
     grads(1)
-    rg.step_z(2)
-    rg.step_x(0)
+    rg.step_z(1)
+    ro.x_plane(p[2])
     grads(2)
-    rg.step_z(1)
-    ro.step_x(3)
-    ro.step_x(2)
+    ro.x_plane(p[1])
+    ro.step_z(3)
+    rg.finish(gsum)
     grads(3)
-    rg.finish(gsum)
-    ro.step_z(3)
-    ro.step_x(1)
-    for j in range(0, 4): yadd(j)
+    ro.x_plane(p[0])
     ro.step_z(2)
-    ro.step_x(0)
-    for j in range(4, 8): yadd(j)
+    for j in range(0, 8): yadd(j)
     ro.step_z(1)
     for j in range(8, 12): yadd(j)
     ro.finish(osum)
@@ -1163,9 +1243,9 @@
 def backward_kernel(block, window, lens, gn2, mlp_out, mid, cot, x_ref, att, q_ref, normed, vec, sel, fold, selk, foldk, rope_ref, kv_ref, wo_ref, wqkv_ref, half_ref,
                     layer_out, grad_input, q_out, pair_out, wo_out, vec_out, g_out,
                     rope, kv, wo, wqkv, gmid, branch, gatt, gqkv, pv,
-                    p_kv, c_kv, x_kv, z_kv, p_wo, c_wo, x_wo, z_wo, p_qk, c_qk, x_qk, z_qk, p_pw, c_pw, x_pw, z_pw, p_ve, c_ve, x_ve, z_ve,
-                    kvsum, y0, y1, y2, y3, y4, y5, y6, y7,
-                    ss, sc, sx, sz, r0, r1, r2, r3, r4, r5, r6, r7, rl, ysem, lsem):
+                    p_kv, c_kv, x_kv, z_kv, p_wo, c_wo, w_wo, x_wo, z_wo, p_qk, c_qk, w_qk, x_qk, z_qk, p_pw, c_pw, x_pw, z_pw, p_ve, c_ve, x_ve, z_ve,
+                    kvsum, low_o, low_q, y4, y5, y6, y7,
+                    ss, sc, sx, sz, r0, r1, r2, r3, r4, r5, r6, r7, rl, ysem, fs, fc, fy, fx, fz, ft, lsem):
     at = place()
     r, z, x, c = at
     width = HEADS * HEAD_DIM
@@ -1177,8 +1257,10 @@
     hail_all(*at)
     back = Return(at, half_ref, g_out, (r0, r1, r2, r3, r4, r5, r6, r7), rl)
     back.begin(window)
-    sets = ((p_kv, c_kv, x_kv, z_kv), (p_wo, c_wo, x_wo, z_wo), (p_qk, c_qk, x_qk, z_qk), (p_pw, c_pw, x_pw, z_pw), (p_ve, c_ve, x_ve, z_ve))
-    ek, eo, eq, ep, ev = [Scatter(at, *b, ss.at[i], sc.at[i], sx.at[i], sz.at[i]) for i, b in enumerate(sets)]
+    sets = ((p_kv, c_kv, x_kv, z_kv), (p_pw, c_pw, x_pw, z_pw), (p_ve, c_ve, x_ve, z_ve))
+    ek, ep, ev = [Scatter(at, *b, ss.at[i], sc.at[i], sx.at[i], sz.at[i]) for i, b in enumerate(sets)]
+    sets = ((p_wo, c_wo, w_wo, x_wo, z_wo), (p_qk, c_qk, w_qk, x_qk, z_qk))
+    eo, eq = [ScatterY(at, *b, fs.at[i], fc.at[i], fy.at[i], fx.at[i], fz.at[i], ft.at[i]) for i, b in enumerate(sets)]
     steps = iter(range(15))
     def some(n):
         for _ in range(n):
@@ -1206,8 +1288,8 @@
         p_wo[blocks] = dot_tn(low, branch[...]).astype(BF).reshape(4, 96, width)
         gatt[:, col] = dot_nt(branch[...], wo[blocks].reshape(384, width))
     eo.begin()
-    eo.step_x(3)
-    eo.step_x(2)
+    for d in (3, 2, 1, 0):
+        eo.step_y(d)
     back.own()
     layer_out[...] = ((mid[...] + mlp_out[...]) * valid).astype(BF)
     loads[1].wait()
@@ -1235,9 +1317,11 @@
         gqkv[rows, cols] = jnp.concatenate([spin(gq[block * i : block * (i + 1)], cos, -sin) for i in range(HEADS // KV_HEADS)], axis=1).astype(BF)
     unit(0)
     some(1)
+    eo.step_x(3)
+    eo.step_x(2)
+    unit(1)
     eo.step_z(3)
     eo.step_x(1)
-    unit(1)
     some(1)
     eo.step_z(2)
     eo.step_x(0)
@@ -1258,12 +1342,11 @@
     ek.step_z(3)
     ek.step_x(1)
     eq.begin()
-    eo.finish(wo_out)
-    trade(0, wo_out, y0, y1)
+    eo.finish(wo_out, low_o)
+    for d in (3, 2, 1, 0):
+        eq.step_y(d)
     ek.step_z(2)
     ek.step_x(0)
-    eq.step_x(3)
-    eq.step_x(2)
     some(1)
     @pl.loop(0, 4)
     def _(t):
@@ -1271,6 +1354,8 @@
         col = pl.ds(pl.multiple_of(384 * t, 384), 384)
         gatt[:, col] = dot_nt(gqkv[:, :width], wqkv[blocks, :, :width].reshape(384, width))
     ek.step_z(1)
+    eq.step_x(3)
+    eq.step_x(2)
     some(1)
     ek.finish(kvsum)
     cos, sin = [jnp.concatenate((rope[i], rope[i]), axis=0) for i in range(2)]
@@ -1309,16 +1394,15 @@
             (eq.step_x if kind == "x" else eq.step_z)(d)
         some(1)
     some(15)
-    eq.finish(q_out)
-    trade(1, q_out, y2, y3)
+    eq.finish(q_out, low_q)
     ep.finish(pair_out)
-    trade(2, pair_out, y4, y5)
+    trade(0, pair_out, y4, y5)
     ev.finish(vec_out)
-    trade(3, vec_out, y6, y7)
-    traded(0, wo_out, y0, y1)
-    traded(1, q_out, y2, y3)
-    traded(2, pair_out, y4, y5)
-    traded(3, vec_out, y6, y7)
+    trade(1, vec_out, y6, y7)
+    eo.traded(wo_out, low_o)
+    eq.traded(q_out, low_q)
+    traded(0, pair_out, y4, y5)
+    traded(1, vec_out, y6, y7)
     back.end()
 
 def backward(lens, gn2, mlp_out, mid, cot, x, att, q, normed, vec, sel, fold, selk, foldk, rope, kv, wo, wqkv, half, ff, block, cid, window=4):
@@ -1333,15 +1417,18 @@
     VM = pltpu.VMEM
     def four(blk):
         return [VM((k,) + blk, BF) for k in (16, 8, 4, 5)]
+    def five(blk):
+        part = (blk[0] // 2, blk[1])
+        return [VM((k,) + blk, BF) for k in (16, 8)] + [VM((k,) + part, BF) for k in (8, 4, 5)]
     return pl.pallas_call(
         functools.partial(backward_kernel, block, window),
         out_shape=[sds((rows, width), BF), sds((rows, width), F32), sds((own, width), F32), sds((own, wide - width), F32), sds((own, width), F32), sds((16, 128), F32), sds((3, own, ff), BF)],
         in_specs=[pl.BlockSpec(memory_space=pltpu.SMEM)] + [vm] * 13 + [any_] * 5,
         out_specs=[vm] * 6 + [any_],
         scratch_shapes=[VM((2, block, HEAD_DIM), F32), VM(kv.shape, BF), VM(wo.shape, BF), VM(wqkv.shape, BF), VM((rows, width), F32), VM((rows, width), BF), VM((rows, width), F32), VM((rows, wide), BF), VM((16, 16, 128), F32)]
-        + four((rows, kvw)) + four((own, width)) + four((own, width)) + four((own, wide - width)) + four((16, 128))
-        + [VM((rows, kvw), F32)] + [VM((own, width), BF)] * 4 + [VM((own, wide - width), BF)] * 2 + [VM((16, 128), BF)] * 2
-        + [dma((5, 16)), dma((5, 8)), dma((5, 4)), dma((5, 5))] + [dma((16,))] * 8 + [dma((2,)), dma((8,)), dma((4,))],
+        + four((rows, kvw)) + five((own, width)) + five((own, width)) + four((own, wide - width)) + four((16, 128))
+        + [VM((rows, kvw), F32)] + [VM((own, width), BF)] * 2 + [VM((own, wide - width), BF)] * 2 + [VM((16, 128), BF)] * 2
+        + [dma((3, 16)), dma((3, 8)), dma((3, 4)), dma((3, 5))] + [dma((16,))] * 8 + [dma((2,)), dma((4,)), dma((2, 24)), dma((2, 8)), dma((2, 8)), dma((2, 4)), dma((2, 5)), dma((2, 2)), dma((4,))],
         compiler_params=pltpu.CompilerParams(collective_id=cid, has_side_effects=True, vmem_limit_bytes=60 * 2**20),
     )(lens, gn2, mlp_out, mid, cot, x, att, q, normed, vec, sel, fold, selk, foldk, rope, kv, wo, wqkv, half)
 

time: 460 us -> 447 us (0.972)
  the two profiles are of different devices: /device:TPU:22 before, /device:TPU:0 now
where the time goes in v8:
time: 447 us; the launch traced here: 439 us
  Pallas kernels  424 us (95%)
  local copies, waits for them, and re-layouts  7.47 us (2%)
  other arithmetic  6.87 us (2%)
    pallas_call x1, Pallas kernels, front(): pl.pallas_call(functools.partial(front_kernel, block), out_shape=[sds(act...  163 us
    pallas_call x1, Pallas kernels, backward(): pl.pallas_call(functools.partial(backward_kernel, block, window), out_sha...  135 us
    pallas_call x1, Pallas kernels, mlp(): pl.pallas_call(mlp_kernel, out_shape=[jax.ShapeDtypeStruct(blk, F32)] * 2...  126 us

profile of v8, /device:TPU:0, one launch (start us, length us, event | category | flops | bytes accessed | tf_op | source)
XLA Modules:
  0.0 439.1 jit_solution(17700712558265588085)
XLA Ops:
  0.6 163.1 %shard_map.299 = (bf16[128,1536]{1,0:T(8,128)(2,1)}, bf16[128,1536]{1,0:T(8,128)(2,1)}, f32[128,1536]{1,0:T(8,128)}, f32[128,1536]{1,0:T(8,128)}, bf16[128,1536]...) custom-call(s32[2]{0:T(128)} %lens.3, ...), custom_call_target="tpu_custom_call" | custom-call | tf_op jit(solution)/shard_map/pallas_call | solution.py:1152
  163.7 125.7 %shard_map.300 = (f32[128,1536]{1,0:T(8,128)}, f32[128,1536]{1,0:T(8,128)}, bf16[16,48,1920]{2,1,0:T(8,128)(2,1)}) custom-call(bf16[128,1536]{1,0:T(8,128)(2,1)} %get-tuple-element.35.n2_ref, bf16[16,128,1536]{2,1,0:T(8,128)(2,1)} %get-tuple-element.36.cot_ref, bf16[1536,1920]{1,0:T(8,128)(2,1)} %get-tuple-element.37.w_ref), custom_call_target="tpu_custom_call" | custom-call | tf_op jit(solution)/shard_map/pallas_call | solution.py:895
  289.5 134.8 %shard_map.301 = (bf16[128,1536]{1,0:T(8,128)(2,1)}, f32[128,1536]{1,0:T(8,128)}, f32[96,1536]{1,0:T(8,128)}, f32[96,512]{1,0:T(8,128)}, f32[96,1536]{1,0:T(8,12...) custom-call(s32[2]{0:T(128)} %lens.3, f32[128,1536]{1,0:T(8,128)} %get-tuple-element.38.gn2, ...), custom_call_target="tpu_custom_call" | custom-call | tf_op jit(solution)/shard_map/pallas_call | solution.py:1423
  424.3 1.3 slice_bitcast_fusion.1
  425.6 1.3 slice_bitcast_fusion
  426.9 1.6 fusion
  428.5 0.0 copy-start.3
  428.5 0.0 copy-start
  428.5 0.0 copy-start.2
  428.5 6.9 %bitcast_convert_fusion = (f32[96,8960]{1,0:T(8,128)}, f32[96,8960]{1,0:T(8,128)}, f32[96,8960]{1,0:T(8,128)}) fusion(bf16[3,96,8960]{2,1,0:T(8,128)(2,1)} %get-tuple-element.55), kind=kLoop, calls=%fused_computation | loop fusion | flops 2580480 | bytes 15482880 | tf_op jit(solution)/shard_map/convert_element_type | solution.py:1528
  435.4 0.0 copy-start.1
  435.4 0.0 copy-done.3
  435.4 0.7 copy.38
  436.1 0.0 copy-done
  436.1 0.9 copy.39
  437.0 0.0 copy-done.2
  437.0 0.8 copy.40
  437.8 0.0 copy-done.1
  437.8 0.8 copy.41
Async XLA Ops:
  428.5 6.9 %copy-start.3 = (bf16[128,1536]{1,0:T(8,128)(2,1)S(1)}, bf16[128,1536]{1,0:T(8,128)(2,1)}, u32[]{:S(2)}) copy-start(bf16[128,1536]{1,0:T(8,128)(2,1)} %get-tuple-element.49) | copy-start | bytes 1179652
  428.5 7.6 %copy-start = (f32[128,1536]{1,0:T(8,128)S(1)}, f32[128,1536]{1,0:T(8,128)}, u32[]{:S(2)}) copy-start(f32[128,1536]{1,0:T(8,128)} %get-tuple-element.50) | copy-start | bytes 2359300
  428.5 8.5 %copy-start.2 = (f32[96,1536]{1,0:T(8,128)S(1)}, f32[96,1536]{1,0:T(8,128)}, u32[]{:S(2)}) copy-start(f32[96,1536]{1,0:T(8,128)} %get-tuple-element.83) | copy-start | bytes 1769476
  435.4 2.5 copy-start.1

commit v9 on v8

--- a/solution.py
+++ b/solution.py
@@ -641,7 +641,7 @@
 
 
 KS = (8, 1, 9, 2, 10, 3, 11, 4, 12, 5, 13, 6, 14, 7, 15)
-WINDOW = 4
+WINDOW = 2
 
 def has(j):
     return lax.rem(j, 3) == 0
@@ -1044,6 +1044,7 @@
     x = x_ref[...].astype(F32)
     gq.first()
     gv.first()
+    some(1)
     gq.second()
     gv.second()
     gq.from_y(gq.p[0])
@@ -1051,6 +1052,7 @@
     gq.third()
     gv.third()
     gq.from_y(gq.p[1])
+    some(1)
     gq.fourth()
     gv.fourth()
     gc.begin()
@@ -1086,17 +1088,20 @@
     some(EARLY[1])
     gc.first()
     gk.first()
+    some(1)
     gw.first()
     some(EARLY[2])
     gk.second()
     gc.second()
     gw.second()
+    some(1)
     gw.from_y(gw.p[0])
     gk.third()
     some(EARLY[3])
     gk.fourth()
     gc.third()
     gw.third()
+    some(1)
     gw.from_y(gw.p[1])
     for zz in range(NZ):
         gk.from_c(zz)
@@ -1116,7 +1121,9 @@
         att_out[rows, cols] = spread_heads(dot(e.astype(BF), v) / total, block)
     some(EARLY[4])
     gw.fourth()
+    some(1)
     gc.fourth()
+    some(1)
     gw.from_y(gw.p[2])
     gw.from_y(gw.p[3])
     for zz in range(NZ):
@@ -1136,7 +1143,7 @@
         k.wait()
     d.end()
 
-EARLY = (2, 1, 1, 2, 3)
+EARLY = (1, 1, 1, 1, 2)
 
 def front(lens, x, cot, vectors, sel, fold, selk, foldk, rope, wq, wk, wv, wg, wu, wd, wo, block, cid):
     rows, width = x.shape
@@ -1171,7 +1178,7 @@
     def places(self, j, spare):
         row = pl.ds(pl.multiple_of(self.r * self.n, self.n), self.n)
         col = spare_at(j) if spare else pl.ds(pl.multiple_of(j * MAIN, MAIN), MAIN)
-        return [self.out.at[i, row, col] for i in range(3)]
+        return [o.at[row, col] for o in self.out]
     def parts(self, j, spare):
         if spare:
             return [self.src.at[j, :, pl.ds(3 * MAIN + 128 * i, 128)] for i in range(3)]
@@ -1241,10 +1248,10 @@
     return factor * weighted - v * (factor * factor * factor) * inner, jnp.sum(upstream * v * factor, axis=0, keepdims=True)
 
 def backward_kernel(block, window, lens, gn2, mlp_out, mid, cot, x_ref, att, q_ref, normed, vec, sel, fold, selk, foldk, rope_ref, kv_ref, wo_ref, wqkv_ref, half_ref,
-                    layer_out, grad_input, q_out, pair_out, wo_out, vec_out, g_out,
+                    layer_out, grad_input, q_out, k_out, v_out, wo_out, vec_out, g0, g1, g2,
                     rope, kv, wo, wqkv, gmid, branch, gatt, gqkv, pv,
-                    p_kv, c_kv, x_kv, z_kv, p_wo, c_wo, w_wo, x_wo, z_wo, p_qk, c_qk, w_qk, x_qk, z_qk, p_pw, c_pw, x_pw, z_pw, p_ve, c_ve, x_ve, z_ve,
-                    kvsum, low_o, low_q, y4, y5, y6, y7,
+                    p_kv, c_kv, x_kv, z_kv, p_wo, c_wo, x_wo, z_wo, p_qk, c_qk, w_qk, x_qk, z_qk, p_pw, c_pw, x_pw, z_pw, p_ve, c_ve, x_ve, z_ve,
+                    kvsum, pair_out, low_q, y2, y3, y4, y5, y6, y7,
                     ss, sc, sx, sz, r0, r1, r2, r3, r4, r5, r6, r7, rl, ysem, fs, fc, fy, fx, fz, ft, lsem):
     at = place()
     r, z, x, c = at
@@ -1255,12 +1262,11 @@
     loads.append(pltpu.make_async_copy(rope_ref.at[:, pl.ds(pl.multiple_of(first_row, block), block)], rope, lsem.at[3]))
     for l in loads: l.start()
     hail_all(*at)
-    back = Return(at, half_ref, g_out, (r0, r1, r2, r3, r4, r5, r6, r7), rl)
+    back = Return(at, half_ref, (g0, g1, g2), (r0, r1, r2, r3, r4, r5, r6, r7), rl)
     back.begin(window)
-    sets = ((p_kv, c_kv, x_kv, z_kv), (p_pw, c_pw, x_pw, z_pw), (p_ve, c_ve, x_ve, z_ve))
-    ek, ep, ev = [Scatter(at, *b, ss.at[i], sc.at[i], sx.at[i], sz.at[i]) for i, b in enumerate(sets)]
-    sets = ((p_wo, c_wo, w_wo, x_wo, z_wo), (p_qk, c_qk, w_qk, x_qk, z_qk))
-    eo, eq = [ScatterY(at, *b, fs.at[i], fc.at[i], fy.at[i], fx.at[i], fz.at[i], ft.at[i]) for i, b in enumerate(sets)]
+    sets = ((p_kv, c_kv, x_kv, z_kv), (p_wo, c_wo, x_wo, z_wo), (p_pw, c_pw, x_pw, z_pw), (p_ve, c_ve, x_ve, z_ve))
+    ek, eo, ep, ev = [Scatter(at, *b, ss.at[i], sc.at[i], sx.at[i], sz.at[i]) for i, b in enumerate(sets)]
+    eq = ScatterY(at, p_qk, c_qk, w_qk, x_qk, z_qk, fs, fc, fy, fx, fz, ft)
     steps = iter(range(15))
     def some(n):
         for _ in range(n):
@@ -1288,8 +1294,8 @@
         p_wo[blocks] = dot_tn(low, branch[...]).astype(BF).reshape(4, 96, width)
         gatt[:, col] = dot_nt(branch[...], wo[blocks].reshape(384, width))
     eo.begin()
-    for d in (3, 2, 1, 0):
-        eo.step_y(d)
+    eo.step_x(3)
+    eo.step_x(2)
     back.own()
     layer_out[...] = ((mid[...] + mlp_out[...]) * valid).astype(BF)
     loads[1].wait()
@@ -1317,11 +1323,9 @@
         gqkv[rows, cols] = jnp.concatenate([spin(gq[block * i : block * (i + 1)], cos, -sin) for i in range(HEADS // KV_HEADS)], axis=1).astype(BF)
     unit(0)
     some(1)
-    eo.step_x(3)
-    eo.step_x(2)
-    unit(1)
     eo.step_z(3)
     eo.step_x(1)
+    unit(1)
     some(1)
     eo.step_z(2)
     eo.step_x(0)
@@ -1342,7 +1346,8 @@
     ek.step_z(3)
     ek.step_x(1)
     eq.begin()
-    eo.finish(wo_out, low_o)
+    eo.finish(wo_out)
+    trade(2, wo_out, y2, y3)
     for d in (3, 2, 1, 0):
         eq.step_y(d)
     ek.step_z(2)
@@ -1399,9 +1404,11 @@
     trade(0, pair_out, y4, y5)
     ev.finish(vec_out)
     trade(1, vec_out, y6, y7)
-    eo.traded(wo_out, low_o)
+    traded(2, wo_out, y2, y3)
     eq.traded(q_out, low_q)
     traded(0, pair_out, y4, y5)
+    k_out[...] = pair_out[:, :kw]
+    v_out[...] = pair_out[:, kw:]
     traded(1, vec_out, y6, y7)
     back.end()
 
@@ -1422,13 +1429,13 @@
         return [VM((k,) + blk, BF) for k in (16, 8)] + [VM((k,) + part, BF) for k in (8, 4, 5)]
     return pl.pallas_call(
         functools.partial(backward_kernel, block, window),
-        out_shape=[sds((rows, width), BF), sds((rows, width), F32), sds((own, width), F32), sds((own, wide - width), F32), sds((own, width), F32), sds((16, 128), F32), sds((3, own, ff), BF)],
+        out_shape=[sds((rows, width), BF), sds((rows, width), F32), sds((own, width), F32), sds((own, (wide - width) // 2), F32), sds((own, (wide - width) // 2), F32), sds((own, width), F32), sds((16, 128), F32), sds((own, ff), BF)] + [sds((own, ff), BF)] * 2,
         in_specs=[pl.BlockSpec(memory_space=pltpu.SMEM)] + [vm] * 13 + [any_] * 5,
-        out_specs=[vm] * 6 + [any_],
+        out_specs=[vm] * 7 + [any_] * 3,
         scratch_shapes=[VM((2, block, HEAD_DIM), F32), VM(kv.shape, BF), VM(wo.shape, BF), VM(wqkv.shape, BF), VM((rows, width), F32), VM((rows, width), BF), VM((rows, width), F32), VM((rows, wide), BF), VM((16, 16, 128), F32)]
-        + four((rows, kvw)) + five((own, width)) + five((own, width)) + four((own, wide - width)) + four((16, 128))
-        + [VM((rows, kvw), F32)] + [VM((own, width), BF)] * 2 + [VM((own, wide - width), BF)] * 2 + [VM((16, 128), BF)] * 2
-        + [dma((3, 16)), dma((3, 8)), dma((3, 4)), dma((3, 5))] + [dma((16,))] * 8 + [dma((2,)), dma((4,)), dma((2, 24)), dma((2, 8)), dma((2, 8)), dma((2, 4)), dma((2, 5)), dma((2, 2)), dma((4,))],
+        + four((rows, kvw)) + four((own, width)) + five((own, width)) + four((own, wide - width)) + four((16, 128))
+        + [VM((rows, kvw), F32), VM((own, wide - width), F32)] + [VM((own, width), BF)] * 3 + [VM((own, wide - width), BF)] * 2 + [VM((16, 128), BF)] * 2
+        + [dma((4, 16)), dma((4, 8)), dma((4, 4)), dma((4, 5))] + [dma((16,))] * 8 + [dma((2,)), dma((6,)), dma((24,)), dma((8,)), dma((8,)), dma((4,)), dma((5,)), dma((2,)), dma((4,))],
         compiler_params=pltpu.CompilerParams(collective_id=cid, has_side_effects=True, vmem_limit_bytes=60 * 2**20),
     )(lens, gn2, mlp_out, mid, cot, x, att, q, normed, vec, sel, fold, selk, foldk, rope, kv, wo, wqkv, half)
 
@@ -1501,7 +1508,7 @@
         1,
     )
     grad_normed_two, mlp_out, half_sum = mlp(normed_two, grad_all, columns, 3)
-    layer_out, grad_input, query_sum, pair_sum, out_sum, vector_sum, ff_sum = backward(
+    layer_out, grad_input, query_sum, key_sum, value_sum, out_sum, vector_sum, *ff_sums = backward(
         lengths,
         grad_normed_two,
         mlp_out,
@@ -1524,8 +1531,9 @@
         hidden_units,
         block_len,
         4,
+        2,
     )
-    ff_sums = [ff_sum[i].astype(F32) for i in range(3)]
+    ff_sums = [p.astype(F32) for p in ff_sums]
     gain_one_sum, query_bias_sum, key_bias_sum, value_bias_sum, gain_two_sum = [
         vector_sum[i, : p.shape[0]] for i, p in enumerate(pieces)
     ]
@@ -1535,9 +1543,9 @@
         gain_one_sum,
         query_sum,
         query_bias_sum,
-        pair_sum[:, :kv_width],
+        key_sum,
         key_bias_sum,
-        pair_sum[:, kv_width:],
+        value_sum,
         value_bias_sum,
         out_sum,
         gain_two_sum,

time: 447 us -> 435 us (0.973)
  Pallas kernels: 424 us -> 411 us
    pallas_call x1, Pallas kernels: 163 us -> 148 us  [front(): pl.pallas_call(functools.partial(front_kernel, block), out_shape=[sds(act...]
    pallas_call x1, Pallas kernels: 126 us -> 133 us  [mlp(): pl.pallas_call(mlp_kernel, out_shape=[jax.ShapeDtypeStruct(blk, F32)] * 2...]
    pallas_call x1, Pallas kernels: 135 us -> 130 us  [backward(): pl.pallas_call(functools.partial(backward_kernel, block, window), out_sha...]
where the time goes in v9:
time: 435 us; the launch traced here: 427 us
  Pallas kernels  411 us (94%)
  other arithmetic  7.41 us (2%)
  local copies, waits for them, and re-layouts  7.35 us (2%)
    pallas_call x1, Pallas kernels, front(): pl.pallas_call(functools.partial(front_kernel, block), out_shape=[sds(act...  148 us
    pallas_call x1, Pallas kernels, mlp(): pl.pallas_call(mlp_kernel, out_shape=[jax.ShapeDtypeStruct(blk, F32)] * 2...  133 us
    pallas_call x1, Pallas kernels, backward(): pl.pallas_call(functools.partial(backward_kernel, block, window), out_sha...  130 us

profile of v9, /device:TPU:0, one launch (start us, length us, event | category | flops | bytes accessed | tf_op | source)
XLA Modules:
  0.0 427.0 jit_solution(7573787175163193760)
XLA Ops:
  0.6 147.9 %shard_map.299 = (bf16[128,1536]{1,0:T(8,128)(2,1)}, bf16[128,1536]{1,0:T(8,128)(2,1)}, f32[128,1536]{1,0:T(8,128)}, f32[128,1536]{1,0:T(8,128)}, bf16[128,1536]...) custom-call(s32[2]{0:T(128)} %lens.3, ...), custom_call_target="tpu_custom_call" | custom-call | tf_op jit(solution)/shard_map/pallas_call | solution.py:1159
  148.6 133.0 %shard_map.300 = (f32[128,1536]{1,0:T(8,128)}, f32[128,1536]{1,0:T(8,128)}, bf16[16,48,1920]{2,1,0:T(8,128)(2,1)}) custom-call(bf16[128,1536]{1,0:T(8,128)(2,1)} %get-tuple-element.38.n2_ref, bf16[16,128,1536]{2,1,0:T(8,128)(2,1)} %get-tuple-element.39.cot_ref, bf16[1536,1920]{1,0:T(8,128)(2,1)} %get-tuple-element.40.w_ref), custom_call_target="tpu_custom_call" | custom-call | tf_op jit(solution)/shard_map/pallas_call | solution.py:895
  281.5 130.3 %shard_map.301 = (bf16[128,1536]{1,0:T(8,128)(2,1)}, f32[128,1536]{1,0:T(8,128)}, f32[96,1536]{1,0:T(8,128)}, f32[96,256]{1,0:T(8,128)}, f32[96,256]{1,0:T(8,128...) custom-call(s32[2]{0:T(128)} %lens.3, ...), custom_call_target="tpu_custom_call" | custom-call | tf_op jit(solution)/shard_map/pallas_call | solution.py:1430
  411.8 0.0 copy-start.1
  411.8 1.3 slice_bitcast_fusion.1
  413.1 1.3 slice_bitcast_fusion
  414.5 3.4 convert_element_type.9
  417.9 0.0 copy-done.1
  417.9 0.0 copy-start
  417.9 2.0 convert_element_type.10
  419.9 0.2 copy-done
  420.0 2.0 convert_element_type.11
  422.0 0.0 copy-done.5
  422.0 0.7 copy.40
  422.8 0.0 copy-done.2
  422.8 0.9 copy.41
  423.7 0.0 copy-done.4
  423.7 0.8 copy.42
  424.5 0.0 copy-done.7
  424.5 0.6 copy.43
  425.1 0.0 copy-done.6
  425.1 0.6 copy.44
  425.8 0.0 copy-done.3
  425.8 0.8 copy.45
  (6 shorter events, 0.0 us)
Async XLA Ops:
  411.8 6.1 %copy-start.1 = (bf16[96,8960]{1,0:T(8,128)(2,1)S(1)}, bf16[96,8960]{1,0:T(8,128)(2,1)}, u32[]{:S(2)}) copy-start(bf16[96,8960]{1,0:T(8,128)(2,1)} %get-tuple-element.60) | copy-start | bytes 5160964
  417.9 2.1 copy-start
  420.0 2.0 copy-start.5
  420.0 2.8 copy-start.2
  420.0 3.6 copy-start.4
  422.0 2.5 copy-start.7
  422.0 3.1 copy-start.6
  422.0 3.7 copy-start.3

commit v10 on v9

--- a/solution.py
+++ b/solution.py
@@ -640,7 +640,7 @@
             when(self.z != zz, lambda zz=zz: self.copy(half, half, 12 + zz, self.rcs.at[0], self.ydev).wait_send())
 
 
-KS = (8, 1, 9, 2, 10, 3, 11, 4, 12, 5, 13, 6, 14, 7, 15)
+KS = (8, 4, 9, 5, 10, 6, 11, 7, 12, 1, 13, 2, 14, 3, 15)
 WINDOW = 2
 
 def has(j):

time: 435 us -> 429 us (0.986)
  the two profiles are of different devices: /device:TPU:0 before, /device:TPU:2 now
where the time goes in v10:
time: 429 us; the launch traced here: 421 us
  Pallas kernels  405 us (94%)
  other arithmetic  7.41 us (2%)
  local copies, waits for them, and re-layouts  7.35 us (2%)
    pallas_call x1, Pallas kernels, front(): pl.pallas_call(functools.partial(front_kernel, block), out_shape=[sds(act...  146 us
    pallas_call x1, Pallas kernels, backward(): pl.pallas_call(functools.partial(backward_kernel, block, window), out_sha...  130 us
    pallas_call x1, Pallas kernels, mlp(): pl.pallas_call(mlp_kernel, out_shape=[jax.ShapeDtypeStruct(blk, F32)] * 2...  128 us

profile of v10, /device:TPU:2, one launch (start us, length us, event | category | flops | bytes accessed | tf_op | source)
XLA Modules:
  0.0 420.7 jit_solution(12231324511315039649)
XLA Ops:
  0.6 146.3 %shard_map.299 = (bf16[128,1536]{1,0:T(8,128)(2,1)}, bf16[128,1536]{1,0:T(8,128)(2,1)}, f32[128,1536]{1,0:T(8,128)}, f32[128,1536]{1,0:T(8,128)}, bf16[128,1536]...) custom-call(s32[2]{0:T(128)} %lens.3, ...), custom_call_target="tpu_custom_call" | custom-call | tf_op jit(solution)/shard_map/pallas_call | solution.py:1159
  146.9 128.2 %shard_map.300 = (f32[128,1536]{1,0:T(8,128)}, f32[128,1536]{1,0:T(8,128)}, bf16[16,48,1920]{2,1,0:T(8,128)(2,1)}) custom-call(bf16[128,1536]{1,0:T(8,128)(2,1)} %get-tuple-element.38.n2_ref, bf16[16,128,1536]{2,1,0:T(8,128)(2,1)} %get-tuple-element.39.cot_ref, bf16[1536,1920]{1,0:T(8,128)(2,1)} %get-tuple-element.40.w_ref), custom_call_target="tpu_custom_call" | custom-call | tf_op jit(solution)/shard_map/pallas_call | solution.py:895
  275.1 130.3 %shard_map.301 = (bf16[128,1536]{1,0:T(8,128)(2,1)}, f32[128,1536]{1,0:T(8,128)}, f32[96,1536]{1,0:T(8,128)}, f32[96,256]{1,0:T(8,128)}, f32[96,256]{1,0:T(8,128...) custom-call(s32[2]{0:T(128)} %lens.3, ...), custom_call_target="tpu_custom_call" | custom-call | tf_op jit(solution)/shard_map/pallas_call | solution.py:1430
  405.4 0.0 copy-start.1
  405.5 1.3 slice_bitcast_fusion.1
  406.8 1.3 slice_bitcast_fusion
  408.1 3.4 convert_element_type.9
  411.5 0.0 copy-done.1
  411.5 0.0 copy-start
  411.5 2.0 convert_element_type.10
  413.5 0.2 copy-done
  413.7 2.0 convert_element_type.11
  415.7 0.0 copy-done.5
  415.7 0.7 copy.40
  416.4 0.0 copy-done.2
  416.4 0.9 copy.41
  417.3 0.0 copy-done.4
  417.3 0.8 copy.42
  418.1 0.0 copy-done.7
  418.1 0.6 copy.43
  418.8 0.0 copy-done.6
  418.8 0.6 copy.44
  419.4 0.0 copy-done.3
  419.4 0.8 copy.45
  (6 shorter events, 0.0 us)
Async XLA Ops:
  405.4 6.1 %copy-start.1 = (bf16[96,8960]{1,0:T(8,128)(2,1)S(1)}, bf16[96,8960]{1,0:T(8,128)(2,1)}, u32[]{:S(2)}) copy-start(bf16[96,8960]{1,0:T(8,128)(2,1)} %get-tuple-element.60) | copy-start | bytes 5160964
  411.5 2.1 copy-start
  413.7 2.0 copy-start.5
  413.7 2.8 copy-start.2
  413.7 3.6 copy-start.4
  415.7 2.5 copy-start.7
  415.7 3.1 copy-start.6
  415.7 3.7 copy-start.3

commit v11 on v10

--- a/solution.py
+++ b/solution.py
@@ -864,10 +864,10 @@
 
     rg.x_plane(p[3])
     rg.x_plane(p[1])
+    rg.x_plane(p[0])
     grads(0)
     rg.step_z(3)
     rg.step_z(2)
-    rg.x_plane(p[0])
     ro.x_plane(p[3])
     grads(1)
     rg.step_z(1)

time: 429 us -> 429 us (level)
  no operation moved by 1% of the time
where the time goes in v11:
time: 429 us; the launch traced here: 421 us
  Pallas kernels  405 us (94%)
  other arithmetic  7.41 us (2%)
  local copies, waits for them, and re-layouts  7.35 us (2%)
    pallas_call x1, Pallas kernels, front(): pl.pallas_call(functools.partial(front_kernel, block), out_shape=[sds(act...  146 us
    pallas_call x1, Pallas kernels, backward(): pl.pallas_call(functools.partial(backward_kernel, block, window), out_sha...  130 us
    pallas_call x1, Pallas kernels, mlp(): pl.pallas_call(mlp_kernel, out_shape=[jax.ShapeDtypeStruct(blk, F32)] * 2...  128 us

profile of v11, /device:TPU:2, one launch (start us, length us, event | category | flops | bytes accessed | tf_op | source)
XLA Modules:
  0.0 420.7 jit_solution(13611629255360340480)
XLA Ops:
  0.6 146.3 %shard_map.299 = (bf16[128,1536]{1,0:T(8,128)(2,1)}, bf16[128,1536]{1,0:T(8,128)(2,1)}, f32[128,1536]{1,0:T(8,128)}, f32[128,1536]{1,0:T(8,128)}, bf16[128,1536]...) custom-call(s32[2]{0:T(128)} %lens.3, ...), custom_call_target="tpu_custom_call" | custom-call | tf_op jit(solution)/shard_map/pallas_call | solution.py:1159
  146.9 128.2 %shard_map.300 = (f32[128,1536]{1,0:T(8,128)}, f32[128,1536]{1,0:T(8,128)}, bf16[16,48,1920]{2,1,0:T(8,128)(2,1)}) custom-call(bf16[128,1536]{1,0:T(8,128)(2,1)} %get-tuple-element.38.n2_ref, bf16[16,128,1536]{2,1,0:T(8,128)(2,1)} %get-tuple-element.39.cot_ref, bf16[1536,1920]{1,0:T(8,128)(2,1)} %get-tuple-element.40.w_ref), custom_call_target="tpu_custom_call" | custom-call | tf_op jit(solution)/shard_map/pallas_call | solution.py:895
  275.1 130.3 %shard_map.301 = (bf16[128,1536]{1,0:T(8,128)(2,1)}, f32[128,1536]{1,0:T(8,128)}, f32[96,1536]{1,0:T(8,128)}, f32[96,256]{1,0:T(8,128)}, f32[96,256]{1,0:T(8,128...) custom-call(s32[2]{0:T(128)} %lens.3, ...), custom_call_target="tpu_custom_call" | custom-call | tf_op jit(solution)/shard_map/pallas_call | solution.py:1430
  405.4 0.0 copy-start.1
  405.5 1.3 slice_bitcast_fusion.1
  406.8 1.3 slice_bitcast_fusion
  408.1 3.4 convert_element_type.9
  411.5 0.0 copy-done.1
  411.5 0.0 copy-start
  411.5 2.0 convert_element_type.10
  413.5 0.2 copy-done
  413.7 2.0 convert_element_type.11
  415.7 0.0 copy-done.5
  415.7 0.7 copy.40
  416.4 0.0 copy-done.2
  416.4 0.9 copy.41
  417.3 0.0 copy-done.4
  417.3 0.8 copy.42
  418.1 0.0 copy-done.7
  418.1 0.6 copy.43
  418.8 0.0 copy-done.6
  418.8 0.6 copy.44
  419.4 0.0 copy-done.3
  419.4 0.8 copy.45
  (6 shorter events, 0.0 us)
Async XLA Ops:
  405.4 6.1 %copy-start.1 = (bf16[96,8960]{1,0:T(8,128)(2,1)S(1)}, bf16[96,8960]{1,0:T(8,128)(2,1)}, u32[]{:S(2)}) copy-start(bf16[96,8960]{1,0:T(8,128)(2,1)} %get-tuple-element.60) | copy-start | bytes 5160964
  411.5 2.1 copy-start
  413.7 2.0 copy-start.5
  413.7 2.8 copy-start.2
  413.7 3.6 copy-start.4
  415.7 2.5 copy-start.7
  415.7 3.1 copy-start.6
  415.7 3.7 copy-start.3
